TPU v7x, 32 devices: a whole 2x2x4 slice. The times are simulated.
32 devices in a mesh: dp: 8 (over z, y), tensor: 4 (over x, core).
Axes of the slice: x: 2, y: 2, z: 4, core: 2. Of those that a mesh axis runs over, the one named last changes fastest.
Arguments:
- visual: bfloat16 [8, 144, 768], P('dp', 'tensor'), may hold values from -6 to 6
- queries: bfloat16 [8, 800, 768], P('dp', 'tensor'), may hold values from -6 to 6
- valid_windows: int32 [8, 1], P('dp'), may hold values from 0 to 1, as said below
- answer_start: int32 [8], P('dp'), may hold values from 1 to 799
- shifts: int32 [8, 2], P('dp'), may hold values from 1 to 11
- norm_scale: float32 [2, 6, 768], replicated, may hold values from 0.5 to 1.5
- norm_shift: float32 [2, 6, 768], replicated, may hold values from -1.25 to 1.25
- attn_in: bfloat16 [2, 4, 768, 3, 768], P(None, None, None, None, 'tensor'), may hold values from -0.21875 to 0.21875
- attn_out: bfloat16 [2, 4, 768, 768], P(None, None, 'tensor'), may hold values from -0.625 to 0.625
- rel_bias: float32 [2, 12, 529], P(None, 'tensor'), may hold values from -6 to 6
- mlp_in: bfloat16 [2, 2, 768, 3072], P(None, None, None, 'tensor'), may hold values from -0.21875 to 0.21875
- mlp_in_bias: float32 [2, 2, 3072], P(None, None, 'tensor'), may hold values from -3 to 3
- mlp_out: bfloat16 [2, 2, 3072, 768], P(None, None, 'tensor'), may hold values from -0.109375 to 0.109375
- mlp_out_bias: float32 [2, 2, 768], replicated, may hold values from -1.25 to 1.25
- grad_visual_out: float32 [8, 144, 768], P('dp', 'tensor'), may hold values from -6 to 6
- grad_query_out: float32 [8, 800, 768], P('dp', 'tensor'), may hold values from -6 to 6
Outputs:
- visual_out: bfloat16 [8, 144, 768], P('dp', 'tensor')
- query_out: bfloat16 [8, 800, 768], P('dp', 'tensor')
- grad_visual: float32 [8, 144, 768], P('dp', 'tensor')
- grad_query: float32 [8, 800, 768], P('dp', 'tensor')
- grad_norm_scale: float32 [2, 6, 768], replicated
- grad_norm_shift: float32 [2, 6, 768], replicated
- grad_attn_in: float32 [2, 4, 768, 3, 768], P(None, None, 'dp', None, 'tensor')
- grad_attn_out: float32 [2, 4, 768, 768], P(None, None, 'tensor', 'dp')
- grad_rel_bias: float32 [2, 12, 529], P(None, 'tensor')
- grad_mlp_in: float32 [2, 2, 768, 3072], P(None, None, 'dp', 'tensor')
- grad_mlp_in_bias: float32 [2, 2, 3072], P(None, None, 'tensor')
- grad_mlp_out: float32 [2, 2, 3072, 768], P(None, None, 'tensor', 'dp')
- grad_mlp_out_bias: float32 [2, 2, 768], replicated
Inputs may be any that keep to these rules, and one draw needn't show every extreme that they name: `valid_windows`: each page has a width w of 1 to 1 window columns; the windows whose column index is below w are 1 in every window row, the others 0; some page has w = 1.
All inputs are finite; a program needn't handle non-finite values.
Results may differ from a plain program's by a relative error of at most 0.029.
Values may be sent and summed in bfloat16 or wider, within the bound.
No kernel may reach another device: no remote copies, remote signals or barrier semaphores. Data moves between devices by JAX's collectives and lax.ppermute only.
A program may use at most 256 MiB of HBM per device.

v0:
```python
import jax
import jax.numpy as jnp
from jax import lax
from jax.sharding import PartitionSpec as P

HDIM = 64
WIN = 12
QLEN = 800
GH = 1
GW = 1


HIGH = lax.Precision.HIGHEST
NEG = -1000000000.0
EPS = 1e-05


def window_cells(field):
    trailing = field.shape[2:]
    blocked = field.reshape((GH, WIN, GW, WIN) + trailing)
    axes_order = (0, 2, 1, 3) + tuple(range(4, 4 + len(trailing)))
    return blocked.transpose(axes_order).reshape((GH * GW, WIN * WIN) + trailing)


def window_parts(tokens, row_shift, col_shift):
    patch_grid = tokens.reshape((GH * WIN, GW * WIN) + tokens.shape[1:])
    patch_grid = jnp.roll(patch_grid, (-row_shift, -col_shift), (0, 1))
    return window_cells(patch_grid)


def window_join(window_rows, row_shift, col_shift):
    trailing = window_rows.shape[2:]
    blocked = window_rows.reshape((GH, GW, WIN, WIN) + trailing)
    axes_order = (0, 2, 1, 3) + tuple(range(4, 4 + len(trailing)))
    patch_grid = blocked.transpose(axes_order).reshape((GH * WIN, GW * WIN) + trailing)
    patch_grid = jnp.roll(patch_grid, (row_shift, col_shift), (0, 1))
    return patch_grid.reshape((GH * WIN * GW * WIN,) + trailing)


def patch_flags(valid_mask, row_shift, col_shift):
    rows_total = GH * WIN
    cols_total = GW * WIN
    source_row = (jnp.arange(rows_total, dtype=jnp.int32)[:, None] + row_shift) % rows_total
    source_col = (jnp.arange(cols_total, dtype=jnp.int32)[None, :] + col_shift) % cols_total
    window_id = source_row // WIN * GW + source_col // WIN
    matches = window_id[:, :, None] == jnp.arange(GH * GW, dtype=jnp.int32)[None, None, :]
    token_ok = jnp.sum(jnp.where(matches, valid_mask[None, None, :], 0), -1) > 0
    wrap_row = jnp.broadcast_to(source_row < row_shift, token_ok.shape)
    wrap_col = jnp.broadcast_to(source_col < col_shift, token_ok.shape)
    return (token_ok, wrap_row, wrap_col)


def window_allowed(valid_mask, row_shift, col_shift):
    token_ok, wrap_row, wrap_col = patch_flags(valid_mask, row_shift, col_shift)
    key_ok = window_cells(token_ok)
    row_class = window_cells(wrap_row)
    col_class = window_cells(wrap_col)
    allowed = (
        key_ok[:, None, :]
        & (row_class[:, :, None] == row_class[:, None, :])
        & (col_class[:, :, None] == col_class[:, None, :])
    )
    return allowed[:, None]


def bias_index():
    places = jnp.arange(WIN * WIN, dtype=jnp.int32)
    row_place = places // WIN
    col_place = places % WIN
    return (
        (row_place[:, None] - row_place[None, :] + WIN - 1) * (2 * WIN - 1)
        + col_place[:, None]
        - col_place[None, :]
        + WIN
        - 1
    )


def norm_forward(values, scale_row, shift_row):
    center = values - jnp.mean(values, -1, keepdims=True)
    inv_std = lax.rsqrt(jnp.mean(center * center, -1, keepdims=True) + EPS)
    unit_rows = center * inv_std
    return (unit_rows * scale_row + shift_row, unit_rows, inv_std)


def norm_backward(grad_norm, unit_rows, inv_std, scale_row):
    grad_unit = grad_norm * scale_row
    grad_input = inv_std * (
        grad_unit
        - jnp.mean(grad_unit, -1, keepdims=True)
        - unit_rows * jnp.mean(grad_unit * unit_rows, -1, keepdims=True)
    )
    return (grad_input, jnp.sum(grad_norm * unit_rows, 0), jnp.sum(grad_norm, 0))


def split_heads(values):
    return values.reshape(values.shape[:-1] + (values.shape[-1] // HDIM, HDIM)).swapaxes(-2, -3)


def join_heads(values):
    joined = values.swapaxes(-2, -3)
    return joined.reshape(joined.shape[:-2] + (joined.shape[-2] * HDIM,))


def masked_scores(queries_h, key_rows, addend, allowed):
    raw_scores = (
        jnp.einsum("bhqd,bhkd->bhqk", queries_h, key_rows, preferred_element_type=jnp.float32)
        * HDIM ** (-0.5)
        + addend
    )
    return jnp.where(allowed, raw_scores, NEG)


def core_forward(queries_h, key_rows, value_rows, addend, allowed):
    scores = masked_scores(queries_h, key_rows, addend, allowed)
    row_max = jnp.max(scores, -1, keepdims=True)
    log_sum = jnp.log(jnp.sum(jnp.exp(scores - row_max), -1, keepdims=True))
    attn_probs = jnp.exp(scores - row_max - log_sum).astype(jnp.bfloat16)
    attended = jnp.einsum(
        "bhqk,bhkd->bhqd", attn_probs, value_rows, preferred_element_type=jnp.float32
    )
    return (attended.astype(jnp.bfloat16), (row_max, log_sum))


def core_backward(queries_h, key_rows, value_rows, addend, allowed, log_total, grad_attended):
    attn_probs = jnp.exp(
        masked_scores(queries_h, key_rows, addend, allowed) - log_total[0] - log_total[1]
    )
    grad_values = jnp.einsum(
        "bhqk,bhqd->bhkd",
        attn_probs.astype(jnp.bfloat16),
        grad_attended,
        preferred_element_type=jnp.float32,
    )
    grad_probs = jnp.einsum(
        "bhqd,bhkd->bhqk", grad_attended, value_rows, preferred_element_type=jnp.float32
    )
    grad_scores = attn_probs * (grad_probs - jnp.sum(attn_probs * grad_probs, -1, keepdims=True))
    grad_scores = jnp.where(allowed, grad_scores, 0.0).astype(jnp.bfloat16)
    grad_queries = jnp.einsum(
        "bhqk,bhkd->bhqd", grad_scores, key_rows, preferred_element_type=jnp.float32
    ) * HDIM ** (-0.5)
    grad_keys = jnp.einsum(
        "bhqk,bhqd->bhkd", grad_scores, queries_h, preferred_element_type=jnp.float32
    ) * HDIM ** (-0.5)
    return (grad_queries, grad_keys, grad_values, grad_scores)


def project(source_q, source_kv, weight):
    queries_p = jnp.einsum(
        "bsd,de->bse", source_q, weight[:, 0], preferred_element_type=jnp.float32
    ).astype(jnp.bfloat16)
    key_value = jnp.einsum(
        "bsd,dce->cbse", source_kv, weight[:, 1:], preferred_element_type=jnp.float32
    ).astype(jnp.bfloat16)
    return (queries_p, key_value)


def unit_forward(source_q, source_kv, weight, addend, allowed):
    queries_p, key_value = project(source_q, source_kv, weight)
    attended, log_total = core_forward(
        split_heads(queries_p),
        split_heads(key_value[0]),
        split_heads(key_value[1]),
        addend,
        allowed,
    )
    return (join_heads(attended), log_total)


def unit_backward(source_q, source_kv, weight, addend, allowed, log_total, grad_joined):
    queries_p, key_value = project(source_q, source_kv, weight)
    grad_queries, grad_keys, grad_values, grad_scores = core_backward(
        split_heads(queries_p),
        split_heads(key_value[0]),
        split_heads(key_value[1]),
        addend,
        allowed,
        log_total,
        split_heads(grad_joined),
    )
    grad_qrows = join_heads(grad_queries).astype(jnp.bfloat16)
    grad_kvrows = jnp.stack([join_heads(grad_keys), join_heads(grad_values)]).astype(jnp.bfloat16)
    weight_query = jnp.einsum(
        "bsd,bse->de", source_q, grad_qrows, preferred_element_type=jnp.float32
    )
    weight_keyval = jnp.einsum(
        "bsd,cbse->dce", source_kv, grad_kvrows, preferred_element_type=jnp.float32
    )
    grad_source_q = jnp.einsum(
        "bse,de->bsd", grad_qrows, weight[:, 0], preferred_element_type=jnp.float32
    )
    grad_source_kv = jnp.einsum(
        "cbse,dce->bsd", grad_kvrows, weight[:, 1:], preferred_element_type=jnp.float32
    )
    return (
        grad_source_q,
        grad_source_kv,
        jnp.concatenate([weight_query[:, None], weight_keyval], 1),
        grad_scores,
    )


def mlp_forward(normed, w_up, b_up, w_down):
    hidden = jnp.dot(normed, w_up, preferred_element_type=jnp.float32) + b_up
    return jnp.dot(
        jax.nn.gelu(hidden).astype(jnp.bfloat16), w_down, preferred_element_type=jnp.float32
    )


def mlp_backward(normed, w_up, b_up, w_down, grad_rows):
    hidden = jnp.dot(normed, w_up, preferred_element_type=jnp.float32) + b_up
    active, gelu_pull = jax.vjp(jax.nn.gelu, hidden)
    active = active.astype(jnp.bfloat16)
    grad_down = jnp.einsum("sf,sd->fd", active, grad_rows, preferred_element_type=jnp.float32)
    grad_active = jnp.einsum("sd,fd->sf", grad_rows, w_down, preferred_element_type=jnp.float32)
    grad_hidden = gelu_pull(grad_active)[0].astype(jnp.bfloat16)
    grad_up = jnp.einsum("sd,sf->df", normed, grad_hidden, preferred_element_type=jnp.float32)
    grad_bias = jnp.sum(grad_hidden.astype(jnp.float32), 0)
    grad_normed = jnp.einsum("sf,df->sd", grad_hidden, w_up, preferred_element_type=jnp.float32)
    return (grad_normed, grad_up, grad_bias, grad_down)


def gather_rows(visual_part, query_part):
    return (
        lax.all_gather(visual_part, "tensor", axis=0, tiled=True),
        lax.all_gather(query_part, "tensor", axis=0, tiled=True),
    )


def scatter_rows(visual_part, query_part):
    return (
        lax.psum_scatter(visual_part, "tensor", scatter_dimension=0, tiled=True),
        lax.psum_scatter(query_part, "tensor", scatter_dimension=0, tiled=True),
    )


def gather_grads(visual_part, query_part):
    return (
        lax.all_gather(visual_part, "tensor", axis=0, tiled=True),
        lax.all_gather(query_part, "tensor", axis=0, tiled=True),
    )


def scatter_grads(visual_part, query_part):
    return (
        lax.psum_scatter(visual_part, "tensor", scatter_dimension=0, tiled=True),
        lax.psum_scatter(query_part, "tensor", scatter_dimension=0, tiled=True),
    )


def on_device(
    visual,
    queries,
    valid_windows,
    answer_start,
    shifts,
    norm_scale,
    norm_shift,
    attn_in,
    attn_out,
    rel_bias,
    mlp_in,
    mlp_in_bias,
    mlp_out,
    mlp_out_bias,
    grad_visual_out,
    grad_query_out,
):
    visual_x = visual[0].astype(jnp.float32)
    queries_x = queries[0].astype(jnp.float32)
    valid_mask = valid_windows[0]
    answer_from = answer_start[0]
    layer_count = attn_in.shape[0]
    heads_dev = attn_in.shape[4] // HDIM
    positions = jnp.arange(QLEN, dtype=jnp.int32)
    before_answer = positions[None, :] < answer_from
    self_allowed = (before_answer | (positions[None, :] <= positions[:, None]))[None, None]
    to_question = before_answer[None, None]
    to_patches = patch_flags(valid_mask, 0, 0)[0].reshape(1, 1, 1, -1)
    table_onehot = (
        bias_index().reshape(-1)[:, None]
        == jnp.arange((2 * WIN - 1) ** 2, dtype=jnp.int32)[None, :]
    ).astype(jnp.float32)

    def window_bias(layer_index):
        flat_bias = jnp.einsum("hr,tr->ht", rel_bias[layer_index], table_onehot, precision=HIGH)
        return flat_bias.reshape(heads_dev, WIN * WIN, WIN * WIN)[None]

    def normed_pair(stream_v, stream_q, layer_index, first):
        visual_norm = norm_forward(
            stream_v, norm_scale[layer_index, first], norm_shift[layer_index, first]
        )
        query_norm = norm_forward(
            stream_q, norm_scale[layer_index, first + 1], norm_shift[layer_index, first + 1]
        )
        return (visual_norm, query_norm)

    def inputs_of(record):
        return record[2]

    def open_section(grad_v, grad_q):
        return ((grad_v, grad_q), gather_grads(grad_v, grad_q))

    def close_section(record, layer_index, first, partial_v, partial_q):
        shard_v, shard_q = scatter_grads(partial_v, partial_q)
        visual_norm, query_norm = normed_pair(record[0], record[1], layer_index, first)
        back_v = norm_backward(
            shard_v, visual_norm[1], visual_norm[2], norm_scale[layer_index, first]
        )
        back_q = norm_backward(
            shard_q, query_norm[1], query_norm[2], norm_scale[layer_index, first + 1]
        )
        return (back_v, back_q)

    records = []
    for layer_index in range(layer_count):
        row_shift = shifts[0, 0] * (layer_index % 2)
        col_shift = shifts[0, 1] * (layer_index % 2)
        window_mask = window_allowed(valid_mask, row_shift, col_shift)
        bias_add = window_bias(layer_index)
        visual_norm, query_norm = normed_pair(visual_x, queries_x, layer_index, 0)
        whole_visual, whole_query = gather_rows(
            visual_norm[0].astype(jnp.bfloat16), query_norm[0].astype(jnp.bfloat16)
        )
        windows = window_parts(whole_visual, row_shift, col_shift)
        local_out, local_lse = unit_forward(
            windows, windows, attn_in[layer_index, 0], bias_add, window_mask
        )
        local_out = window_join(local_out, row_shift, col_shift)
        self_out, self_lse = unit_forward(
            whole_query[None], whole_query[None], attn_in[layer_index, 1], 0.0, self_allowed
        )
        part_v, part_q = scatter_rows(
            jnp.dot(local_out, attn_out[layer_index, 0], preferred_element_type=jnp.float32),
            jnp.dot(self_out[0], attn_out[layer_index, 1], preferred_element_type=jnp.float32),
        )
        records.append(
            (
                visual_x,
                queries_x,
                (whole_visual, whole_query),
                (local_out, local_lse, self_out[0], self_lse),
            )
        )
        visual_x = visual_x + part_v
        queries_x = queries_x + part_q
        visual_norm, query_norm = normed_pair(visual_x, queries_x, layer_index, 2)
        whole_visual, whole_query = gather_rows(
            visual_norm[0].astype(jnp.bfloat16), query_norm[0].astype(jnp.bfloat16)
        )
        query_side, query_lse = unit_forward(
            whole_query[None], whole_visual[None], attn_in[layer_index, 2], 0.0, to_patches
        )
        visual_side, visual_lse = unit_forward(
            whole_visual[None], whole_query[None], attn_in[layer_index, 3], 0.0, to_question
        )
        part_v, part_q = scatter_rows(
            jnp.dot(visual_side[0], attn_out[layer_index, 3], preferred_element_type=jnp.float32),
            jnp.dot(query_side[0], attn_out[layer_index, 2], preferred_element_type=jnp.float32),
        )
        records.append(
            (
                visual_x,
                queries_x,
                (whole_visual, whole_query),
                (query_side[0], query_lse, visual_side[0], visual_lse),
            )
        )
        visual_x = visual_x + part_v
        queries_x = queries_x + part_q
        visual_norm, query_norm = normed_pair(visual_x, queries_x, layer_index, 4)
        whole_visual, whole_query = gather_rows(
            visual_norm[0].astype(jnp.bfloat16), query_norm[0].astype(jnp.bfloat16)
        )
        part_v, part_q = scatter_rows(
            mlp_forward(
                whole_visual,
                mlp_in[layer_index, 0],
                mlp_in_bias[layer_index, 0],
                mlp_out[layer_index, 0],
            ),
            mlp_forward(
                whole_query,
                mlp_in[layer_index, 1],
                mlp_in_bias[layer_index, 1],
                mlp_out[layer_index, 1],
            ),
        )
        records.append((visual_x, queries_x, (whole_visual, whole_query), ()))
        visual_x = visual_x + part_v + mlp_out_bias[layer_index, 0]
        queries_x = queries_x + part_q + mlp_out_bias[layer_index, 1]
    grad_v = grad_visual_out[0]
    grad_q = grad_query_out[0]
    layer_grads = [None] * layer_count
    for layer_index in reversed(range(layer_count)):
        row_shift = shifts[0, 0] * (layer_index % 2)
        col_shift = shifts[0, 1] * (layer_index % 2)
        window_mask = window_allowed(valid_mask, row_shift, col_shift)
        bias_add = window_bias(layer_index)
        record = records[3 * layer_index + 2]
        whole_visual, whole_query = inputs_of(record)
        rounded, whole_grads = open_section(grad_v, grad_q)
        feed_v = mlp_backward(
            whole_visual,
            mlp_in[layer_index, 0],
            mlp_in_bias[layer_index, 0],
            mlp_out[layer_index, 0],
            whole_grads[0],
        )
        feed_q = mlp_backward(
            whole_query,
            mlp_in[layer_index, 1],
            mlp_in_bias[layer_index, 1],
            mlp_out[layer_index, 1],
            whole_grads[1],
        )
        tail_v, tail_q = close_section(record, layer_index, 4, feed_v[0], feed_q[0])
        out_bias_grad = jnp.stack([jnp.sum(rounded[0], 0), jnp.sum(rounded[1], 0)])
        grad_v = grad_v + tail_v[0]
        grad_q = grad_q + tail_q[0]
        record = records[3 * layer_index + 1]
        whole_visual, whole_query = inputs_of(record)
        query_side, query_lse, visual_side, visual_lse = record[3]
        rounded, whole_grads = open_section(grad_v, grad_q)
        out_grad_query = jnp.einsum(
            "se,sd->ed", query_side, whole_grads[1], preferred_element_type=jnp.float32
        )
        out_grad_visual = jnp.einsum(
            "se,sd->ed", visual_side, whole_grads[0], preferred_element_type=jnp.float32
        )
        grad_query_side = jnp.einsum(
            "sd,ed->se",
            whole_grads[1],
            attn_out[layer_index, 2],
            preferred_element_type=jnp.float32,
        ).astype(jnp.bfloat16)
        grad_visual_side = jnp.einsum(
            "sd,ed->se",
            whole_grads[0],
            attn_out[layer_index, 3],
            preferred_element_type=jnp.float32,
        ).astype(jnp.bfloat16)
        toward_patches = unit_backward(
            whole_query[None],
            whole_visual[None],
            attn_in[layer_index, 2],
            0.0,
            to_patches,
            query_lse,
            grad_query_side[None],
        )
        toward_question = unit_backward(
            whole_visual[None],
            whole_query[None],
            attn_in[layer_index, 3],
            0.0,
            to_question,
            visual_lse,
            grad_visual_side[None],
        )
        cross_v, cross_q = close_section(
            record,
            layer_index,
            2,
            toward_patches[1][0] + toward_question[0][0],
            toward_patches[0][0] + toward_question[1][0],
        )
        grad_v = grad_v + cross_v[0]
        grad_q = grad_q + cross_q[0]
        record = records[3 * layer_index]
        whole_visual, whole_query = inputs_of(record)
        local_out, local_lse, self_out, self_lse = record[3]
        rounded, whole_grads = open_section(grad_v, grad_q)
        out_grad_local = jnp.einsum(
            "se,sd->ed", local_out, whole_grads[0], preferred_element_type=jnp.float32
        )
        out_grad_self = jnp.einsum(
            "se,sd->ed", self_out, whole_grads[1], preferred_element_type=jnp.float32
        )
        grad_local = jnp.einsum(
            "sd,ed->se",
            whole_grads[0],
            attn_out[layer_index, 0],
            preferred_element_type=jnp.float32,
        ).astype(jnp.bfloat16)
        grad_self = jnp.einsum(
            "sd,ed->se",
            whole_grads[1],
            attn_out[layer_index, 1],
            preferred_element_type=jnp.float32,
        ).astype(jnp.bfloat16)
        windows = window_parts(whole_visual, row_shift, col_shift)
        local_back = unit_backward(
            windows,
            windows,
            attn_in[layer_index, 0],
            bias_add,
            window_mask,
            local_lse,
            window_parts(grad_local, row_shift, col_shift),
        )
        grad_windows = window_join(local_back[0] + local_back[1], row_shift, col_shift)
        score_sum = jnp.sum(local_back[3].astype(jnp.float32), 0).reshape(
            heads_dev, WIN * WIN * WIN * WIN
        )
        rel_grad = jnp.einsum("ht,tr->hr", score_sum, table_onehot, precision=HIGH)
        self_back = unit_backward(
            whole_query[None],
            whole_query[None],
            attn_in[layer_index, 1],
            0.0,
            self_allowed,
            self_lse,
            grad_self[None],
        )
        first_v, first_q = close_section(
            record, layer_index, 0, grad_windows, self_back[0][0] + self_back[1][0]
        )
        grad_v = grad_v + first_v[0]
        grad_q = grad_q + first_q[0]
        attn_in_grad = jnp.stack(
            [local_back[2], self_back[2], toward_patches[2], toward_question[2]]
        )
        attn_out_grad = jnp.stack([out_grad_local, out_grad_self, out_grad_query, out_grad_visual])
        mlp_in_grad = jnp.stack([feed_v[1], feed_q[1]])
        mlp_out_grad = jnp.stack([feed_v[3], feed_q[3]])
        large_grads = (attn_in_grad, attn_out_grad, mlp_in_grad, mlp_out_grad)
        large_grads = (
            lax.psum_scatter(attn_in_grad, "dp", scatter_dimension=1, tiled=True),
            lax.psum_scatter(attn_out_grad, "dp", scatter_dimension=2, tiled=True),
            lax.psum_scatter(mlp_in_grad, "dp", scatter_dimension=1, tiled=True),
            lax.psum_scatter(mlp_out_grad, "dp", scatter_dimension=2, tiled=True),
        )
        scale_grad = jnp.stack(
            [first_v[1], first_q[1], cross_v[1], cross_q[1], tail_v[1], tail_q[1]]
        )
        shift_grad = jnp.stack(
            [first_v[2], first_q[2], cross_v[2], cross_q[2], tail_v[2], tail_q[2]]
        )
        in_bias_grad = jnp.stack([feed_v[2], feed_q[2]])
        layer_grads[layer_index] = (
            large_grads,
            scale_grad,
            shift_grad,
            out_bias_grad,
            rel_grad,
            in_bias_grad,
        )
    stacked_large = tuple(
        (
            jnp.stack([layer_grads[which][0][member] for which in range(layer_count)])
            for member in range(4)
        )
    )
    stacked_small = tuple(
        (
            jnp.stack([layer_grads[which][member] for which in range(layer_count)])
            for member in range(1, 6)
        )
    )
    scale_total, shift_total, out_bias_total = lax.psum(
        (stacked_small[0], stacked_small[1], stacked_small[2]), ("dp", "tensor")
    )
    rel_total, in_bias_total = lax.psum((stacked_small[3], stacked_small[4]), "dp")
    return (
        visual_x.astype(jnp.bfloat16)[None],
        queries_x.astype(jnp.bfloat16)[None],
        grad_v[None],
        grad_q[None],
        scale_total,
        shift_total,
        stacked_large[0],
        stacked_large[1],
        rel_total,
        stacked_large[2],
        in_bias_total,
        stacked_large[3],
        out_bias_total,
    )


def solution(mesh):
    return jax.shard_map(
        on_device,
        mesh=mesh,
        in_specs=(
            P("dp", "tensor", None),
            P("dp", "tensor", None),
            P("dp", None),
            P("dp"),
            P("dp", None),
            P(),
            P(),
            P(None, None, None, None, "tensor"),
            P(None, None, "tensor", None),
            P(None, "tensor", None),
            P(None, None, None, "tensor"),
            P(None, None, "tensor"),
            P(None, None, "tensor", None),
            P(),
            P("dp", "tensor", None),
            P("dp", "tensor", None),
        ),
        out_specs=(
            P("dp", "tensor", None),
            P("dp", "tensor", None),
            P("dp", "tensor", None),
            P("dp", "tensor", None),
            P(),
            P(),
            P(None, None, "dp", None, "tensor"),
            P(None, None, "tensor", "dp"),
            P(None, "tensor", None),
            P(None, None, "dp", "tensor"),
            P(None, None, "tensor"),
            P(None, None, "tensor", "dp"),
            P(),
        ),
        check_vma=False,
    )
```

profile of v0, /device:TPU:0, one launch (start us, length us, event | category | flops | bytes accessed | tf_op | source)
XLA Modules:
  0.0 2049.3 jit_solution(1882051925938046236)
XLA Ops:
  21.8 13.4 all-gather.26.cloned.1.call-done
  68.0 14.7 fusion.40
  130.1 34.4 %reduce-scatter.53.cloned.1.call-done = f32[200,768]{1,0:T(8,128)} async-done(((f32[800,768]{1,0:T(8,128)}), f32[200,768]{1,0:T(8,128)}) %reduce-scatter.53.cloned.1.call-update) | async-done | bytes 614416 | tf_op jit(solution)/shard_map/reduce_scatter | solution.py:234
  167.6 17.2 all-gather.30.cloned.1.call-done
  197.0 15.4 fusion.41
  236.5 13.8 fusion.1
  373.0 34.6 %reduce-scatter.59.cloned.1.call-done = f32[200,768]{1,0:T(8,128)} async-done(((f32[800,768]{1,0:T(8,128)}), f32[200,768]{1,0:T(8,128)}) %reduce-scatter.59.cloned.1.call-update) | async-done | bytes 614416 | tf_op jit(solution)/shard_map/reduce_scatter | solution.py:234
  412.8 15.1 all-gather.36.cloned.1.call-done
  432.2 15.6 all-gather.48.cloned.1.call-done
  592.3 33.7 %reduce-scatter.65.cloned.1.call-done = f32[200,768]{1,0:T(8,128)} async-done(((f32[800,768]{1,0:T(8,128)}), f32[200,768]{1,0:T(8,128)}) %reduce-scatter.65.cloned.1.call-update) | async-done | bytes 614416 | tf_op jit(solution)/shard_map/reduce_scatter | solution.py:248
  666.1 13.9 fusion.204
  679.9 13.4 fusion.207
  711.6 14.8 fusion.7
  859.2 34.3 %reduce-scatter.71.cloned.1.call-done = f32[200,768]{1,0:T(8,128)} async-done(((f32[800,768]{1,0:T(8,128)}), f32[200,768]{1,0:T(8,128)}) %reduce-scatter.71.cloned.1.call-update) | async-done | bytes 614416 | tf_op jit(solution)/shard_map/reduce_scatter | solution.py:248
  996.7 14.4 reshape.1941
  1128.6 14.3 fusion.654
  1174.1 14.3 reshape.1939
  1213.4 40.0 %all-reduce.27 = (f32[2,3,529]{2,1,0:T(4,128)S(1)}, f32[2,2,768]{2,1,0:T(2,128)}) all-reduce(f32[2,3,529]{2,1,0:T(4,128)S(1)} %pad_maximum_fusion.30, f32[2,2,768]{2,1,0:T(2,128)S(1)} %pad_maximum_fusion.31), channel_id=1, replica_groups=mesh['dp'=8,'tensor'=4] {'dp'}, use_global_device_ids=true, to_apply=%region_126.130 | all-reduce | flops 6246 | bytes 49968 | tf_op jit(solution)/shard_map/psum | solution.py:565
  1258.6 243.4 %all-reduce.35.cloned.1.call-done = (f32[2,768,768]{1,0,2:T(2,128)}, f32[2,768,768]{1,0,2:T(2,128)}) async-done(((f32[2,768,768]{1,0,2:T(2,128)}, f32[2,768,768]{1,0,2:T(2,128)}), (f32[2,768,768]{1,0,2:T(2,128)}, f32[2,768,768]{1,0,2:T(2,128)})) %all-reduce.35.cloned.1.call-update) | async-done | bytes 9437200
  1505.9 94.5 %reduce-scatter.77.cloned.1.call-done = f32[2,96,768]{2,1,0:T(8,128)} async-done(((f32[2,768,768]{2,1,0:T(8,128)}), f32[2,96,768]{2,1,0:T(8,128)}) %reduce-scatter.77.cloned.1.call-update) | async-done | bytes 589840 | tf_op jit(solution)/shard_map/reduce_scatter | solution.py:532
  1600.4 99.1 %reduce-scatter.75.cloned.1.call-done = f32[2,96,768]{2,1,0:T(8,128)} async-done(((f32[2,768,768]{2,1,0:T(8,128)}), f32[2,96,768]{2,1,0:T(8,128)}) %reduce-scatter.75.cloned.1.call-update) | async-done | bytes 589840 | tf_op jit(solution)/shard_map/reduce_scatter | solution.py:532
  1701.9 70.2 %reduce-scatter.83.cloned.1.call-done = f32[96,768]{1,0:T(8,128)} async-done(((f32[768,768]{1,0:T(8,128)}), f32[96,768]{1,0:T(8,128)}) %reduce-scatter.83.cloned.1.call-update) | async-done | bytes 294928
  1777.3 123.1 %all-reduce.33.cloned.1.call-done = (f32[2,6,768]{2,1,0:T(8,128)}, f32[2,6,768]{2,1,0:T(8,128)}, f32[2,2,768]{2,1,0:T(2,128)}) async-done(((f32[2,6,768]{2,1,0:T(8,128)}, f32[2,6,768]{2,1,0:T(8,128)}, f32[2,2,768]{2,1,0:T(2,128)}), (f32[2,6,768]{2,1,0:T(8,128)}, f32[2,6,768]{2,1,0:T(8,128)}, f32[2,2,768]{2,1,0:T(2,128)})) %all-reduce.33.cloned.1.call-update) | async-done | bytes 86032 | tf_op jit(solution)/shard_map/psum | solution.py:562
  1903.3 131.3 %reduce-scatter.79.cloned.1.call-done = f32[96,2304]{1,0:T(8,128)} async-done(((f32[768,2304]{1,0:T(8,128)}), f32[96,2304]{1,0:T(8,128)}) %reduce-scatter.79.cloned.1.call-update) | async-done | bytes 884752
  (1300 shorter events, 895.3 us)
Async XLA Ops:
  14.6 77.8 %reduce-scatter.51.cloned.1.call-start = ((), (), s32[]{:S(2)}) async-start(), calls=%async_computation.19 | async-start | bytes 3072000 | tf_op jit(solution)/shard_map/reduce_scatter | solution.py:234
  94.9 69.6 %reduce-scatter.53.cloned.1.call-start = ((), (), s32[]{:S(2)}) async-start(), calls=%async_computation.21 | async-start | bytes 3072000 | tf_op jit(solution)/shard_map/reduce_scatter | solution.py:234
  193.5 61.9 %all-gather.32.cloned.1.call-start = ((), (), s32[]{:S(2)}) async-start(), calls=%async_computation.24 | async-start | bytes 1536000 | tf_op jit(solution)/shard_map/all_gather | solution.py:227
  229.7 102.3 %reduce-scatter.57.cloned.1.call-start = ((), (), s32[]{:S(2)}) async-start(), calls=%async_computation.25 | async-start | bytes 3072000 | tf_op jit(solution)/shard_map/reduce_scatter | solution.py:234
  279.1 82.8 %all-gather.34.cloned.1.call-start = ((), (), s32[]{:S(2)}) async-start(), calls=%async_computation.26 | async-start | bytes 1536000 | tf_op jit(solution)/shard_map/all_gather | solution.py:227
  334.5 73.2 %reduce-scatter.59.cloned.1.call-start = ((), (), s32[]{:S(2)}) async-start(), calls=%async_computation.27 | async-start | bytes 3072000 | tf_op jit(solution)/shard_map/reduce_scatter | solution.py:234
  412.8 141.4 %reduce-scatter.63.cloned.1.call-start = ((), (), s32[]{:S(2)}) async-start(), calls=%async_computation.30 | async-start | bytes 3072000 | tf_op jit(solution)/shard_map/reduce_scatter | solution.py:248
  458.3 95.8 %reduce-scatter.61.cloned.1.call-start = ((), (), s32[]{:S(2)}) async-start(), calls=%async_computation.29 | async-start | bytes 3072000 | tf_op jit(solution)/shard_map/reduce_scatter | solution.py:234
  480.9 99.6 %all-gather.38.cloned.1.call-start = ((), (), s32[]{:S(2)}) async-start(), calls=%async_computation.31 | async-start | bytes 1536000 | tf_op jit(solution)/shard_map/all_gather | solution.py:241
  558.4 67.7 %reduce-scatter.65.cloned.1.call-start = ((), (), s32[]{:S(2)}) async-start(), calls=%async_computation.32 | async-start | bytes 3072000 | tf_op jit(solution)/shard_map/reduce_scatter | solution.py:248
  630.4 104.3 %reduce-scatter.67.cloned.1.call-start = ((), (), s32[]{:S(2)}) async-start(), calls=%async_computation.34 | async-start | bytes 3072000 | tf_op jit(solution)/shard_map/reduce_scatter | solution.py:248
  697.7 60.9 %all-gather.42.cloned.1.call-start = ((), (), s32[]{:S(2)}) async-start(), calls=%async_computation.35 | async-start | bytes 1536000 | tf_op jit(solution)/shard_map/all_gather | solution.py:241
  739.4 85.0 %reduce-scatter.69.cloned.1.call-start = ((), (), s32[]{:S(2)}) async-start(), calls=%async_computation.36 | async-start | bytes 3072000 | tf_op jit(solution)/shard_map/reduce_scatter | solution.py:248
  769.2 79.0 %all-gather.44.cloned.1.call-start = ((), (), s32[]{:S(2)}) async-start(), calls=%async_computation.37 | async-start | bytes 1536000 | tf_op jit(solution)/shard_map/all_gather | solution.py:241
  828.8 64.7 %reduce-scatter.71.cloned.1.call-start = ((), (), s32[]{:S(2)}) async-start(), calls=%async_computation.38 | async-start | bytes 3072000 | tf_op jit(solution)/shard_map/reduce_scatter | solution.py:248
  897.8 254.8 %reduce-scatter.73.cloned.1.call-start = ((), (), s32[]{:S(2)}) async-start(), calls=%async_computation.40 | async-start | bytes 3072000 | tf_op jit(solution)/shard_map/reduce_scatter | solution.py:248
  960.6 238.5 %reduce-scatter.85.cloned.1.call-start = ((), (), s32[]{:S(2)}) async-start(), calls=%async_computation.47 | async-start | bytes 2654208
  971.5 284.2 %reduce-scatter.81.cloned.1.call-start = ((), (), s32[]{:S(2)}) async-start(), calls=%async_computation.45 | async-start | bytes 7962624
  1011.1 490.9 %all-reduce.35.cloned.1.call-start = ((), (), s32[]{:S(2)}) async-start(), calls=%async_computation.49 | async-start | bytes 18874368
  1042.9 557.5 %reduce-scatter.77.cloned.1.call-start = ((), (), s32[]{:S(2)}) async-start(), calls=%async_computation.42 | async-start | bytes 5308416 | tf_op jit(solution)/shard_map/reduce_scatter | solution.py:532
  1049.2 650.4 %reduce-scatter.75.cloned.1.call-start = ((), (), s32[]{:S(2)}) async-start(), calls=%async_computation.41 | async-start | bytes 5308416 | tf_op jit(solution)/shard_map/reduce_scatter | solution.py:532
  1055.5 716.5 %reduce-scatter.83.cloned.1.call-start = ((), (), s32[]{:S(2)}) async-start(), calls=%async_computation.46 | async-start | bytes 2654208
  1119.2 781.3 %all-reduce.33.cloned.1.call-start = ((), (), s32[]{:S(2)}) async-start(), calls=%async_computation.48 | async-start | bytes 221184 | tf_op jit(solution)/shard_map/psum | solution.py:562
  1156.0 878.6 %reduce-scatter.79.cloned.1.call-start = ((), (), s32[]{:S(2)}) async-start(), calls=%async_computation.44 | async-start | bytes 7962624
  (357 other events, 4858.7 us)
Sparse Core Ops, SparseCore 0:
  14.8 20.4 all-gather.25
  58.7 33.6 reduce-scatter.50
  130.1 34.3 reduce-scatter.52
  193.6 33.6 reduce-scatter.54
  229.8 21.1 all-gather.31
  279.2 35.8 reduce-scatter.56
  373.0 34.5 reduce-scatter.58
  458.4 33.6 reduce-scatter.62
  494.6 34.9 reduce-scatter.60
  592.4 33.5 reduce-scatter.64
  697.8 36.8 reduce-scatter.66
  739.5 19.0 all-gather.41
  769.3 35.4 reduce-scatter.68
  828.9 19.1 all-gather.43
  859.3 34.1 reduce-scatter.70
  960.7 33.6 reduce-scatter.72
  998.4 68.9 reduce-scatter.84
  1071.0 128.0 reduce-scatter.80
  1203.4 298.5 all-reduce.34
  1506.1 94.2 reduce-scatter.76
  1604.5 94.9 reduce-scatter.74
  1703.3 68.7 reduce-scatter.82
  1779.6 120.7 all-reduce.32
  1904.6 129.9 reduce-scatter.78
  (8 shorter events, 143.3 us)
where the time goes:
time: 2060 us; the launch traced here: 2050 us
  waiting for transfers between devices  1000 us (49%)
  matrix products  400 us (19%)
  blocking collectives  263 us (13%)
  local copies, waits for them, and re-layouts  193 us (9%)
  other arithmetic  142 us (7%)
  between operations  25.1 us (1%)
  starting transfers between devices  22.8 us (1%)
    unnamed x49, waiting for transfers between devices  446 us
    reduce_scatter x2, waiting for transfers between devices, on_device(): lax.psum_scatter(mlp_in_grad, 'dp', scatter_dimension=1, tiled=True)  194 us
    unnamed x11, blocking collectives  136 us
    unnamed x734, local copies, waits for them, and re-layouts  133 us
    psum x1, waiting for transfers between devices, on_device(): lax.psum((stacked_small[0], stacked_small[1], stacked_small[2]), ('dp', '...  123 us
    reduce_scatter x6, waiting for transfers between devices, scatter_rows(): lax.psum_scatter(query_part, 'tensor', scatter_dimension=0, tiled=True)  84.9 us
    reduce_scatter x6, waiting for transfers between devices, scatter_grads(): lax.psum_scatter(query_part, 'tensor', scatter_dimension=0, tiled=True)  75 us
    all_gather x6, waiting for transfers between devices, gather_rows(): lax.all_gather(query_part, 'tensor', axis=0, tiled=True)  45.8 us
  transfers between devices with their start and end apart: 44, of which 21 were waited for; matrix products, arithmetic and copies ran while one was open for 29% of the time, Pallas kernels for 0%

commit v1 on v0

v1 whole, which is shorter than its diff:
```python
import jax
import jax.numpy as jnp
from jax import lax
from jax.experimental import pallas as pl
from jax.experimental.pallas import tpu as pltpu
from jax.sharding import PartitionSpec as P

HDIM = 64
WIN = 12
SPAN = 2 * WIN - 1
EPS = 1e-05
NEG = -1000000000.0
OUT = -1e30
F32 = jnp.float32
BF16 = jnp.bfloat16
VMEM_LIMIT = 44 * 2**20


def nn(a, b):
    return lax.dot_general(a, b, (((1,), (0,)), ((), ())), preferred_element_type=F32)


def nt(a, b):
    return lax.dot_general(a, b, (((1,), (1,)), ((), ())), preferred_element_type=F32)


def tn(a, b):
    return lax.dot_general(a, b, (((0,), (0,)), ((), ())), preferred_element_type=F32)


def call(body, outs, scalars, args, flops=0, name=None):
    vmem = pl.BlockSpec(memory_space=pltpu.VMEM)
    smem = pl.BlockSpec(memory_space=pltpu.SMEM)
    moved = sum(a.size * a.dtype.itemsize for a in list(args) + list(outs))
    return pl.pallas_call(
        body,
        out_shape=tuple(outs),
        in_specs=[smem] * len(scalars) + [vmem] * len(args),
        out_specs=tuple(vmem for _ in outs),
        compiler_params=pltpu.CompilerParams(vmem_limit_bytes=VMEM_LIMIT),
        cost_estimate=pl.CostEstimate(flops=flops, bytes_accessed=moved, transcendentals=0),
        name=name,
    )(*scalars, *args)


def shaped(shape, dtype=BF16):
    return jax.ShapeDtypeStruct(shape, dtype)


class Sizes:
    def __init__(self, vis, qlen):
        self.vis, self.qlen = vis, qlen
        self.vh, self.qh = vis // 2, qlen // 2
        self.vp = -(-self.vh // 16) * 16
        self.half = self.vp + self.qh
        self.vquart, self.qquart = vis // 4, qlen // 4


def iota(shape, dim):
    return lax.broadcasted_iota(jnp.int32, shape, dim)


def div12(x):
    return (x * 171) >> 11


def patch_of(index, core, sz):
    second = (index >= sz.vp).astype(jnp.int32)
    row = index - second * sz.vp
    half = second + core - 2 * second * core
    patch = row + jnp.where(row >= sz.vquart, sz.vquart, 0) + half * sz.vquart
    return jnp.where(row < sz.vh, patch, -1)


def query_of(index, core, sz):
    second = (index >= sz.qh).astype(jnp.int32)
    row = index - second * sz.qh
    half = second + core - 2 * second * core
    return row + jnp.where(row >= sz.qquart, sz.qquart, 0) + half * sz.qquart


def window_permutation(sc, sz):
    core, down, right = sc[0], sc[2], sc[3]
    place = iota((sz.vis, sz.vp), 0)
    a = div12(place)
    b = place - a * WIN
    a = a + down
    b = b + right
    a = jnp.where(a >= WIN, a - WIN, a)
    b = jnp.where(b >= WIN, b - WIN, b)
    source = a * WIN + b
    stored = iota((sz.vis, sz.vp), 1)
    mine = (source == patch_of(stored, core, sz)).astype(F32).astype(BF16)
    theirs = (source == patch_of(stored + sz.vp, core, sz)).astype(F32).astype(BF16)
    return mine, theirs


def window_class(index, sc):
    a = div12(index)
    b = index - a * WIN
    return jnp.where(a >= WIN - sc[2], 2, 0) + jnp.where(b >= WIN - sc[3], 1, 0)


def window_mask(sc, sz):
    keys = window_class(iota((sz.vis, 1), 0), sc)
    asks = window_class(iota((1, sz.vis), 1), sc)
    keys = jnp.where(sc[4] > 0, keys, -1)
    return keys == asks


def self_mask(sc, sz):
    keys = query_of(iota((sz.qlen, 1), 0), sc[0], sz)
    asks = query_of(iota((1, sz.qlen), 1), sc[0], sz)
    return keys <= jnp.maximum(asks, sc[1] - 1)


def question_mask(sc, sz):
    return query_of(iota((sz.qlen, 1), 0), sc[0], sz) < sc[1]


def patch_pad(sc, sz):
    return patch_of(iota((2 * sz.vp, 1), 0), sc[0], sz) >= 0


def masked(scores, kind, sc, sz):
    if kind == "self":
        return jnp.where(self_mask(sc, sz), scores, NEG)
    if kind == "question":
        return jnp.where(question_mask(sc, sz), scores, NEG)
    if kind == "window":
        return jnp.where(window_mask(sc, sz), scores, NEG)
    real = patch_pad(sc, sz)
    return jnp.where(real & (sc[4] > 0), scores, jnp.where(real, NEG, OUT))


def allowed(kind, sc, sz):
    if kind == "self":
        return self_mask(sc, sz)
    if kind == "question":
        return question_mask(sc, sz)
    if kind == "window":
        return window_mask(sc, sz)
    return patch_pad(sc, sz) & (sc[4] > 0)


SCALE = HDIM**-0.5


def attend(q, k, v, addend, kind, sc, sz):
    scores = nt(k, q) * SCALE
    if addend is not None:
        scores = scores + addend
    scores = masked(scores, kind, sc, sz)
    top = jnp.max(scores, 0, keepdims=True)
    e = jnp.exp(scores - top)
    inv = 1.0 / jnp.sum(e, 0, keepdims=True)
    o_t = tn(v, (e * inv).astype(BF16))
    return o_t, top, inv


def attend_back(q, k, v, addend, kind, sc, sz, top, inv, do):
    scores = nt(k, q) * SCALE
    if addend is not None:
        scores = scores + addend
    scores = masked(scores, kind, sc, sz)
    p = jnp.exp(scores - top) * inv
    dv = nn(p.astype(BF16), do)
    dp = nt(v, do)
    ds = p * (dp - jnp.sum(p * dp, 0, keepdims=True))
    ds = jnp.where(allowed(kind, sc, sz), ds, 0.0).astype(BF16)
    dk = nn(ds, q) * SCALE
    dq = tn(k, ds) * SCALE
    return dq, dk, dv, ds


def head(ref, part, h, heads):
    start = (part * heads + h) * HDIM
    return ref[:, start : start + HDIM]


def run_heads(q_of, k_of, v_of, bias, kind, sc, sz, o_ref, st_ref, heads):
    outs = []
    for h in range(heads):
        o_t, top, inv = attend(
            q_of(h), k_of(h), v_of(h), None if bias is None else bias[h], kind, sc, sz
        )
        outs.append(o_t)
        st_ref[h : h + 1, :] = top
        st_ref[heads + h : heads + h + 1, :] = inv
    o_ref[...] = jnp.concatenate(outs, 0).T.astype(BF16)


def section1(sz, heads, sc, nm, nth, w0, w1, wo0, wo1, bias, pm, pt, nvw, qkvv, ov, stv, qkvq, oq, stq, ow):
    vp, qh = sz.vp, sz.qh
    mine, theirs = window_permutation(sc, sz)
    nv = (nn(mine, nm[0:vp, :]) + nn(theirs, nth[0:vp, :])).astype(BF16)
    nvw[...] = nv
    qkvv[...] = nt(nv, w0[...]).astype(BF16)
    run_heads(
        lambda h: head(qkvv, 0, h, heads),
        lambda h: head(qkvv, 1, h, heads),
        lambda h: head(qkvv, 2, h, heads),
        bias, "window", sc, sz, ow, stv, heads,
    )
    ov[0:vp, :] = tn(mine, ow[...]).astype(BF16)
    ov[vp : 2 * vp, :] = tn(theirs, ow[...]).astype(BF16)
    pm[0:vp, :] = nn(ov[0:vp, :], wo0[...]).astype(BF16)
    pt[0:vp, :] = nn(ov[vp : 2 * vp, :], wo0[...]).astype(BF16)
    qkvq[0:qh, :] = nt(nm[vp:, :], w1[...]).astype(BF16)
    qkvq[qh:, :] = nt(nth[vp:, :], w1[...]).astype(BF16)
    run_heads(
        lambda h: head(qkvq, 0, h, heads),
        lambda h: head(qkvq, 1, h, heads),
        lambda h: head(qkvq, 2, h, heads),
        None, "self", sc, sz, oq, stq, heads,
    )
    pm[vp:, :] = nn(oq[0:qh, :], wo1[...]).astype(BF16)
    pt[vp:, :] = nn(oq[qh:, :], wo1[...]).astype(BF16)


def section2(sz, heads, sc, nm, nth, w2, w3, wo2, wo3, pm, pt, qq, kvv, oq, stq, qv, kvq, ov, stv):
    vp, qh = sz.vp, sz.qh
    e = heads * HDIM
    for rows, ref in ((slice(0, qh), nm), (slice(qh, 2 * qh), nth)):
        x = ref[vp:, :]
        qq[rows, :] = nt(x, w2[0:e, :]).astype(BF16)
        kvq[rows, :] = nt(x, w3[e:, :]).astype(BF16)
    for rows, ref in ((slice(0, vp), nm), (slice(vp, 2 * vp), nth)):
        x = ref[0:vp, :]
        qv[rows, :] = nt(x, w3[0:e, :]).astype(BF16)
        kvv[rows, :] = nt(x, w2[e:, :]).astype(BF16)
    run_heads(
        lambda h: head(qq, 0, h, heads),
        lambda h: head(kvv, 0, h, heads),
        lambda h: head(kvv, 1, h, heads),
        None, "patch", sc, sz, oq, stq, heads,
    )
    run_heads(
        lambda h: head(qv, 0, h, heads),
        lambda h: head(kvq, 0, h, heads),
        lambda h: head(kvq, 1, h, heads),
        None, "question", sc, sz, ov, stv, heads,
    )
    pm[0:vp, :] = nn(ov[0:vp, :], wo3[...]).astype(BF16)
    pt[0:vp, :] = nn(ov[vp:, :], wo3[...]).astype(BF16)
    pm[vp:, :] = nn(oq[0:qh, :], wo2[...]).astype(BF16)
    pt[vp:, :] = nn(oq[qh:, :], wo2[...]).astype(BF16)


GELU_C = 0.7978845608028654
GELU_A = 0.044715


def section3(sz, nm, nth, wi, bi, wo, pm, pt, g, gp):
    vp, half = sz.vp, sz.half
    for ref, out, base in ((nm, pm, 0), (nth, pt, half)):
        for lo, hi, e in ((0, vp, 0), (vp, half, 1)):
            h = nn(ref[lo:hi, :], wi[e]) + bi[e : e + 1, :]
            h2 = h * h
            t = jnp.tanh(GELU_C * h * (1.0 + GELU_A * h2))
            half_t = 0.5 + 0.5 * t
            act = (h * half_t).astype(BF16)
            slope = half_t + (0.5 * GELU_C) * h * (1.0 - t * t) * (1.0 + 3.0 * GELU_A * h2)
            g[base + lo : base + hi, :] = act
            gp[base + lo : base + hi, :] = slope.astype(BF16)
            out[lo:hi, :] = nn(act, wo[e]).astype(BF16)


def section3_back(sz, dm, dt, wi, wo, gp, pm, pt, dh):
    vp, half = sz.vp, sz.half
    for ref, out, base in ((dm, pm, 0), (dt, pt, half)):
        for lo, hi, e in ((0, vp, 0), (vp, half, 1)):
            dg = nt(ref[lo:hi, :], wo[e])
            d = (dg * gp[base + lo : base + hi, :].astype(F32)).astype(BF16)
            dh[base + lo : base + hi, :] = d
            out[lo:hi, :] = nt(d, wi[e]).astype(BF16)


def back_heads(q_of, k_of, v_of, bias, kind, sc, sz, st, do_of, ds_ref, heads):
    dqs, dks, dvs = [], [], []
    for h in range(heads):
        dq, dk, dv, ds = attend_back(
            q_of(h), k_of(h), v_of(h), None if bias is None else bias[h], kind, sc, sz,
            st[h : h + 1, :], st[heads + h : heads + h + 1, :], do_of(h),
        )
        dqs.append(dq)
        dks.append(dk)
        dvs.append(dv)
        if ds_ref is not None:
            ds_ref[h] = ds
    dq = jnp.concatenate(dqs, 0).T.astype(BF16)
    dkv = jnp.concatenate(dks + dvs, 1).astype(BF16)
    return dq, dkv


def section2_back(sz, heads, sc, dm, dt, w2, w3, wo2, wo3, qq, kvv, stq, qv, kvq, stv, pm, pt, dqq, dkvv, dqv, dkvq, doq, dov):
    vp, qh = sz.vp, sz.qh
    e = heads * HDIM
    doq[0:qh, :] = nt(dm[vp:, :], wo2[...]).astype(BF16)
    doq[qh:, :] = nt(dt[vp:, :], wo2[...]).astype(BF16)
    dov[0:vp, :] = nt(dm[0:vp, :], wo3[...]).astype(BF16)
    dov[vp:, :] = nt(dt[0:vp, :], wo3[...]).astype(BF16)
    dq, dkv = back_heads(
        lambda h: head(qq, 0, h, heads),
        lambda h: head(kvv, 0, h, heads),
        lambda h: head(kvv, 1, h, heads),
        None, "patch", sc, sz, stq, lambda h: head(doq, 0, h, heads), None, heads,
    )
    dqq[...] = dq
    dkvv[...] = dkv
    dq, dkv = back_heads(
        lambda h: head(qv, 0, h, heads),
        lambda h: head(kvq, 0, h, heads),
        lambda h: head(kvq, 1, h, heads),
        None, "question", sc, sz, stv, lambda h: head(dov, 0, h, heads), None, heads,
    )
    dqv[...] = dq
    dkvq[...] = dkv
    for out, qrow, vrow in ((pm, slice(0, qh), slice(0, vp)), (pt, slice(qh, 2 * qh), slice(vp, 2 * vp))):
        out[vp:, :] = (nn(dqq[qrow, :], w2[0:e, :]) + nn(dkvq[qrow, :], w3[e:, :])).astype(BF16)
        out[0:vp, :] = (nn(dqv[vrow, :], w3[0:e, :]) + nn(dkvv[vrow, :], w2[e:, :])).astype(BF16)


def section1_back(sz, heads, sc, dm, dt, w0, w1, wo0, wo1, bias, qkvv, stv, qkvq, stq, pm, pt, dqkvv, dqkvq, ds, doq, dov):
    vp, qh = sz.vp, sz.qh
    e = heads * HDIM
    mine, theirs = window_permutation(sc, sz)
    do_m = nt(dm[0:vp, :], wo0[...]).astype(BF16)
    do_t = nt(dt[0:vp, :], wo0[...]).astype(BF16)
    dov[...] = (nn(mine, do_m) + nn(theirs, do_t)).astype(BF16)
    dq, dkv = back_heads(
        lambda h: head(qkvv, 0, h, heads),
        lambda h: head(qkvv, 1, h, heads),
        lambda h: head(qkvv, 2, h, heads),
        bias, "window", sc, sz, stv, lambda h: head(dov, 0, h, heads), ds, heads,
    )
    dqkvv[:, 0:e] = dq
    dqkvv[:, e:] = dkv
    dn = nn(dqkvv[...], w0[...]).astype(BF16)
    pm[0:vp, :] = tn(mine, dn).astype(BF16)
    pt[0:vp, :] = tn(theirs, dn).astype(BF16)
    doq[0:qh, :] = nt(dm[vp:, :], wo1[...]).astype(BF16)
    doq[qh:, :] = nt(dt[vp:, :], wo1[...]).astype(BF16)
    dq, dkv = back_heads(
        lambda h: head(qkvq, 0, h, heads),
        lambda h: head(qkvq, 1, h, heads),
        lambda h: head(qkvq, 2, h, heads),
        None, "self", sc, sz, stq, lambda h: head(doq, 0, h, heads), None, heads,
    )
    dqkvq[:, 0:e] = dq
    dqkvq[:, e:] = dkv
    pm[vp:, :] = nn(dqkvq[0:qh, :], w1[...]).astype(BF16)
    pt[vp:, :] = nn(dqkvq[qh:, :], w1[...]).astype(BF16)


def store_blocks(sc, out, col, value):
    value = value.astype(BF16)
    blocks, rows = out.shape[0], out.shape[1]
    width = value.shape[1]
    ring = blocks // 2
    for d in range(blocks):
        if blocks == 1:
            slot = 0
        else:
            flip = (d % 2) + sc[5] - 2 * (d % 2) * sc[5]
            away = d // 2 - sc[6]
            away = jnp.where(away < 0, away + ring, away)
            slot = flip * ring + away
        out[slot, :, col : col + width] = value[d * rows : (d + 1) * rows, :]


def section3_weights(sz, sc, nm, nth, dm, dt, g, dh, out, db):
    vp, half = sz.vp, sz.half
    hid = g.shape[1]
    for e, lo, hi in ((0, 0, vp), (1, vp, half)):
        store_blocks(sc, out, e * hid, tn(nm[lo:hi, :], dh[lo:hi, :]) + tn(nth[lo:hi, :], dh[half + lo : half + hi, :]))
        store_blocks(
            sc, out, (2 + e) * hid, tn(dm[lo:hi, :], g[lo:hi, :]) + tn(dt[lo:hi, :], g[half + lo : half + hi, :])
        )
        db[e : e + 1, :] = jnp.sum(dh[lo:hi, :].astype(F32), 0, keepdims=True) + jnp.sum(
            dh[half + lo : half + hi, :].astype(F32), 0, keepdims=True
        )


def section2_weights(sz, heads, sc, nm, nth, dm, dt, dqq, dkvv, dqv, dkvq, oq, ov, out):
    vp, qh = sz.vp, sz.qh
    e = heads * HDIM

    def both(a_m, a_t, b, cut, lo, hi):
        return tn(a_m[lo:hi, :], b[0:cut, :]) + tn(a_t[lo:hi, :], b[cut:, :])

    store_blocks(sc, out, 0, both(nm, nth, dqq, qh, vp, sz.half))
    store_blocks(sc, out, e, both(nm, nth, dkvv, vp, 0, vp))
    store_blocks(sc, out, 3 * e, both(nm, nth, dqv, vp, 0, vp))
    store_blocks(sc, out, 4 * e, both(nm, nth, dkvq, qh, vp, sz.half))
    store_blocks(sc, out, 6 * e, both(dm, dt, oq, qh, vp, sz.half))
    store_blocks(sc, out, 7 * e, both(dm, dt, ov, vp, 0, vp))


def section1_weights(sz, heads, sc, nm, nth, dm, dt, nvw, dqkvv, dqkvq, oq, ov, out):
    vp, qh = sz.vp, sz.qh
    e = heads * HDIM

    def both(a_m, a_t, b, cut, lo, hi):
        return tn(a_m[lo:hi, :], b[0:cut, :]) + tn(a_t[lo:hi, :], b[cut:, :])

    store_blocks(sc, out, 0, tn(nvw[...], dqkvv[...]))
    store_blocks(sc, out, 3 * e, both(nm, nth, dqkvq, qh, vp, sz.half))
    store_blocks(sc, out, 6 * e, both(dm, dt, ov, vp, 0, vp))
    store_blocks(sc, out, 7 * e, both(dm, dt, oq, qh, vp, sz.half))


def norm_rows(x):
    center = x - jnp.mean(x, -1, keepdims=True)
    inv = lax.rsqrt(jnp.mean(center * center, -1, keepdims=True) + EPS)
    return center * inv, inv


def first_norm(sz, x, scale, shift, n):
    for lo, hi, e in ((0, sz.vp, 0), (sz.vp, sz.half, 1)):
        n[lo:hi, :] = (norm_rows(x[lo:hi, :])[0] * scale[e : e + 1, :] + shift[e : e + 1, :]).astype(BF16)


def add_norm(sz, x, a, b, extra, scale, shift, y, n):
    for lo, hi, e in ((0, sz.vp, 0), (sz.vp, sz.half, 1)):
        value = x[lo:hi, :] + (a[lo:hi, :].astype(F32) + b[lo:hi, :].astype(F32)) + extra[e : e + 1, :]
        y[lo:hi, :] = value
        n[lo:hi, :] = (norm_rows(value)[0] * scale[e : e + 1, :] + shift[e : e + 1, :]).astype(BF16)


def norm_back(sz, d, a, b, x, scale, out, dy, sums):
    for lo, hi, e in ((0, sz.vp, 0), (sz.vp, sz.half, 1)):
        dn = a[lo:hi, :].astype(F32) + b[lo:hi, :].astype(F32)
        unit, inv = norm_rows(x[lo:hi, :])
        du = dn * scale[e : e + 1, :]
        dnu = dn * unit
        dx = inv * (
            du
            - jnp.mean(du, -1, keepdims=True)
            - unit * jnp.mean(du * unit, -1, keepdims=True)
        )
        value = d[lo:hi, :] + dx
        out[lo:hi, :] = value
        dy[lo:hi, :] = value.astype(BF16)
        sums[e : e + 1, :] = jnp.sum(dnu, 0, keepdims=True)
        sums[2 + e : 3 + e, :] = jnp.sum(dn, 0, keepdims=True)
        sums[4 + e : 5 + e, :] = jnp.sum(value, 0, keepdims=True)


def table_bias(table):
    heads = table.shape[0]
    grid = table.reshape(heads, SPAN, SPAN)
    cols = jnp.stack([grid[:, :, WIN - 1 - u : SPAN - u] for u in range(WIN)], 1)
    cols = cols.reshape(heads, WIN, SPAN * WIN)
    first = [(WIN - 1 - u) * WIN for u in range(WIN)]
    rows = jnp.stack([cols[:, :, f : f + WIN * WIN] for f in first], 1)
    return rows.reshape(heads, WIN * WIN, WIN * WIN)


def table_grad(ds):
    heads = ds.shape[0]
    rows = ds.astype(F32).reshape(heads, WIN, WIN, WIN * WIN)
    total = SPAN * WIN
    cols = sum(
        jnp.pad(rows[:, u], ((0, 0), (0, 0), ((WIN - 1 - u) * WIN, total - (WIN - 1 - u) * WIN - WIN * WIN)))
        for u in range(WIN)
    )
    cols = cols.reshape(heads, WIN, SPAN, WIN)
    grid = sum(jnp.pad(cols[:, u], ((0, 0), (0, 0), (WIN - 1 - u, u))) for u in range(WIN))
    return grid.reshape(heads, SPAN * SPAN)


def on_device(
    dp_size,
    visual,
    queries,
    valid_windows,
    answer_start,
    shifts,
    norm_scale,
    norm_shift,
    attn_in,
    attn_out,
    rel_bias,
    mlp_in,
    mlp_in_bias,
    mlp_out,
    mlp_out_bias,
    grad_visual_out,
    grad_query_out,
):
    layers, width = attn_in.shape[0], attn_in.shape[2]
    edev = attn_in.shape[4]
    heads = edev // HDIM
    hid = mlp_in.shape[3]
    sz = Sizes(4 * visual.shape[1], 4 * queries.shape[1])
    half, vp, qh = sz.half, sz.vp, sz.qh
    vq, qq_ = sz.vquart, sz.qquart
    t_index = lax.axis_index("tensor")
    d_index = lax.axis_index("dp")
    core, chip = t_index % 2, t_index // 2
    swap = [(i, i ^ 1) for i in range(4)]
    cross = [(i, i ^ 2) for i in range(4)]
    block_rows = width // dp_size
    ring_ok = dp_size % 2 == 0 and block_rows % 16 == 0
    blocks = dp_size if ring_ok else 1
    ring = dp_size // 2

    def scalars(layer):
        on = layer % 2
        return jnp.stack(
            [
                core,
                answer_start[0],
                shifts[0, 0] * on,
                shifts[0, 1] * on,
                valid_windows[0, 0],
                d_index % 2,
                d_index // 2,
                0,
            ]
        ).astype(jnp.int32)

    w_in = attn_in.transpose(0, 1, 3, 4, 2).reshape(layers, 4, 3 * edev, width)

    def to_half(own_v, own_q):
        packed = jnp.concatenate([own_v, own_q], 0)
        other = lax.ppermute(packed, "tensor", cross)
        first = jnp.where(chip == 0, packed, other)
        second = jnp.where(chip == 0, other, packed)
        pad = jnp.zeros((vp - 2 * vq, width), packed.dtype)
        return jnp.concatenate([first[:vq], second[:vq], pad, first[vq:], second[vq:]], 0)

    def own_rows(rows):
        v = jnp.where(chip == 0, rows[0:vq], rows[vq : 2 * vq])
        q = jnp.where(chip == 0, rows[vp : vp + qq_], rows[vp + qq_ :])
        return v, q

    def total(mine, theirs):
        got = lax.ppermute(theirs, "tensor", swap)
        kept = (mine.astype(F32) + got.astype(F32)).astype(BF16)
        return kept, lax.ppermute(kept, "tensor", cross)

    stream = to_half(visual[0], queries[0]).astype(F32)
    grad_rounded = [lax.reduce_precision(g[0], 8, 7) for g in (grad_visual_out, grad_query_out)]
    scal = [scalars(layer) for layer in range(layers)]
    biases = [table_bias(rel_bias[layer]) for layer in range(layers)]
    rows_bf = shaped((half, width))
    rows_f = shaped((half, width), F32)
    mac = 2 * half * width

    def pair(x):
        return x, lax.ppermute(x, "tensor", swap)

    zero_bias = jnp.zeros((2, width), F32)
    (normed,) = call(
        lambda *r: first_norm(sz, *r),
        [rows_bf],
        [],
        [stream, norm_scale[0, 0:2], norm_shift[0, 0:2]],
        name="norm",
    )
    saved = []
    for layer in range(layers):
        sc = scal[layer]
        nm, nth = pair(normed)
        part = call(
            lambda *r: section1(sz, heads, *r),
            [
                rows_bf,
                rows_bf,
                shaped((sz.vis, width)),
                shaped((sz.vis, 3 * edev)),
                shaped((2 * vp, edev)),
                shaped((8, sz.vis), F32),
                shaped((sz.qlen, 3 * edev)),
                shaped((sz.qlen, edev)),
                shaped((8, sz.qlen), F32),
                shaped((sz.vis, edev)),
            ],
            [sc],
            [nm, nth, w_in[layer, 0], w_in[layer, 1], attn_out[layer, 0], attn_out[layer, 1], biases[layer]],
            flops=mac * 4 * edev * 2 + 8 * heads * HDIM * sz.qlen * sz.qlen,
            name="section1",
        )
        kept1 = (stream, nm, nth) + tuple(part[2:9])
        a, b = total(part[0], part[1])
        stream, normed = call(
            lambda *r: add_norm(sz, *r),
            [rows_f, rows_bf],
            [],
            [stream, a, b, zero_bias, norm_scale[layer, 2:4], norm_shift[layer, 2:4]],
            name="norm",
        )
        nm, nth = pair(normed)
        part = call(
            lambda *r: section2(sz, heads, *r),
            [
                rows_bf,
                rows_bf,
                shaped((sz.qlen, edev)),
                shaped((2 * vp, 2 * edev)),
                shaped((sz.qlen, edev)),
                shaped((8, sz.qlen), F32),
                shaped((2 * vp, edev)),
                shaped((sz.qlen, 2 * edev)),
                shaped((2 * vp, edev)),
                shaped((8, 2 * vp), F32),
            ],
            [sc],
            [nm, nth, w_in[layer, 2], w_in[layer, 3], attn_out[layer, 2], attn_out[layer, 3]],
            flops=mac * 4 * edev * 2,
            name="section2",
        )
        kept2 = (stream, nm, nth) + tuple(part[2:])
        a, b = total(part[0], part[1])
        stream, normed = call(
            lambda *r: add_norm(sz, *r),
            [rows_f, rows_bf],
            [],
            [stream, a, b, zero_bias, norm_scale[layer, 4:6], norm_shift[layer, 4:6]],
            name="norm",
        )
        nm, nth = pair(normed)
        part = call(
            lambda *r: section3(sz, *r),
            [rows_bf, rows_bf, shaped((2 * half, hid)), shaped((2 * half, hid))],
            [],
            [nm, nth, mlp_in[layer], mlp_in_bias[layer], mlp_out[layer]],
            flops=mac * hid * 4,
            name="section3",
        )
        kept3 = (stream, nm, nth) + tuple(part[2:])
        saved.append((kept1, kept2, kept3))
        a, b = total(part[0], part[1])
        if layer + 1 < layers:
            stream, normed = call(
                lambda *r: add_norm(sz, *r),
                [rows_f, rows_bf],
                [],
                [stream, a, b, mlp_out_bias[layer], norm_scale[layer + 1, 0:2], norm_shift[layer + 1, 0:2]],
                name="norm",
            )
        else:
            added = stream + (a.astype(F32) + b.astype(F32))
            out_v, out_q = own_rows(added)
            out_v = (out_v + mlp_out_bias[layer, 0]).astype(BF16)
            out_q = (out_q + mlp_out_bias[layer, 1]).astype(BF16)

    dy = to_half(*(g.astype(BF16) for g in grad_rounded))
    grad = dy.astype(F32)
    bias_sums = jnp.stack([jnp.sum(grad[:vp], 0), jnp.sum(grad[vp:], 0)])

    def reduce_weights(parts):
        if not ring_ok:
            return lax.psum_scatter(parts[0].astype(F32), "dp", scatter_dimension=0, tiled=True)
        flip = [(i, i ^ 1) for i in range(dp_size)]
        onward = [(i, (i + 2) % dp_size) for i in range(dp_size)]
        got = lax.ppermute(parts[ring:], "dp", flip)
        if ring == 1:
            return parts[0].astype(F32) + got[0].astype(F32)
        moving = parts[ring - 1].astype(F32) + got[ring - 1].astype(F32)
        for away in reversed(range(ring - 1)):
            moving = lax.ppermute(moving.astype(BF16), "dp", onward).astype(F32)
            moving = moving + (parts[away].astype(F32) + got[away].astype(F32))
        return moving

    def close(grad, a, b, kept, layer, first):
        return call(
            lambda *r: norm_back(sz, *r),
            [rows_f, rows_bf, shaped((8, width), F32)],
            [],
            [grad, a, b, kept[0], norm_scale[layer, first : first + 2]],
            name="norm_back",
        )

    grads = [None] * layers
    for layer in reversed(range(layers)):
        sc = scal[layer]
        kept1, kept2, kept3 = saved[layer]
        dm, dt = pair(dy)
        _, nm, nth, act, slope = kept3
        pm, pt, dh = call(
            lambda *r: section3_back(sz, *r),
            [rows_bf, rows_bf, shaped((2 * half, hid))],
            [],
            [dm, dt, mlp_in[layer], mlp_out[layer], slope],
            flops=mac * hid * 4,
            name="section3_back",
        )
        a, b = total(pm, pt)
        w3, db = call(
            lambda *r: section3_weights(sz, *r),
            [shaped((blocks, width // blocks, 4 * hid)), shaped((2, hid), F32)],
            [sc],
            [nm, nth, dm, dt, act, dh],
            flops=mac * hid * 4,
            name="section3_weights",
        )
        out_bias_sums = bias_sums
        grad, dy, sums3 = close(grad, a, b, kept3, layer, 4)

        dm, dt = pair(dy)
        _, nm, nth, qq, kvv, oq, stq, qv, kvq, ov, stv = kept2
        part = call(
            lambda *r: section2_back(sz, heads, *r),
            [
                rows_bf,
                rows_bf,
                shaped((sz.qlen, edev)),
                shaped((2 * vp, 2 * edev)),
                shaped((2 * vp, edev)),
                shaped((sz.qlen, 2 * edev)),
                shaped((sz.qlen, edev)),
                shaped((2 * vp, edev)),
            ],
            [sc],
            [dm, dt, w_in[layer, 2], w_in[layer, 3], attn_out[layer, 2], attn_out[layer, 3], qq, kvv, stq, qv, kvq, stv],
            flops=mac * 4 * edev * 2,
            name="section2_back",
        )
        a, b = total(part[0], part[1])
        (w2,) = call(
            lambda *r: section2_weights(sz, heads, *r),
            [shaped((blocks, width // blocks, 8 * edev))],
            [sc],
            [nm, nth, dm, dt, part[2], part[3], part[4], part[5], oq, ov],
            flops=mac * 4 * edev * 2,
            name="section2_weights",
        )
        grad, dy, sums2 = close(grad, a, b, kept2, layer, 2)

        dm, dt = pair(dy)
        _, nm, nth, nvw, qkvv, ov, stv, qkvq, oq, stq = kept1
        part = call(
            lambda *r: section1_back(sz, heads, *r),
            [
                rows_bf,
                rows_bf,
                shaped((sz.vis, 3 * edev)),
                shaped((sz.qlen, 3 * edev)),
                shaped((heads, sz.vis, sz.vis)),
                shaped((sz.qlen, edev)),
                shaped((sz.vis, edev)),
            ],
            [sc],
            [
                dm, dt, w_in[layer, 0], w_in[layer, 1], attn_out[layer, 0], attn_out[layer, 1],
                biases[layer], qkvv, stv, qkvq, stq,
            ],
            flops=mac * 4 * edev * 2 + 20 * heads * HDIM * sz.qlen * sz.qlen,
            name="section1_back",
        )
        a, b = total(part[0], part[1])
        (w1,) = call(
            lambda *r: section1_weights(sz, heads, *r),
            [shaped((blocks, width // blocks, 8 * edev))],
            [sc],
            [nm, nth, dm, dt, nvw, part[2], part[3], oq, ov],
            flops=mac * 4 * edev * 2,
            name="section1_weights",
        )
        table = table_grad(part[4])
        grad, dy, sums1 = close(grad, a, b, kept1, layer, 0)
        bias_sums = sums1[4:6]

        w3, w2, w1 = reduce_weights(w3), reduce_weights(w2), reduce_weights(w1)
        grads[layer] = (w3, w2, w1, db, table, sums1, sums2, sums3, out_bias_sums)

    rest_v = grad_visual_out[0] - grad_rounded[0]
    rest_q = grad_query_out[0] - grad_rounded[1]
    own_v, own_q = own_rows(grad)
    grad_v, grad_q = own_v + rest_v, own_q + rest_q

    def summed(x, axis, size, bits):
        for bit in bits:
            x = x + lax.ppermute(x, axis, [(i, i ^ bit) for i in range(size)])
        return x

    dp_bits = [1 << k for k in range(dp_size.bit_length() - 1)]
    norms = jnp.stack(
        [
            jnp.concatenate([g[5][0:4], g[6][0:4], g[7][0:4], g[8]], 0)
            for g in grads
        ]
    )
    norms = summed(norms, "tensor", 4, [1])
    local = jnp.concatenate([jnp.concatenate([g[3].reshape(-1), g[4].reshape(-1)]) for g in grads])
    packed = jnp.concatenate([norms.reshape(-1), local])
    packed = summed(packed, "dp", dp_size, dp_bits)
    norms = packed[: norms.size].reshape(norms.shape)
    local = packed[norms.size :].reshape(layers, -1)
    scale_total = jnp.concatenate([norms[:, 0:2], norms[:, 4:6], norms[:, 8:10]], 1)
    shift_total = jnp.concatenate([norms[:, 2:4], norms[:, 6:8], norms[:, 10:12]], 1)
    out_bias_total = norms[:, 12:14]
    in_bias_total = local[:, : 2 * hid].reshape(layers, 2, hid)
    rel_total = local[:, 2 * hid :].reshape(layers, heads, SPAN * SPAN)

    def projections(w):
        return [w[:, k * edev : (k + 1) * edev] for k in range(8)]

    d_in, d_out, d_up, d_down = [], [], [], []
    for g in grads:
        one, two = projections(g[2]), projections(g[1])
        d_in.append(
            jnp.stack([jnp.stack(p, 0) for p in (one[0:3], one[3:6], two[0:3], two[3:6])])
        )
        d_out.append(jnp.stack([one[6].T, one[7].T, two[6].T, two[7].T]))
        d_up.append(jnp.stack([g[0][:, 0:hid], g[0][:, hid : 2 * hid]]))
        d_down.append(jnp.stack([g[0][:, 2 * hid : 3 * hid], g[0][:, 3 * hid :]]))
    return (
        out_v[None],
        out_q[None],
        grad_v[None],
        grad_q[None],
        scale_total,
        shift_total,
        jnp.stack(d_in).transpose(0, 1, 3, 2, 4),
        jnp.stack(d_out),
        rel_total,
        jnp.stack(d_up),
        in_bias_total,
        jnp.stack(d_down).transpose(0, 1, 3, 2),
        out_bias_total,
    )


def solution(mesh):
    dp_size = mesh.shape["dp"]
    return jax.shard_map(
        lambda *args: on_device(dp_size, *args),
        mesh=mesh,
        in_specs=(
            P("dp", "tensor", None),
            P("dp", "tensor", None),
            P("dp", None),
            P("dp"),
            P("dp", None),
            P(),
            P(),
            P(None, None, None, None, "tensor"),
            P(None, None, "tensor", None),
            P(None, "tensor", None),
            P(None, None, None, "tensor"),
            P(None, None, "tensor"),
            P(None, None, "tensor", None),
            P(),
            P("dp", "tensor", None),
            P("dp", "tensor", None),
        ),
        out_specs=(
            P("dp", "tensor", None),
            P("dp", "tensor", None),
            P("dp", "tensor", None),
            P("dp", "tensor", None),
            P(),
            P(),
            P(None, None, "dp", None, "tensor"),
            P(None, None, "tensor", "dp"),
            P(None, "tensor", None),
            P(None, None, "dp", "tensor"),
            P(None, None, "tensor"),
            P(None, None, "tensor", "dp"),
            P(),
        ),
        check_vma=False,
    )
```

time: 2060 us -> 708 us (0.34)
  waiting for transfers between devices: 1000 us -> 288 us
  matrix products: 400 us -> 0 us
  blocking collectives: 263 us -> 0 us
  Pallas kernels: 0 us -> 147 us
  other arithmetic: 142 us -> 57.9 us
  local copies, waits for them, and re-layouts: 193 us -> 151 us
  starting transfers between devices: 22.8 us -> 52.6 us
    unnamed x49 -> x0, waiting for transfers between devices: 446 us -> none
    dot_general x132 -> x0, matrix products: 362 us -> none  [the longest x8 43.5 us: core_backward(): jnp.einsum('bhqk,bhqd->bhkd', grad_scores, queries_h, preferred_element_t...]
    reduce_scatter x14 -> x0, waiting for transfers between devices: 354 us -> none  [the longest x2 194 us: on_device(): lax.psum_scatter(mlp_in_grad, 'dp', scatter_dimension=1, tiled=True)]
    ppermute x0 -> x66, waiting for transfers between devices: none -> 288 us  [the longest x12 129 us: total(): return (kept, lax.ppermute(kept, 'tensor', cross))]
    pallas_call x0 -> x30, Pallas kernels: none -> 147 us  [call(): pl.pallas_call(body, out_shape=tuple(outs), in_specs=[smem] * len(scalars...]
    unnamed x11 -> x0, blocking collectives: 136 us -> none
    psum x1 -> x0, waiting for transfers between devices: 123 us -> none  [on_device(): lax.psum((stacked_small[0], stacked_small[1], stacked_small[2]), ('dp', '...]
    all_gather x12 -> x0, blocking collectives: 86.6 us -> none  [the longest x6 44.4 us: gather_rows(): lax.all_gather(visual_part, 'tensor', axis=0, tiled=True)]
  transfers between devices with their start and end apart: 44 -> 66, of which waited for: 21 -> 32; matrix products, arithmetic and copies ran while one was open for 29% -> 20% of each run, Pallas kernels for 0% -> 11%
where the time goes in v1:
time: 708 us; the launch traced here: 702 us
  waiting for transfers between devices  288 us (41%)
  local copies, waits for them, and re-layouts  151 us (21%)
  Pallas kernels  147 us (21%)
  other arithmetic  57.9 us (8%)
  starting transfers between devices  52.6 us (7%)
    pallas_call x30, Pallas kernels, call(): pl.pallas_call(body, out_shape=tuple(outs), in_specs=[smem] * len(scalars...  147 us
    ppermute x12, waiting for transfers between devices, total(): return (kept, lax.ppermute(kept, 'tensor', cross))  129 us
    unnamed x523, local copies, waits for them, and re-layouts  67.6 us
    ppermute x6, waiting for transfers between devices, reduce_weights(): got = lax.ppermute(parts[ring:], 'dp', flip)  64.3 us
    ppermute x18, waiting for transfers between devices, reduce_weights(): moving = lax.ppermute(moving.astype(BF16), 'dp', onward).astype(F32)  49.8 us
    ppermute x4, waiting for transfers between devices, summed(): x = x + lax.ppermute(x, axis, [(i, i ^ bit) for i in range(size)])  20.9 us
    convert_element_type x18, other arithmetic, reduce_weights(): moving = lax.ppermute(moving.astype(BF16), 'dp', onward).astype(F32)  20 us
    ppermute x12, starting transfers between devices, total(): return (kept, lax.ppermute(kept, 'tensor', cross))  18.8 us
  transfers between devices with their start and end apart: 66, of which 32 were waited for; matrix products, arithmetic and copies ran while one was open for 20% of the time, Pallas kernels for 11%

profile of v1, /device:TPU:0, one launch (start us, length us, event | category | flops | bytes accessed | tf_op | source)
XLA Modules:
  0.0 701.7 jit_solution(11342057763601009661)
XLA Ops:
  36.4 9.1 %section1.2 = (bf16[480,768]{1,0:T(8,128)(2,1)S(1)}, bf16[480,768]{1,0:T(8,128)(2,1)S(1)}, bf16[144,768]{1,0:T(8,128)(2,1)S(1)}, bf16[144,576]{1,0:T(8,128)(2,1)...) custom-call(s32[8]{0:T(128)S(1)} %stack.420.r_0_, ...), custom_call_target="tpu_custom_call" | custom-call | flops 2115502080 | bytes 7320064 | tf_op jit(solution)/shard_map/section1/pallas_call | solution.py:35
  53.9 14.5 %collective-permute-done.3.r_2_ = bf16[480,768]{1,0:T(8,128)(2,1)S(1)} collective-permute-done((bf16[480,768]{1,0:T(8,128)(2,1)S(1)}, bf16[480,768]{1,0:T(8,128)(2,1)S(1)}, u32[]{:S(2)}, u32[]{:S(2)}) %collective-permute-start.3) | collective-permute-done | bytes 737312 | tf_op jit(solution)/shard_map/ppermute | solution.py:542
  111.0 16.7 %collective-permute-done.6.r_2_ = bf16[480,768]{1,0:T(8,128)(2,1)S(1)} collective-permute-done((bf16[480,768]{1,0:T(8,128)(2,1)S(1)}, bf16[480,768]{1,0:T(8,128)(2,1)S(1)}, u32[]{:S(2)}, u32[]{:S(2)}) %collective-permute-start.6) | collective-permute-done | bytes 737312 | tf_op jit(solution)/shard_map/ppermute | solution.py:542
  148.0 16.7 %collective-permute-done.9.r_2_ = bf16[480,768]{1,0:T(8,128)(2,1)S(1)} collective-permute-done((bf16[480,768]{1,0:T(8,128)(2,1)S(1)}, bf16[480,768]{1,0:T(8,128)(2,1)S(1)}, u32[]{:S(2)}, u32[]{:S(2)}) %collective-permute-start.9) | collective-permute-done | bytes 737312 | tf_op jit(solution)/shard_map/ppermute | solution.py:542
  177.0 8.8 %section1.3 = (bf16[480,768]{1,0:T(8,128)(2,1)S(1)}, bf16[480,768]{1,0:T(8,128)(2,1)S(1)}, bf16[144,768]{1,0:T(8,128)(2,1)S(1)}, bf16[144,576]{1,0:T(8,128)(2,1)...) custom-call(s32[8]{0:T(128)S(1)} %copy-done.135, ...), custom_call_target="tpu_custom_call" | custom-call | flops 2115502080 | bytes 7320064 | tf_op jit(solution)/shard_map/section1/pallas_call | solution.py:35
  192.0 17.0 %collective-permute-done.12.r_2_ = bf16[480,768]{1,0:T(8,128)(2,1)S(1)} collective-permute-done((bf16[480,768]{1,0:T(8,128)(2,1)S(1)}, bf16[480,768]{1,0:T(8,128)(2,1)S(1)}, u32[]{:S(2)}, u32[]{:S(2)}) %collective-permute-start.12) | collective-permute-done | bytes 737312 | tf_op jit(solution)/shard_map/ppermute | solution.py:542
  226.0 16.8 %collective-permute-done.15.r_2_ = bf16[480,768]{1,0:T(8,128)(2,1)S(1)} collective-permute-done((bf16[480,768]{1,0:T(8,128)(2,1)S(1)}, bf16[480,768]{1,0:T(8,128)(2,1)S(1)}, u32[]{:S(2)}, u32[]{:S(2)}) %collective-permute-start.15) | collective-permute-done | bytes 737312 | tf_op jit(solution)/shard_map/ppermute | solution.py:542
  248.4 9.3 %concatenate.32.r_0_.r_3_ = bf16[480,768]{1,0:T(8,128)(2,1)} concatenate(bf16[36,768]{1,0:T(8,128)(2,1)} %slice.1158, bf16[36,768]{1,0:T(8,128)(2,1)} %slice.1159, bf16[8,768]{1,0:T(8,128)(2,1)} %copy-done.209, bf16[200,768]{1,0:T(8,128)(2,1)} %slice.1160, bf16[200,768]{1,0:T(8,128)(2,1)} %slice.1161), dimensions={0} | concatenate | bytes 1474560 | tf_op jit(solution)/shard_map/concatenate | solution.py:532
  271.6 7.5 %section3_weights.3 = (bf16[8,96,3072]{2,1,0:T(8,128)(2,1)}, f32[2,768]{1,0:T(2,128)S(1)}) custom-call(s32[8]{0:T(128)S(1)} %copy-done.137, bf16[480,768]{1,0:T(8,128)(2,1)} %get-tuple-element.137.r_0_.r_1_, bf16[480,768]{1,0:T(8,128)(2,1)} %collective-permute-done.16.r_1_.r_2_, bf16[480,768]{1,0:T(8,128)(2,1)S(1)} %copy-done.25, ...), custom_call_target="tpu_custom_call" | custom-call | flops 2264924160 | bytes 10622976 | tf_op jit(solution)/shard_map/section3_weights/pallas_call | solution.py:35
  287.6 16.2 %collective-permute-done.22.r_2_ = bf16[480,768]{1,0:T(8,128)(2,1)S(1)} collective-permute-done((bf16[480,768]{1,0:T(8,128)(2,1)S(1)}, bf16[480,768]{1,0:T(8,128)(2,1)S(1)}, u32[]{:S(2)}, u32[]{:S(2)}) %collective-permute-start.22) | collective-permute-done | bytes 737312 | tf_op jit(solution)/shard_map/ppermute | solution.py:542
  309.7 8.8 %collective-permute-done.18 = bf16[480,768]{1,0:T(8,128)(2,1)} collective-permute-done((bf16[480,768]{1,0:T(8,128)(2,1)}, bf16[480,768]{1,0:T(8,128)(2,1)}, u32[]{:S(2)}, u32[]{:S(2)}) %collective-permute-start.18) | collective-permute-done | bytes 737312 | tf_op jit(solution)/shard_map/ppermute | solution.py:542
  320.6 8.6 %section2_back.2 = (bf16[480,768]{1,0:T(8,128)(2,1)S(1)}, bf16[480,768]{1,0:T(8,128)(2,1)S(1)}, bf16[800,192]{1,0:T(8,128)(2,1)S(1)}, bf16[160,384]{1,0:T(8,128)...) custom-call(s32[8]{0:T(128)S(1)} %copy-done.137, ...), custom_call_target="tpu_custom_call" | custom-call | flops 1132462080 | bytes 7919616 | tf_op jit(solution)/shard_map/section2_back/pallas_call | solution.py:35
  341.0 20.8 %collective-permute-done.54 = bf16[4,96,1536]{2,1,0:T(8,128)(2,1)S(1)} collective-permute-done((bf16[4,96,1536]{2,1,0:T(8,128)(2,1)S(1)}, bf16[4,96,1536]{2,1,0:T(8,128)(2,1)S(1)}, u32[]{:S(2)}, u32[]{:S(2)}) %collective-permute-start.54) | collective-permute-done | bytes 1179680 | tf_op jit(solution)/shard_map/ppermute | solution.py:659
  374.1 12.2 %collective-permute-done.64 = bf16[96,3072]{1,0:T(8,128)(2,1)S(1)} collective-permute-done((bf16[96,3072]{1,0:T(8,128)(2,1)S(1)}, bf16[96,3072]{1,0:T(8,128)(2,1)S(1)}, u32[]{:S(2)}, u32[]{:S(2)}) %collective-permute-start.64) | collective-permute-done | bytes 589856 | tf_op jit(solution)/shard_map/ppermute | solution.py:664
  392.9 11.2 %section1_back.2 = (bf16[480,768]{1,0:T(8,128)(2,1)S(1)}, bf16[480,768]{1,0:T(8,128)(2,1)S(1)}, bf16[144,576]{1,0:T(8,128)(2,1)S(1)}, bf16[800,576]{1,0:T(8,128)...) custom-call(s32[8]{0:T(128)S(1)} %copy-done.137, ...), custom_call_target="tpu_custom_call" | custom-call | flops 3590062080 | bytes 8249344 | tf_op jit(solution)/shard_map/section1_back/pallas_call | solution.py:35
  419.7 12.6 %collective-permute-done.28.r_2_ = bf16[480,768]{1,0:T(8,128)(2,1)S(1)} collective-permute-done((bf16[480,768]{1,0:T(8,128)(2,1)S(1)}, bf16[480,768]{1,0:T(8,128)(2,1)S(1)}, u32[]{:S(2)}, u32[]{:S(2)}) %collective-permute-start.28) | collective-permute-done | bytes 737312 | tf_op jit(solution)/shard_map/ppermute | solution.py:542
  485.3 10.2 %collective-permute-done.31.r_2_ = bf16[480,768]{1,0:T(8,128)(2,1)} collective-permute-done((bf16[480,768]{1,0:T(8,128)(2,1)}, bf16[480,768]{1,0:T(8,128)(2,1)}, u32[]{:S(2)}, u32[]{:S(2)}) %collective-permute-start.31) | collective-permute-done | bytes 737312 | tf_op jit(solution)/shard_map/ppermute | solution.py:542
  516.6 8.5 %section2_back.3 = (bf16[480,768]{1,0:T(8,128)(2,1)S(1)}, bf16[480,768]{1,0:T(8,128)(2,1)S(1)}, bf16[800,192]{1,0:T(8,128)(2,1)S(1)}, bf16[160,384]{1,0:T(8,128)...) custom-call(s32[8]{0:T(128)S(1)} %copy-done.141, ...), custom_call_target="tpu_custom_call" | custom-call | flops 1132462080 | bytes 7919616 | tf_op jit(solution)/shard_map/section2_back/pallas_call | solution.py:35
  535.5 22.6 %collective-permute-done.46 = bf16[4,96,1536]{2,1,0:T(8,128)(2,1)S(1)} collective-permute-done((bf16[4,96,1536]{2,1,0:T(8,128)(2,1)S(1)}, bf16[4,96,1536]{2,1,0:T(8,128)(2,1)S(1)}, u32[]{:S(2)}, u32[]{:S(2)}) %collective-permute-start.46) | collective-permute-done | bytes 1179680 | tf_op jit(solution)/shard_map/ppermute | solution.py:659
  570.3 12.2 %collective-permute-done.60 = bf16[96,3072]{1,0:T(8,128)(2,1)S(1)} collective-permute-done((bf16[96,3072]{1,0:T(8,128)(2,1)S(1)}, bf16[96,3072]{1,0:T(8,128)(2,1)S(1)}, u32[]{:S(2)}, u32[]{:S(2)}) %collective-permute-start.60) | collective-permute-done | bytes 589856 | tf_op jit(solution)/shard_map/ppermute | solution.py:664
  593.3 9.7 %collective-permute-done.61 = bf16[96,3072]{1,0:T(8,128)(2,1)} collective-permute-done((bf16[96,3072]{1,0:T(8,128)(2,1)}, bf16[96,3072]{1,0:T(8,128)(2,1)}, u32[]{:S(2)}, u32[]{:S(2)}) %collective-permute-start.61) | collective-permute-done | bytes 589856 | tf_op jit(solution)/shard_map/ppermute | solution.py:664
  609.7 12.1 %section1_back.3 = (bf16[480,768]{1,0:T(8,128)(2,1)S(1)}, bf16[480,768]{1,0:T(8,128)(2,1)}, bf16[144,576]{1,0:T(8,128)(2,1)S(1)}, bf16[800,576]{1,0:T(8,128)(2,1...) custom-call(s32[8]{0:T(128)S(1)} %copy-done.143, ...), custom_call_target="tpu_custom_call" | custom-call | flops 3590062080 | bytes 8249344 | tf_op jit(solution)/shard_map/section1_back/pallas_call | solution.py:35
  636.0 15.8 %collective-permute-done.42 = bf16[4,96,1536]{2,1,0:T(8,128)(2,1)} collective-permute-done((bf16[4,96,1536]{2,1,0:T(8,128)(2,1)}, bf16[4,96,1536]{2,1,0:T(8,128)(2,1)}, u32[]{:S(2)}, u32[]{:S(2)}) %collective-permute-start.42) | collective-permute-done | bytes 1179680 | tf_op jit(solution)/shard_map/ppermute | solution.py:659
  680.1 11.5 %collective-permute-done.41 = f32[27750]{0:T(1024)S(1)} collective-permute-done((f32[27750]{0:T(1024)S(1)}, f32[27750]{0:T(1024)S(1)}, u32[]{:S(2)}, u32[]{:S(2)}) %collective-permute-start.41) | collective-permute-done | bytes 111032 | tf_op jit(solution)/shard_map/ppermute | solution.py:777
  (853 shorter events, 387.2 us)
Async XLA Ops:
  73.1 22.6 %collective-permute-start.4 = (bf16[480,768]{1,0:T(8,128)(2,1)}, bf16[480,768]{1,0:T(8,128)(2,1)}, u32[]{:S(2)}, u32[]{:S(2)}) collective-permute-start(bf16[480,768]{1,0:T(8,128)(2,1)} %get-tuple-element.121.r_1_), channel_id=1, source_target_pairs={{0,1},{1,0},{2,3},{3,2},{4,5},{5,4},{6,7},{7,6},{8,9},{9,8},{10,11... | collective-permute-start | bytes 2211848 | tf_op jit(solution)/shard_map/ppermute | solution.py:553
  145.9 18.8 %collective-permute-start.9 = (bf16[480,768]{1,0:T(8,128)(2,1)S(1)}, bf16[480,768]{1,0:T(8,128)(2,1)S(1)}, u32[]{:S(2)}, u32[]{:S(2)}) collective-permute-start(bf16[480,768]{1,0:T(8,128)(2,1)S(1)} %add_convert_fusion.9.r_1_), channel_id=1, source_target_pairs={{0,2},{1,3},{2,0},{3,1},{4,6},{5,7},{6,4},{7,5},{8,10},{9,11},{10,... | collective-permute-start | bytes 2211848 | tf_op jit(solution)/shard_map/ppermute | solution.py:542
  282.4 53.6 %collective-permute-start.62 = (bf16[4,96,3072]{2,1,0:T(8,128)(2,1)}, bf16[4,96,3072]{2,1,0:T(8,128)(2,1)}, u32[]{:S(2)}, u32[]{:S(2)}) collective-permute-start(bf16[4,96,3072]{2,1,0:T(8,128)(2,1)} %slice.1078), channel_id=1, source_target_pairs={{0,4},{4,0},{8,12},{12,8},{16,20},{20,16},{24,28},{28,24},{1,5},{5... | collective-permute-start | bytes 7077896 | tf_op jit(solution)/shard_map/ppermute | solution.py:659
  284.4 19.4 %collective-permute-start.22 = (bf16[480,768]{1,0:T(8,128)(2,1)S(1)}, bf16[480,768]{1,0:T(8,128)(2,1)S(1)}, u32[]{:S(2)}, u32[]{:S(2)}) collective-permute-start(bf16[480,768]{1,0:T(8,128)(2,1)S(1)} %add_convert_fusion.5.r_1_), channel_id=1, source_target_pairs={{0,2},{1,3},{2,0},{3,1},{4,6},{5,7},{6,4},{7,5},{8,10},{9,11},{10,... | collective-permute-start | bytes 2211848 | tf_op jit(solution)/shard_map/ppermute | solution.py:542
  287.0 31.5 %collective-permute-start.18 = (bf16[480,768]{1,0:T(8,128)(2,1)}, bf16[480,768]{1,0:T(8,128)(2,1)}, u32[]{:S(2)}, u32[]{:S(2)}) collective-permute-start(bf16[480,768]{1,0:T(8,128)(2,1)} %add_convert_fusion.6), channel_id=1, source_target_pairs={{0,2},{1,3},{2,0},{3,1},{4,6},{5,7},{6,4},{7,5},{8,10},{9,11},{10,... | collective-permute-start | bytes 2211848 | tf_op jit(solution)/shard_map/ppermute | solution.py:542
  333.4 28.4 %collective-permute-start.54 = (bf16[4,96,1536]{2,1,0:T(8,128)(2,1)S(1)}, bf16[4,96,1536]{2,1,0:T(8,128)(2,1)S(1)}, u32[]{:S(2)}, u32[]{:S(2)}) collective-permute-start(bf16[4,96,1536]{2,1,0:T(8,128)(2,1)S(1)} %slice.1265), channel_id=1, source_target_pairs={{0,4},{4,0},{8,12},{12,8},{16,20},{20,16},{24,28},{28,24},{1,5},{5... | collective-permute-start | bytes 3538952 | tf_op jit(solution)/shard_map/ppermute | solution.py:659
  337.4 26.2 %collective-permute-start.63 = (bf16[96,3072]{1,0:T(8,128)(2,1)S(1)}, bf16[96,3072]{1,0:T(8,128)(2,1)S(1)}, u32[]{:S(2)}, u32[]{:S(2)}) collective-permute-start(bf16[96,3072]{1,0:T(8,128)(2,1)S(1)} %fusion.9), channel_id=1, source_target_pairs={{0,8},{4,12},{8,16},{12,20},{16,24},{20,28},{24,0},{28,4},{1,9},{5... | collective-permute-start | bytes 1769480 | tf_op jit(solution)/shard_map/ppermute | solution.py:664
  339.4 28.5 %collective-permute-start.25 = (bf16[480,768]{1,0:T(8,128)(2,1)S(1)}, bf16[480,768]{1,0:T(8,128)(2,1)S(1)}, u32[]{:S(2)}, u32[]{:S(2)}) collective-permute-start(bf16[480,768]{1,0:T(8,128)(2,1)S(1)} %add_convert_fusion.4.r_1_), channel_id=1, source_target_pairs={{0,2},{1,3},{2,0},{3,1},{4,6},{5,7},{6,4},{7,5},{8,10},{9,11},{10,... | collective-permute-start | bytes 2211848 | tf_op jit(solution)/shard_map/ppermute | solution.py:542
  365.0 21.3 %collective-permute-start.64 = (bf16[96,3072]{1,0:T(8,128)(2,1)S(1)}, bf16[96,3072]{1,0:T(8,128)(2,1)S(1)}, u32[]{:S(2)}, u32[]{:S(2)}) collective-permute-start(bf16[96,3072]{1,0:T(8,128)(2,1)S(1)} %fusion.1), channel_id=1, source_target_pairs={{0,8},{4,12},{8,16},{12,20},{16,24},{20,28},{24,0},{28,4},{1,9},{5... | collective-permute-start | bytes 1769480 | tf_op jit(solution)/shard_map/ppermute | solution.py:664
  369.1 23.7 %collective-permute-start.26 = (bf16[480,768]{1,0:T(8,128)(2,1)S(1)}, bf16[480,768]{1,0:T(8,128)(2,1)S(1)}, u32[]{:S(2)}, u32[]{:S(2)}) collective-permute-start(bf16[480,768]{1,0:T(8,128)(2,1)S(1)} %get-tuple-element.154.r_1_.r_3_), channel_id=1, source_target_pairs={{0,1},{1,0},{2,3},{3,2},{4,5},{5,4},{6,7},{7,6},{8,9},{9,8},{10,11... | collective-permute-start | bytes 2211848 | tf_op jit(solution)/shard_map/ppermute | solution.py:553
  392.7 25.9 %collective-permute-start.57 = (bf16[96,1536]{1,0:T(8,128)(2,1)S(1)}, bf16[96,1536]{1,0:T(8,128)(2,1)S(1)}, u32[]{:S(2)}, u32[]{:S(2)}) collective-permute-start(bf16[96,1536]{1,0:T(8,128)(2,1)S(1)} %fusion.10), channel_id=1, source_target_pairs={{0,8},{4,12},{8,16},{12,20},{16,24},{20,28},{24,0},{28,4},{1,9},{5... | collective-permute-start | bytes 884744 | tf_op jit(solution)/shard_map/ppermute | solution.py:664
  412.9 26.7 %collective-permute-start.50 = (bf16[4,96,1536]{2,1,0:T(8,128)(2,1)S(1)}, bf16[4,96,1536]{2,1,0:T(8,128)(2,1)S(1)}, u32[]{:S(2)}, u32[]{:S(2)}) collective-permute-start(bf16[4,96,1536]{2,1,0:T(8,128)(2,1)S(1)} %slice.1250), channel_id=1, source_target_pairs={{0,4},{4,0},{8,12},{12,8},{16,20},{20,16},{24,28},{28,24},{1,5},{5... | collective-permute-start | bytes 3538952 | tf_op jit(solution)/shard_map/ppermute | solution.py:659
  450.2 24.5 %collective-permute-start.30 = (bf16[480,768]{1,0:T(8,128)(2,1)}, bf16[480,768]{1,0:T(8,128)(2,1)}, u32[]{:S(2)}, u32[]{:S(2)}) collective-permute-start(bf16[480,768]{1,0:T(8,128)(2,1)} %get-tuple-element.165), channel_id=1, source_target_pairs={{0,1},{1,0},{2,3},{3,2},{4,5},{5,4},{6,7},{7,6},{8,9},{9,8},{10,11... | collective-permute-start | bytes 2211848 | tf_op jit(solution)/shard_map/ppermute | solution.py:540
  454.8 26.4 %collective-permute-start.52 = (bf16[96,1536]{1,0:T(8,128)(2,1)}, bf16[96,1536]{1,0:T(8,128)(2,1)}, u32[]{:S(2)}, u32[]{:S(2)}) collective-permute-start(bf16[96,1536]{1,0:T(8,128)(2,1)} %fusion.13), channel_id=1, source_target_pairs={{0,8},{4,12},{8,16},{12,20},{16,24},{20,28},{24,0},{28,4},{1,9},{5... | collective-permute-start | bytes 884744 | tf_op jit(solution)/shard_map/ppermute | solution.py:664
  473.6 57.3 %collective-permute-start.58 = (bf16[4,96,3072]{2,1,0:T(8,128)(2,1)}, bf16[4,96,3072]{2,1,0:T(8,128)(2,1)}, u32[]{:S(2)}, u32[]{:S(2)}) collective-permute-start(bf16[4,96,3072]{2,1,0:T(8,128)(2,1)} %slice.1067), channel_id=1, source_target_pairs={{0,4},{4,0},{8,12},{12,8},{16,20},{20,16},{24,28},{28,24},{1,5},{5... | collective-permute-start | bytes 7077896 | tf_op jit(solution)/shard_map/ppermute | solution.py:659
  483.1 28.1 %collective-permute-start.53 = (bf16[96,1536]{1,0:T(8,128)(2,1)}, bf16[96,1536]{1,0:T(8,128)(2,1)}, u32[]{:S(2)}, u32[]{:S(2)}) collective-permute-start(bf16[96,1536]{1,0:T(8,128)(2,1)} %fusion.12), channel_id=1, source_target_pairs={{0,8},{4,12},{8,16},{12,20},{16,24},{20,28},{24,0},{28,4},{1,9},{5... | collective-permute-start | bytes 884744 | tf_op jit(solution)/shard_map/ppermute | solution.py:664
  529.6 28.5 %collective-permute-start.46 = (bf16[4,96,1536]{2,1,0:T(8,128)(2,1)S(1)}, bf16[4,96,1536]{2,1,0:T(8,128)(2,1)S(1)}, u32[]{:S(2)}, u32[]{:S(2)}) collective-permute-start(bf16[4,96,1536]{2,1,0:T(8,128)(2,1)S(1)} %slice.1235), channel_id=1, source_target_pairs={{0,4},{4,0},{8,12},{12,8},{16,20},{20,16},{24,28},{28,24},{1,5},{5... | collective-permute-start | bytes 3538952 | tf_op jit(solution)/shard_map/ppermute | solution.py:659
  532.3 27.9 %collective-permute-start.59 = (bf16[96,3072]{1,0:T(8,128)(2,1)S(1)}, bf16[96,3072]{1,0:T(8,128)(2,1)S(1)}, u32[]{:S(2)}, u32[]{:S(2)}) collective-permute-start(bf16[96,3072]{1,0:T(8,128)(2,1)S(1)} %fusion.8), channel_id=1, source_target_pairs={{0,8},{4,12},{8,16},{12,20},{16,24},{20,28},{24,0},{28,4},{1,9},{5... | collective-permute-start | bytes 1769480 | tf_op jit(solution)/shard_map/ppermute | solution.py:664
  535.5 26.5 %collective-permute-start.33 = (bf16[480,768]{1,0:T(8,128)(2,1)S(1)}, bf16[480,768]{1,0:T(8,128)(2,1)S(1)}, u32[]{:S(2)}, u32[]{:S(2)}) collective-permute-start(bf16[480,768]{1,0:T(8,128)(2,1)S(1)} %get-tuple-element.175), channel_id=1, source_target_pairs={{0,1},{1,0},{2,3},{3,2},{4,5},{5,4},{6,7},{7,6},{8,9},{9,8},{10,11... | collective-permute-start | bytes 2211848 | tf_op jit(solution)/shard_map/ppermute | solution.py:540
  561.7 20.9 %collective-permute-start.60 = (bf16[96,3072]{1,0:T(8,128)(2,1)S(1)}, bf16[96,3072]{1,0:T(8,128)(2,1)S(1)}, u32[]{:S(2)}, u32[]{:S(2)}) collective-permute-start(bf16[96,3072]{1,0:T(8,128)(2,1)S(1)} %fusion.3), channel_id=1, source_target_pairs={{0,8},{4,12},{8,16},{12,20},{16,24},{20,28},{24,0},{28,4},{1,9},{5... | collective-permute-start | bytes 1769480 | tf_op jit(solution)/shard_map/ppermute | solution.py:664
  563.1 24.0 %collective-permute-start.34 = (bf16[480,768]{1,0:T(8,128)(2,1)}, bf16[480,768]{1,0:T(8,128)(2,1)}, u32[]{:S(2)}, u32[]{:S(2)}) collective-permute-start(bf16[480,768]{1,0:T(8,128)(2,1)} %add_convert_fusion.1.r_1_), channel_id=1, source_target_pairs={{0,2},{1,3},{2,0},{3,1},{4,6},{5,7},{6,4},{7,5},{8,10},{9,11},{10,... | collective-permute-start | bytes 2211848 | tf_op jit(solution)/shard_map/ppermute | solution.py:542
  570.1 21.1 %collective-permute-start.48 = (bf16[96,1536]{1,0:T(8,128)(2,1)S(1)}, bf16[96,1536]{1,0:T(8,128)(2,1)}, u32[]{:S(2)}, u32[]{:S(2)}) collective-permute-start(bf16[96,1536]{1,0:T(8,128)(2,1)S(1)} %fusion.15), channel_id=1, source_target_pairs={{0,8},{4,12},{8,16},{12,20},{16,24},{20,28},{24,0},{28,4},{1,9},{5... | collective-permute-start | bytes 884744 | tf_op jit(solution)/shard_map/ppermute | solution.py:664
  628.0 23.7 %collective-permute-start.42 = (bf16[4,96,1536]{2,1,0:T(8,128)(2,1)}, bf16[4,96,1536]{2,1,0:T(8,128)(2,1)}, u32[]{:S(2)}, u32[]{:S(2)}) collective-permute-start(bf16[4,96,1536]{2,1,0:T(8,128)(2,1)} %slice.1220), channel_id=1, source_target_pairs={{0,4},{4,0},{8,12},{12,8},{16,20},{20,16},{24,28},{28,24},{1,5},{5... | collective-permute-start | bytes 3538952 | tf_op jit(solution)/shard_map/ppermute | solution.py:659
  633.5 21.3 %collective-permute-start.37 = (bf16[480,768]{1,0:T(8,128)(2,1)S(1)}, bf16[480,768]{1,0:T(8,128)(2,1)S(1)}, u32[]{:S(2)}, u32[]{:S(2)}) collective-permute-start(bf16[480,768]{1,0:T(8,128)(2,1)S(1)} %add_convert_fusion.r_1_), channel_id=1, source_target_pairs={{0,2},{1,3},{2,0},{3,1},{4,6},{5,7},{6,4},{7,5},{8,10},{9,11},{10,... | collective-permute-start | bytes 2211848 | tf_op jit(solution)/shard_map/ppermute | solution.py:542
  (279 other events, 2262.0 us)

commit v2 on v1

--- a/solution.py
+++ b/solution.py
@@ -13,7 +13,7 @@
 OUT = -1e30
 F32 = jnp.float32
 BF16 = jnp.bfloat16
-VMEM_LIMIT = 44 * 2**20
+VMEM_LIMIT = 20 * 2**20
 
 
 def nn(a, b):
@@ -28,19 +28,71 @@
     return lax.dot_general(a, b, (((0,), (0,)), ((), ())), preferred_element_type=F32)
 
 
-def call(body, outs, scalars, args, flops=0, name=None):
+class Part:
+    def __init__(self, array, *lead):
+        self.array, self.lead = array, lead
+        self.rest = array.shape[len(lead) :]
+        self.dtype = array.dtype
+        self.size = 1
+        for n in self.rest:
+            self.size *= n
+
+
+class Arriving:
+    def __init__(self, ref, copy):
+        self.ref, self.copy, self.shape = ref, copy, ref.shape
+
+    def __getitem__(self, at):
+        if self.copy is not None:
+            self.copy.wait()
+            self.copy = None
+        return self.ref[at]
+
+
+def call(body, outs, scalars, args, flops=0, name=None, scratch=()):
     vmem = pl.BlockSpec(memory_space=pltpu.VMEM)
     smem = pl.BlockSpec(memory_space=pltpu.SMEM)
+    anywhere = pl.BlockSpec(memory_space=pltpu.HBM)
     moved = sum(a.size * a.dtype.itemsize for a in list(args) + list(outs))
+    parts = [i for i, a in enumerate(args) if isinstance(a, Part)]
+    specs = [anywhere if isinstance(a, Part) else vmem for a in args]
+    arrays = [a.array if isinstance(a, Part) else a for a in args]
+    landing = [pltpu.VMEM(args[i].rest, args[i].dtype) for i in parts]
+    if parts:
+        landing.append(pltpu.SemaphoreType.DMA((len(parts),)))
+    first, end = len(scalars), len(scalars) + len(args) + len(outs) + len(scratch)
+
+    def wrapped(*refs):
+        refs = list(refs)
+        buffers = refs[end:]
+        coming = []
+        for k, i in enumerate(parts):
+            source = refs[first + i]
+            if args[i].lead:
+                source = source.at[args[i].lead]
+            copy = pltpu.make_async_copy(source, buffers[k], buffers[-1].at[k])
+            copy.start()
+            coming.append(Arriving(buffers[k], copy))
+            refs[first + i] = coming[-1]
+        body(*refs[:end])
+        for piece in coming:
+            if piece.copy is not None:
+                piece.copy.wait()
+
     return pl.pallas_call(
-        body,
+        wrapped,
         out_shape=tuple(outs),
-        in_specs=[smem] * len(scalars) + [vmem] * len(args),
+        in_specs=[smem] * len(scalars) + specs,
         out_specs=tuple(vmem for _ in outs),
+        scratch_shapes=list(scratch) + landing,
         compiler_params=pltpu.CompilerParams(vmem_limit_bytes=VMEM_LIMIT),
-        cost_estimate=pl.CostEstimate(flops=flops, bytes_accessed=moved, transcendentals=0),
+        cost_estimate=pl.CostEstimate(flops=1, bytes_accessed=1, transcendentals=0),
         name=name,
-    )(*scalars, *args)
+    )(*scalars, *arrays)
+
+
+def tie(*groups):
+    return lax.optimization_barrier(groups)
 
 
 def shaped(shape, dtype=BF16):
@@ -50,10 +102,12 @@
 class Sizes:
     def __init__(self, vis, qlen):
         self.vis, self.qlen = vis, qlen
-        self.vh, self.qh = vis // 2, qlen // 2
-        self.vp = -(-self.vh // 16) * 16
-        self.half = self.vp + self.qh
+        self.qh = qlen // 2
         self.vquart, self.qquart = vis // 4, qlen // 4
+        self.vpiece = -(-self.vquart // 8) * 8
+        self.vp = 2 * self.vpiece
+        self.piece = self.vpiece + self.qquart
+        self.half = 2 * self.piece
 
 
 def iota(shape, dim):
@@ -68,8 +122,9 @@
     second = (index >= sz.vp).astype(jnp.int32)
     row = index - second * sz.vp
     half = second + core - 2 * second * core
-    patch = row + jnp.where(row >= sz.vquart, sz.vquart, 0) + half * sz.vquart
-    return jnp.where(row < sz.vh, patch, -1)
+    late = (row >= sz.vpiece).astype(jnp.int32)
+    row = row - late * sz.vpiece
+    return jnp.where(row < sz.vquart, row + (2 * late + half) * sz.vquart, -1)
 
 
 def query_of(index, core, sz):
@@ -251,11 +306,11 @@
 GELU_A = 0.044715
 
 
-def section3(sz, nm, nth, wi, bi, wo, pm, pt, g, gp):
+def section3(sz, layer, nm, nth, wi, bi, wo, pm, pt, g, gp):
     vp, half = sz.vp, sz.half
     for ref, out, base in ((nm, pm, 0), (nth, pt, half)):
         for lo, hi, e in ((0, vp, 0), (vp, half, 1)):
-            h = nn(ref[lo:hi, :], wi[e]) + bi[e : e + 1, :]
+            h = nn(ref[lo:hi, :], wi[e]) + bi[layer, e : e + 1, :]
             h2 = h * h
             t = jnp.tanh(GELU_C * h * (1.0 + GELU_A * h2))
             half_t = 0.5 + 0.5 * t
@@ -353,61 +408,79 @@
     pt[vp:, :] = nn(dqkvq[qh:, :], w1[...]).astype(BF16)
 
 
-def store_blocks(sc, out, col, value):
+def kept_order(order):
+    return sorted(range(1 << len(order)), key=lambda r: [(r >> k) & 1 for k in order])
+
+
+def store_blocks(sc, store, col, value):
+    keep, send, scr, order = store
+    width = value.shape[1]
     value = value.astype(BF16)
-    blocks, rows = out.shape[0], out.shape[1]
-    width = value.shape[1]
-    ring = blocks // 2
-    for d in range(blocks):
-        if blocks == 1:
-            slot = 0
+    cols = slice(col, col + width)
+    if send is None:
+        keep[0, :, cols] = value
+        return
+    count, rows = keep.shape[0], keep.shape[1]
+    scr[:, 0:width] = value
+    for slot, relative in enumerate(kept_order(order)):
+        owner = relative ^ sc[5]
+        block = scr[pl.ds(pl.multiple_of(owner * rows, 16), rows), 0:width]
+        if slot < count:
+            keep[slot, :, cols] = block
         else:
-            flip = (d % 2) + sc[5] - 2 * (d % 2) * sc[5]
-            away = d // 2 - sc[6]
-            away = jnp.where(away < 0, away + ring, away)
-            slot = flip * ring + away
-        out[slot, :, col : col + width] = value[d * rows : (d + 1) * rows, :]
-
-
-def section3_weights(sz, sc, nm, nth, dm, dt, g, dh, out, db):
+            send[slot - count, :, cols] = block
+
+
+def section3_weights(sz, sc, nm, nth, dm, dt, g, dh, db, out):
     vp, half = sz.vp, sz.half
     hid = g.shape[1]
     for e, lo, hi in ((0, 0, vp), (1, vp, half)):
-        store_blocks(sc, out, e * hid, tn(nm[lo:hi, :], dh[lo:hi, :]) + tn(nth[lo:hi, :], dh[half + lo : half + hi, :]))
-        store_blocks(
-            sc, out, (2 + e) * hid, tn(dm[lo:hi, :], g[lo:hi, :]) + tn(dt[lo:hi, :], g[half + lo : half + hi, :])
-        )
+        into = tn(nm[lo:hi, :], dh[lo:hi, :]) + tn(nth[lo:hi, :], dh[half + lo : half + hi, :])
+        away = tn(dm[lo:hi, :], g[lo:hi, :]) + tn(dt[lo:hi, :], g[half + lo : half + hi, :])
+        out[:, e * hid : (e + 1) * hid] = into.astype(BF16)
+        out[:, (2 + e) * hid : (3 + e) * hid] = away.astype(BF16)
         db[e : e + 1, :] = jnp.sum(dh[lo:hi, :].astype(F32), 0, keepdims=True) + jnp.sum(
             dh[half + lo : half + hi, :].astype(F32), 0, keepdims=True
         )
 
 
-def section2_weights(sz, heads, sc, nm, nth, dm, dt, dqq, dkvv, dqv, dkvq, oq, ov, out):
+def section2_weights(sz, heads, sc, nm, nth, dm, dt, dqq, dkvv, dqv, dkvq, oq, ov, store):
     vp, qh = sz.vp, sz.qh
     e = heads * HDIM
 
     def both(a_m, a_t, b, cut, lo, hi):
         return tn(a_m[lo:hi, :], b[0:cut, :]) + tn(a_t[lo:hi, :], b[cut:, :])
 
-    store_blocks(sc, out, 0, both(nm, nth, dqq, qh, vp, sz.half))
-    store_blocks(sc, out, e, both(nm, nth, dkvv, vp, 0, vp))
-    store_blocks(sc, out, 3 * e, both(nm, nth, dqv, vp, 0, vp))
-    store_blocks(sc, out, 4 * e, both(nm, nth, dkvq, qh, vp, sz.half))
-    store_blocks(sc, out, 6 * e, both(dm, dt, oq, qh, vp, sz.half))
-    store_blocks(sc, out, 7 * e, both(dm, dt, ov, vp, 0, vp))
-
-
-def section1_weights(sz, heads, sc, nm, nth, dm, dt, nvw, dqkvv, dqkvq, oq, ov, out):
+    store_blocks(sc, store, 0, both(nm, nth, dqq, qh, vp, sz.half))
+    store_blocks(sc, store, e, both(nm, nth, dkvv, vp, 0, vp))
+    store_blocks(sc, store, 3 * e, both(nm, nth, dqv, vp, 0, vp))
+    store_blocks(sc, store, 4 * e, both(nm, nth, dkvq, qh, vp, sz.half))
+    store_blocks(sc, store, 6 * e, both(dm, dt, oq, qh, vp, sz.half))
+    store_blocks(sc, store, 7 * e, both(dm, dt, ov, vp, 0, vp))
+
+
+def section1_weights(sz, heads, sc, nm, nth, dm, dt, nvw, dqkvv, dqkvq, oq, ov, store):
     vp, qh = sz.vp, sz.qh
     e = heads * HDIM
 
     def both(a_m, a_t, b, cut, lo, hi):
         return tn(a_m[lo:hi, :], b[0:cut, :]) + tn(a_t[lo:hi, :], b[cut:, :])
 
-    store_blocks(sc, out, 0, tn(nvw[...], dqkvv[...]))
-    store_blocks(sc, out, 3 * e, both(nm, nth, dqkvq, qh, vp, sz.half))
-    store_blocks(sc, out, 6 * e, both(dm, dt, ov, vp, 0, vp))
-    store_blocks(sc, out, 7 * e, both(dm, dt, oq, qh, vp, sz.half))
+    store_blocks(sc, store, 0, tn(nvw[...], dqkvv[...]))
+    store_blocks(sc, store, 3 * e, both(nm, nth, dqkvq, qh, vp, sz.half))
+    store_blocks(sc, store, 6 * e, both(dm, dt, ov, vp, 0, vp))
+    store_blocks(sc, store, 7 * e, both(dm, dt, oq, qh, vp, sz.half))
+
+
+def in_order(sz, chip, own, other, out):
+    v, piece = sz.vpiece, sz.piece
+    mine, theirs = own[...].astype(F32), other[...].astype(F32)
+    first = jnp.where(chip == 0, mine, theirs)
+    second = jnp.where(chip == 0, theirs, mine)
+    out[0:v, :] = first[0:v]
+    out[v : 2 * v, :] = second[0:v]
+    out[2 * v : v + piece, :] = first[v:]
+    out[v + piece :, :] = second[v:]
 
 
 def norm_rows(x):
@@ -416,24 +489,36 @@
     return center * inv, inv
 
 
-def first_norm(sz, x, scale, shift, n):
+def open_stream(sz, sc, own, other, scale, shift, x, n):
+    layer = first = 0
+    in_order(sz, sc[6], own, other, x)
     for lo, hi, e in ((0, sz.vp, 0), (sz.vp, sz.half, 1)):
-        n[lo:hi, :] = (norm_rows(x[lo:hi, :])[0] * scale[e : e + 1, :] + shift[e : e + 1, :]).astype(BF16)
-
-
-def add_norm(sz, x, a, b, extra, scale, shift, y, n):
+        gain, bias = scale[first + e, layer : layer + 1, :], shift[first + e, layer : layer + 1, :]
+        n[lo:hi, :] = (norm_rows(x[lo:hi, :])[0] * gain + bias).astype(BF16)
+
+
+def open_grad(sz, sc, own, other, grad, dy, sums):
+    in_order(sz, sc[6], own, other, grad)
+    dy[...] = grad[...].astype(BF16)
     for lo, hi, e in ((0, sz.vp, 0), (sz.vp, sz.half, 1)):
-        value = x[lo:hi, :] + (a[lo:hi, :].astype(F32) + b[lo:hi, :].astype(F32)) + extra[e : e + 1, :]
+        sums[4 + e : 5 + e, :] = jnp.sum(grad[lo:hi, :], 0, keepdims=True)
+
+
+def add_norm(sz, layer, first, x, a, b, extra, scale, shift, y, n):
+    for lo, hi, e in ((0, sz.vp, 0), (sz.vp, sz.half, 1)):
+        gain, bias = scale[first + e, layer : layer + 1, :], shift[first + e, layer : layer + 1, :]
+        value = x[lo:hi, :] + (a[lo:hi, :].astype(F32) + b[lo:hi, :].astype(F32))
+        if extra is not None:
+            value = value + extra[layer - 1, e : e + 1, :]
         y[lo:hi, :] = value
-        n[lo:hi, :] = (norm_rows(value)[0] * scale[e : e + 1, :] + shift[e : e + 1, :]).astype(BF16)
-
-
-def norm_back(sz, d, a, b, x, scale, out, dy, sums):
+        n[lo:hi, :] = (norm_rows(value)[0] * gain + bias).astype(BF16)
+
+
+def norm_back(sz, layer, first, d, a, b, x, scale, out, dy, sums):
     for lo, hi, e in ((0, sz.vp, 0), (sz.vp, sz.half, 1)):
         dn = a[lo:hi, :].astype(F32) + b[lo:hi, :].astype(F32)
         unit, inv = norm_rows(x[lo:hi, :])
-        du = dn * scale[e : e + 1, :]
-        dnu = dn * unit
+        du = dn * scale[first + e, layer : layer + 1, :]
         dx = inv * (
             du
             - jnp.mean(du, -1, keepdims=True)
@@ -442,32 +527,118 @@
         value = d[lo:hi, :] + dx
         out[lo:hi, :] = value
         dy[lo:hi, :] = value.astype(BF16)
-        sums[e : e + 1, :] = jnp.sum(dnu, 0, keepdims=True)
+        sums[e : e + 1, :] = jnp.sum(dn * unit, 0, keepdims=True)
         sums[2 + e : 3 + e, :] = jnp.sum(dn, 0, keepdims=True)
         sums[4 + e : 5 + e, :] = jnp.sum(value, 0, keepdims=True)
 
 
-def table_bias(table):
-    heads = table.shape[0]
-    grid = table.reshape(heads, SPAN, SPAN)
-    cols = jnp.stack([grid[:, :, WIN - 1 - u : SPAN - u] for u in range(WIN)], 1)
-    cols = cols.reshape(heads, WIN, SPAN * WIN)
-    first = [(WIN - 1 - u) * WIN for u in range(WIN)]
-    rows = jnp.stack([cols[:, :, f : f + WIN * WIN] for f in first], 1)
-    return rows.reshape(heads, WIN * WIN, WIN * WIN)
-
-
-def table_grad(ds):
+TABLE = SPAN * SPAN
+TABLE_PAD = -(-TABLE // 128) * 128
+CELLS_PAD = -(-SPAN * WIN // 128) * 128
+
+
+def spread_matrix():
+    cell = iota((TABLE_PAD, CELLS_PAD), 1)
+    row = (cell * 171) >> 11
+    place = row * SPAN + cell - row * WIN
+    return ((iota((TABLE_PAD, CELLS_PAD), 0) == place) & (cell < SPAN * WIN)).astype(F32)
+
+
+def table_bias(tables, out, spread, rows):
+    spread[...] = spread_matrix()
+    count = out.shape[0]
+    for i in range(count):
+        table = tables[i : i + 1, :]
+        for b in range(WIN):
+            at = i * WIN + b
+            rows[at : at + 1, :] = pltpu.roll(table, (TABLE_PAD - (WIN - 1 - b)) % TABLE_PAD, 1)
+    cells = jnp.dot(rows[...], spread[...], precision=lax.Precision.HIGHEST, preferred_element_type=F32)
+    for a in range(WIN):
+        moved = pltpu.roll(cells, (CELLS_PAD - WIN * (WIN - 1 - a)) % CELLS_PAD, 1)
+        for i in range(count):
+            out[i, WIN * a : WIN * (a + 1), :] = moved[WIN * i : WIN * (i + 1), 0 : WIN * WIN]
+
+
+def table_grad(ds, spread, out):
     heads = ds.shape[0]
-    rows = ds.astype(F32).reshape(heads, WIN, WIN, WIN * WIN)
-    total = SPAN * WIN
-    cols = sum(
-        jnp.pad(rows[:, u], ((0, 0), (0, 0), ((WIN - 1 - u) * WIN, total - (WIN - 1 - u) * WIN - WIN * WIN)))
-        for u in range(WIN)
-    )
-    cols = cols.reshape(heads, WIN, SPAN, WIN)
-    grid = sum(jnp.pad(cols[:, u], ((0, 0), (0, 0), (WIN - 1 - u, u))) for u in range(WIN))
-    return grid.reshape(heads, SPAN * SPAN)
+    rows = jnp.zeros((WIN, CELLS_PAD - WIN * WIN), F32)
+    every = []
+    for h in range(heads):
+        grad = ds[h].astype(F32)
+        cells = jnp.zeros((WIN, CELLS_PAD), F32)
+        for a in range(WIN):
+            part = jnp.concatenate([grad[WIN * a : WIN * (a + 1), :], rows], 1)
+            cells = cells + pltpu.roll(part, WIN * (WIN - 1 - a), 1)
+        every.append(cells)
+    places = lax.dot_general(
+        jnp.concatenate(every, 0),
+        spread[...],
+        (((1,), (1,)), ((), ())),
+        precision=lax.Precision.HIGHEST,
+        preferred_element_type=F32,
+    )
+    for h in range(heads):
+        total = jnp.zeros((1, TABLE_PAD), F32)
+        for b in range(WIN):
+            total = total + pltpu.roll(places[h * WIN + b : h * WIN + b + 1, :], WIN - 1 - b, 1)
+        out[h : h + 1, :] = total
+
+
+def collect(layers, heads, *refs):
+    out = refs[-1]
+    out[...] = jnp.zeros(out.shape, F32)
+    row = 0
+    for layer in range(layers):
+        sums1, sums2, sums3, after = refs[6 * layer : 6 * layer + 4]
+        for ref, lo, count in ((sums1, 0, 4), (sums2, 0, 4), (sums3, 0, 4), (after, 4, 2)):
+            out[row : row + count, :] = ref[lo : lo + count, :]
+            row += count
+    for layer in range(layers):
+        db, table = refs[6 * layer + 4 : 6 * layer + 6]
+        out[row : row + 2, :] = db[...]
+        row += 2
+        out[row : row + heads, 0:TABLE_PAD] = table[0:heads, :]
+        row += heads
+
+
+def deal(layers, heads, rows, scale, shift, out_bias, in_bias, rel):
+    for layer in range(layers):
+        at = 14 * layer
+        for section in range(3):
+            for e in range(2):
+                scale[2 * section + e, layer : layer + 1, :] = rows[at + 4 * section + e : at + 4 * section + e + 1, :]
+                row = at + 4 * section + 2 + e
+                shift[2 * section + e, layer : layer + 1, :] = rows[row : row + 1, :]
+        out_bias[layer] = rows[at + 12 : at + 14, :]
+        at = 14 * layers + (2 + heads) * layer
+        in_bias[layer] = rows[at : at + 2, :]
+        for h in range(heads):
+            rel[h, layer : layer + 1, :] = rows[at + 2 + h : at + 3 + h, 0:TABLE]
+
+
+def finish_mlp(layers, *refs):
+    up, down = refs[layers:]
+    hid = up.shape[3]
+    for layer in range(layers):
+        total = refs[layer][...].astype(F32)
+        for e in range(2):
+            up[layer, e] = total[:, e * hid : (e + 1) * hid]
+            down[layer, e] = total[:, (2 + e) * hid : (3 + e) * hid]
+
+
+def finish_attn(layers, *refs):
+    d_in, d_out = refs[8 * layers :]
+    e = d_in.shape[4]
+    for layer in range(layers):
+        for pair in range(2):
+            first = 8 * layer + 4 * pair
+            total = sum(r[...].astype(F32) for r in refs[first : first + 4])
+            for which in range(2):
+                for c in range(3):
+                    col = (3 * which + c) * e
+                    d_in[layer, 2 * pair + which, c] = total[:, col : col + e]
+                col = (6 + which) * e
+                d_out[layer, 2 * pair + which] = total[:, col : col + e].T
 
 
 def on_device(
@@ -502,68 +673,117 @@
     swap = [(i, i ^ 1) for i in range(4)]
     cross = [(i, i ^ 2) for i in range(4)]
     block_rows = width // dp_size
-    ring_ok = dp_size % 2 == 0 and block_rows % 16 == 0
-    blocks = dp_size if ring_ok else 1
-    ring = dp_size // 2
+    halving = dp_size > 1 and dp_size & (dp_size - 1) == 0 and block_rows % 16 == 0
+    bits = dp_size.bit_length() - 1
 
     def scalars(layer):
         on = layer % 2
-        return jnp.stack(
-            [
-                core,
-                answer_start[0],
-                shifts[0, 0] * on,
-                shifts[0, 1] * on,
-                valid_windows[0, 0],
-                d_index % 2,
-                d_index // 2,
-                0,
-            ]
-        ).astype(jnp.int32)
+        values = [core, answer_start[0], shifts[0, 0] * on, shifts[0, 1] * on, valid_windows[0, 0], d_index, chip, 0]
+        return jnp.stack(values).astype(jnp.int32)
 
     w_in = attn_in.transpose(0, 1, 3, 4, 2).reshape(layers, 4, 3 * edev, width)
-
-    def to_half(own_v, own_q):
-        packed = jnp.concatenate([own_v, own_q], 0)
-        other = lax.ppermute(packed, "tensor", cross)
-        first = jnp.where(chip == 0, packed, other)
-        second = jnp.where(chip == 0, other, packed)
-        pad = jnp.zeros((vp - 2 * vq, width), packed.dtype)
-        return jnp.concatenate([first[:vq], second[:vq], pad, first[vq:], second[vq:]], 0)
-
-    def own_rows(rows):
-        v = jnp.where(chip == 0, rows[0:vq], rows[vq : 2 * vq])
-        q = jnp.where(chip == 0, rows[vp : vp + qq_], rows[vp + qq_ :])
-        return v, q
-
-    def total(mine, theirs):
+    scale, shift = norm_scale.transpose(1, 0, 2), norm_shift.transpose(1, 0, 2)
+
+    def packed(own_v, own_q):
+        pad = jnp.zeros((sz.vpiece - vq, width), own_v.dtype)
+        return jnp.concatenate([own_v, pad, own_q], 0)
+
+    def piece_of(rows, place):
+        v = jnp.where(place == 0, rows[0 : sz.vpiece], rows[sz.vpiece : vp])
+        q = jnp.where(place == 0, rows[vp : vp + qq_], rows[vp + qq_ :])
+        return jnp.concatenate([v, q], 0)
+
+    def pair_sum(mine, theirs):
         got = lax.ppermute(theirs, "tensor", swap)
-        kept = (mine.astype(F32) + got.astype(F32)).astype(BF16)
-        return kept, lax.ppermute(kept, "tensor", cross)
-
-    stream = to_half(visual[0], queries[0]).astype(F32)
-    grad_rounded = [lax.reduce_precision(g[0], 8, 7) for g in (grad_visual_out, grad_query_out)]
-    scal = [scalars(layer) for layer in range(layers)]
-    biases = [table_bias(rel_bias[layer]) for layer in range(layers)]
+        return (mine.astype(F32) + got.astype(F32)).astype(BF16)
+
+    def pair(x):
+        return x, lax.ppermute(x, "tensor", swap)
+
     rows_bf = shaped((half, width))
     rows_f = shaped((half, width), F32)
     mac = 2 * half * width
 
-    def pair(x):
-        return x, lax.ppermute(x, "tensor", swap)
-
-    zero_bias = jnp.zeros((2, width), F32)
-    (normed,) = call(
-        lambda *r: first_norm(sz, *r),
-        [rows_bf],
+    own = packed(visual[0], queries[0])
+    other = lax.ppermute(own, "tensor", cross)
+    tables = jnp.pad(rel_bias.reshape(layers * heads, TABLE), ((0, 0), (0, TABLE_PAD - TABLE)))
+    bias_all, spread = call(
+        table_bias,
+        [shaped((layers * heads, sz.vis, sz.vis), F32), shaped((TABLE_PAD, CELLS_PAD), F32)],
         [],
-        [stream, norm_scale[0, 0:2], norm_shift[0, 0:2]],
-        name="norm",
-    )
+        [tables],
+        name="table_bias",
+        scratch=[pltpu.VMEM((layers * heads * WIN, TABLE_PAD), F32)],
+    )
+    bias_all = bias_all.reshape(layers, heads, sz.vis, sz.vis)
+    scal = [scalars(layer) for layer in range(layers)]
+    own_grad = packed(grad_visual_out[0], grad_query_out[0])
+    rounded_grad = lax.reduce_precision(own_grad, 8, 7)
+
+    def next_norm(stream, a, b, layer, first, extra):
+        args = [stream, a, b] + ([mlp_out_bias] if extra else []) + [scale, shift]
+
+        def body(x, a, b, *rest):
+            if not extra:
+                rest = (None,) + rest
+            add_norm(sz, layer, first, x, a, b, *rest)
+
+        return call(body, [rows_f, rows_bf], [], args, name="norm")
+
+    def shares(kept):
+        return kept, lax.ppermute(kept, "tensor", cross)
+
+    fetched = {}
+
+    def fetch(layer, section, after):
+        if section == 3:
+            arrays = [mlp_in, mlp_out]
+            blocks = [(0, (layer,)), (1, (layer,))]
+        else:
+            arrays = [w_in, attn_out]
+            first = 2 * (section - 1)
+            blocks = [(0, (layer, first)), (0, (layer, first + 1)), (1, (layer, first)), (1, (layer, first + 1))]
+        arrays = tie(after, arrays)[1]
+        outs = [shaped(arrays[k].shape[len(lead) :]) for k, lead in blocks]
+
+        def body(one, two, *refs):
+            copies = [
+                pltpu.make_async_copy((one, two)[k].at[lead], refs[j], refs[-1].at[j])
+                for j, (k, lead) in enumerate(blocks)
+            ]
+            for copy in copies:
+                copy.start()
+            for copy in copies:
+                copy.wait()
+
+        fetched[layer, section] = pl.pallas_call(
+            body,
+            out_shape=outs,
+            in_specs=[pl.BlockSpec(memory_space=pltpu.HBM)] * 2,
+            out_specs=[pl.BlockSpec(memory_space=pltpu.VMEM)] * len(outs),
+            scratch_shapes=[pltpu.SemaphoreType.DMA((len(outs),))],
+            compiler_params=pltpu.CompilerParams(vmem_limit_bytes=VMEM_LIMIT),
+            name="fetch",
+        )(*arrays)
+
+    def fetch_beside(layer, section, a, b):
+        fetch(layer, section, a)
+        b, fetched[layer, section] = tie(b, fetched[layer, section])
+        return b
+
+    fetch(0, 1, own)
+    other, fetched[0, 1] = tie(other, fetched[0, 1])
+    stream, normed = call(
+        lambda *r: open_stream(sz, *r), [rows_f, rows_bf], scal[0:1], [own, other, scale, shift], name="open_stream"
+    )
+
     saved = []
     for layer in range(layers):
         sc = scal[layer]
         nm, nth = pair(normed)
+        if layer == 0:
+            sent_grad, nth = tie(rounded_grad.astype(BF16), nth)
+            other_grad = lax.ppermute(sent_grad, "tensor", cross)
         part = call(
             lambda *r: section1(sz, heads, *r),
             [
@@ -576,22 +796,32 @@
                 shaped((sz.qlen, 3 * edev)),
                 shaped((sz.qlen, edev)),
                 shaped((8, sz.qlen), F32),
-                shaped((sz.vis, edev)),
             ],
             [sc],
-            [nm, nth, w_in[layer, 0], w_in[layer, 1], attn_out[layer, 0], attn_out[layer, 1], biases[layer]],
+            [
+                nm, nth, *fetched[layer, 1], Part(bias_all, layer),
+            ],
             flops=mac * 4 * edev * 2 + 8 * heads * HDIM * sz.qlen * sz.qlen,
             name="section1",
+            scratch=[pltpu.VMEM((sz.vis, edev), BF16)],
         )
         kept1 = (stream, nm, nth) + tuple(part[2:9])
-        a, b = total(part[0], part[1])
-        stream, normed = call(
-            lambda *r: add_norm(sz, *r),
-            [rows_f, rows_bf],
-            [],
-            [stream, a, b, zero_bias, norm_scale[layer, 2:4], norm_shift[layer, 2:4]],
-            name="norm",
-        )
+        kept = pair_sum(part[0], part[1])
+        if layer == 0:
+            kept, other_grad = tie(kept, other_grad)
+        a, b = shares(kept)
+        if layer == 0:
+            other_grad, sent_grad, a2 = tie(other_grad, sent_grad, a)
+            grad, dy, grad_sums = call(
+                lambda *r: open_grad(sz, *r),
+                [rows_f, rows_bf, shaped((8, width), F32)],
+                scal[0:1],
+                [sent_grad, other_grad],
+                name="open_grad",
+            )
+            b, grad, dy = tie(b, grad, dy)
+        b = fetch_beside(layer, 2, a, b)
+        stream, normed = next_norm(stream, a, b, layer, 2, False)
         nm, nth = pair(normed)
         part = call(
             lambda *r: section2(sz, heads, *r),
@@ -608,95 +838,161 @@
                 shaped((8, 2 * vp), F32),
             ],
             [sc],
-            [nm, nth, w_in[layer, 2], w_in[layer, 3], attn_out[layer, 2], attn_out[layer, 3]],
+            [nm, nth, *fetched[layer, 2]],
             flops=mac * 4 * edev * 2,
             name="section2",
         )
         kept2 = (stream, nm, nth) + tuple(part[2:])
-        a, b = total(part[0], part[1])
-        stream, normed = call(
-            lambda *r: add_norm(sz, *r),
-            [rows_f, rows_bf],
-            [],
-            [stream, a, b, zero_bias, norm_scale[layer, 4:6], norm_shift[layer, 4:6]],
-            name="norm",
-        )
+        a, b = shares(pair_sum(part[0], part[1]))
+        b = fetch_beside(layer, 3, a, b)
+        stream, normed = next_norm(stream, a, b, layer, 4, False)
         nm, nth = pair(normed)
         part = call(
-            lambda *r: section3(sz, *r),
+            lambda *r: section3(sz, layer, *r),
             [rows_bf, rows_bf, shaped((2 * half, hid)), shaped((2 * half, hid))],
             [],
-            [nm, nth, mlp_in[layer], mlp_in_bias[layer], mlp_out[layer]],
+            [nm, nth, fetched[layer, 3][0], mlp_in_bias, fetched[layer, 3][1]],
             flops=mac * hid * 4,
             name="section3",
         )
         kept3 = (stream, nm, nth) + tuple(part[2:])
         saved.append((kept1, kept2, kept3))
-        a, b = total(part[0], part[1])
         if layer + 1 < layers:
-            stream, normed = call(
-                lambda *r: add_norm(sz, *r),
-                [rows_f, rows_bf],
-                [],
-                [stream, a, b, mlp_out_bias[layer], norm_scale[layer + 1, 0:2], norm_shift[layer + 1, 0:2]],
-                name="norm",
-            )
-        else:
-            added = stream + (a.astype(F32) + b.astype(F32))
-            out_v, out_q = own_rows(added)
-            out_v = (out_v + mlp_out_bias[layer, 0]).astype(BF16)
-            out_q = (out_q + mlp_out_bias[layer, 1]).astype(BF16)
-
-    dy = to_half(*(g.astype(BF16) for g in grad_rounded))
-    grad = dy.astype(F32)
-    bias_sums = jnp.stack([jnp.sum(grad[:vp], 0), jnp.sum(grad[vp:], 0)])
-
-    def reduce_weights(parts):
-        if not ring_ok:
-            return lax.psum_scatter(parts[0].astype(F32), "dp", scatter_dimension=0, tiled=True)
-        flip = [(i, i ^ 1) for i in range(dp_size)]
-        onward = [(i, (i + 2) % dp_size) for i in range(dp_size)]
-        got = lax.ppermute(parts[ring:], "dp", flip)
-        if ring == 1:
-            return parts[0].astype(F32) + got[0].astype(F32)
-        moving = parts[ring - 1].astype(F32) + got[ring - 1].astype(F32)
-        for away in reversed(range(ring - 1)):
-            moving = lax.ppermute(moving.astype(BF16), "dp", onward).astype(F32)
-            moving = moving + (parts[away].astype(F32) + got[away].astype(F32))
-        return moving
+            a, b = shares(pair_sum(part[0], part[1]))
+            b = fetch_beside(layer + 1, 1, a, b)
+            stream, normed = next_norm(stream, a, b, layer + 1, 0, True)
+    last = pair_sum(part[0], part[1])
+    away = lax.ppermute(piece_of(last, 1 - chip), "tensor", cross)
+    out = piece_of(stream, chip) + (piece_of(last, chip).astype(F32) + away.astype(F32))
+    out_v = (out[0:vq] + mlp_out_bias[layers - 1, 0]).astype(BF16)
+    out_q = (out[sz.vpiece :] + mlp_out_bias[layers - 1, 1]).astype(BF16)
+
+    bias_sums = grad_sums
+
+    def whole_sum(rows):
+        return lax.psum_scatter(rows, "dp", scatter_dimension=0, tiled=True)
+
+    class Reduction:
+        def __init__(self, outs, order):
+            self.order = order
+            if halving:
+                self.parts, self.step = [outs[0]], 0
+                self.ready = outs[1]
+                self.move()
+            else:
+                self.sum = whole_sum(outs[0][0])
+                self.step = bits
+
+        def move(self):
+            bit = 1 << self.order[self.step]
+            got = lax.ppermute(self.ready, "dp", [(i, i ^ bit) for i in range(dp_size)])
+            self.parts.append(got)
+            self.step += 1
+
+        def advance(self):
+            count = 1 << (bits - 1 - self.step)
+            self.ready = sum(p[count : 2 * count].astype(F32) for p in self.parts).astype(BF16)
+            self.move()
+
+        def pieces(self):
+            if not halving:
+                zero = jnp.zeros_like(self.sum)
+                return [self.sum, zero, zero, zero]
+            lead = [Part(p, 0) for p in self.parts]
+            while len(lead) < 4:
+                lead.append(jnp.zeros(lead[0].rest, BF16))
+            return lead
 
     def close(grad, a, b, kept, layer, first):
         return call(
-            lambda *r: norm_back(sz, *r),
+            lambda *r: norm_back(sz, layer, first, *r),
             [rows_f, rows_bf, shaped((8, width), F32)],
             [],
-            [grad, a, b, kept[0], norm_scale[layer, first : first + 2]],
+            [grad, a, b, kept[0], scale],
             name="norm_back",
         )
 
+    straight = tuple(range(bits))
+    turned = straight[1:] + straight[:1]
+
+    def weights(body, extra_outs, orders, columns, args, wide, name):
+        outs = []
+        for _ in orders:
+            if halving:
+                outs += [shaped((dp_size // 2, block_rows, columns))] * 2
+            else:
+                outs += [shaped((1, width, columns))]
+        lead = 1 + len(args) + len(extra_outs)
+        each = 2 if halving else 1
+
+        def wrapped(*refs):
+            stores = []
+            for k, order in enumerate(orders):
+                given = refs[lead + k * each : lead + (k + 1) * each]
+                stores.append((given[0], given[1] if halving else None, refs[-1], order))
+            body(*refs[:lead], *stores)
+
+        got = call(
+            wrapped,
+            list(extra_outs) + outs,
+            [scal[0]],
+            args,
+            name=name,
+            scratch=[pltpu.VMEM((width, wide), BF16)],
+        )
+        extra, rest = got[: len(extra_outs)], got[len(extra_outs) :]
+        return extra, [Reduction(rest[k * each : (k + 1) * each], order) for k, order in enumerate(orders)]
+
+    reductions = []
+    feeds = []
+    arrivals = {}
+    if halving and bits == 3 and layers == 2:
+        arrivals = {2: [0], 3: [0, 1], 4: [1], 5: [2]}
+
+    def window(kept, args):
+        return tie(kept, list(args))[1]
+
+    def seal(index, got, extra, made):
+        due = [reductions[g] for g in arrivals.get(index, ()) if reductions[g].step < bits]
+        firsts = [r.parts[0] for r in made] if halving else []
+        extra, firsts, parts = tie(list(extra), firsts, [r.parts for r in due])
+        for r, p in zip(due, parts):
+            r.parts = list(p)
+            r.advance()
+        got, extra, firsts = tie(got, extra, firsts)
+        for r, part in zip(made, firsts):
+            r.parts[0] = part
+        reductions.extend(made)
+        return got, extra
+
     grads = [None] * layers
+    index = 0
     for layer in reversed(range(layers)):
         sc = scal[layer]
         kept1, kept2, kept3 = saved[layer]
         dm, dt = pair(dy)
         _, nm, nth, act, slope = kept3
+        up, down = fetched[layer, 3]
         pm, pt, dh = call(
             lambda *r: section3_back(sz, *r),
             [rows_bf, rows_bf, shaped((2 * half, hid))],
             [],
-            [dm, dt, mlp_in[layer], mlp_out[layer], slope],
+            [dm, dt, up, down, slope],
             flops=mac * hid * 4,
             name="section3_back",
         )
-        a, b = total(pm, pt)
-        w3, db = call(
+        a, b = shares(pair_sum(pm, pt))
+        args = window(a, [nm, nth, dm, dt, act, dh])
+        db, feed = call(
             lambda *r: section3_weights(sz, *r),
-            [shaped((blocks, width // blocks, 4 * hid)), shaped((2, hid), F32)],
+            [shaped((2, hid), F32), shaped((width, 4 * hid))],
             [sc],
-            [nm, nth, dm, dt, act, dh],
-            flops=mac * hid * 4,
+            args,
             name="section3_weights",
         )
+        feeds.append(whole_sum(feed))
+        b, (db,) = seal(index, b, [db], [])
+        index += 1
         out_bias_sums = bias_sums
         grad, dy, sums3 = close(grad, a, b, kept3, layer, 4)
 
@@ -711,23 +1007,23 @@
                 shaped((2 * vp, 2 * edev)),
                 shaped((2 * vp, edev)),
                 shaped((sz.qlen, 2 * edev)),
-                shaped((sz.qlen, edev)),
-                shaped((2 * vp, edev)),
             ],
             [sc],
-            [dm, dt, w_in[layer, 2], w_in[layer, 3], attn_out[layer, 2], attn_out[layer, 3], qq, kvv, stq, qv, kvq, stv],
+            [
+                dm, dt, *fetched[layer, 2],
+                qq, kvv, stq, qv, kvq, stv,
+            ],
             flops=mac * 4 * edev * 2,
             name="section2_back",
-        )
-        a, b = total(part[0], part[1])
-        (w2,) = call(
-            lambda *r: section2_weights(sz, heads, *r),
-            [shaped((blocks, width // blocks, 8 * edev))],
-            [sc],
-            [nm, nth, dm, dt, part[2], part[3], part[4], part[5], oq, ov],
-            flops=mac * 4 * edev * 2,
-            name="section2_weights",
-        )
+            scratch=[pltpu.VMEM((sz.qlen, edev), BF16), pltpu.VMEM((2 * vp, edev), BF16)],
+        )
+        a, b = shares(pair_sum(part[0], part[1]))
+        args = window(a, [nm, nth, dm, dt, part[2], part[3], part[4], part[5], oq, ov])
+        _, made = weights(
+            lambda *r: section2_weights(sz, heads, *r), [], [straight], 8 * edev, args, 2 * edev, "section2_weights"
+        )
+        b, _ = seal(index, b, [], made)
+        index += 1
         grad, dy, sums2 = close(grad, a, b, kept2, layer, 2)
 
         dm, dt = pair(dy)
@@ -740,87 +1036,90 @@
                 shaped((sz.vis, 3 * edev)),
                 shaped((sz.qlen, 3 * edev)),
                 shaped((heads, sz.vis, sz.vis)),
-                shaped((sz.qlen, edev)),
-                shaped((sz.vis, edev)),
             ],
             [sc],
             [
-                dm, dt, w_in[layer, 0], w_in[layer, 1], attn_out[layer, 0], attn_out[layer, 1],
-                biases[layer], qkvv, stv, qkvq, stq,
+                dm, dt, *fetched[layer, 1],
+                Part(bias_all, layer), qkvv, stv, qkvq, stq,
             ],
             flops=mac * 4 * edev * 2 + 20 * heads * HDIM * sz.qlen * sz.qlen,
             name="section1_back",
-        )
-        a, b = total(part[0], part[1])
-        (w1,) = call(
-            lambda *r: section1_weights(sz, heads, *r),
-            [shaped((blocks, width // blocks, 8 * edev))],
-            [sc],
-            [nm, nth, dm, dt, nvw, part[2], part[3], oq, ov],
-            flops=mac * 4 * edev * 2,
-            name="section1_weights",
-        )
-        table = table_grad(part[4])
+            scratch=[pltpu.VMEM((sz.qlen, edev), BF16), pltpu.VMEM((sz.vis, edev), BF16)],
+        )
+        a, b = shares(pair_sum(part[0], part[1]))
+        args = window(a, [nm, nth, dm, dt, nvw, part[2], part[3], oq, ov])
+        _, made = weights(
+            lambda *r: section1_weights(sz, heads, *r), [], [straight], 8 * edev, args, 3 * edev, "section1_weights"
+        )
+        b, _ = seal(index, b, [], made)
+        (table,) = call(table_grad, [shaped((8, TABLE_PAD), F32)], [], [part[4], spread], name="table_grad")
+        index += 1
         grad, dy, sums1 = close(grad, a, b, kept1, layer, 0)
-        bias_sums = sums1[4:6]
-
-        w3, w2, w1 = reduce_weights(w3), reduce_weights(w2), reduce_weights(w1)
-        grads[layer] = (w3, w2, w1, db, table, sums1, sums2, sums3, out_bias_sums)
-
-    rest_v = grad_visual_out[0] - grad_rounded[0]
-    rest_q = grad_query_out[0] - grad_rounded[1]
-    own_v, own_q = own_rows(grad)
-    grad_v, grad_q = own_v + rest_v, own_q + rest_q
-
-    def summed(x, axis, size, bits):
-        for bit in bits:
+        bias_sums = sums1
+        grads[layer] = (sums1, sums2, sums3, out_bias_sums, db, table)
+
+    if halving:
+        for r in reductions:
+            while r.step < bits:
+                r.advance()
+
+    own_total = piece_of(grad, chip) + (own_grad - rounded_grad)
+    grad_v, grad_q = own_total[0:vq], own_total[sz.vpiece :]
+
+    def summed(x, axis, size, steps):
+        for bit in steps:
             x = x + lax.ppermute(x, axis, [(i, i ^ bit) for i in range(size)])
         return x
 
-    dp_bits = [1 << k for k in range(dp_size.bit_length() - 1)]
-    norms = jnp.stack(
-        [
-            jnp.concatenate([g[5][0:4], g[6][0:4], g[7][0:4], g[8]], 0)
-            for g in grads
-        ]
-    )
-    norms = summed(norms, "tensor", 4, [1])
-    local = jnp.concatenate([jnp.concatenate([g[3].reshape(-1), g[4].reshape(-1)]) for g in grads])
-    packed = jnp.concatenate([norms.reshape(-1), local])
-    packed = summed(packed, "dp", dp_size, dp_bits)
-    norms = packed[: norms.size].reshape(norms.shape)
-    local = packed[norms.size :].reshape(layers, -1)
-    scale_total = jnp.concatenate([norms[:, 0:2], norms[:, 4:6], norms[:, 8:10]], 1)
-    shift_total = jnp.concatenate([norms[:, 2:4], norms[:, 6:8], norms[:, 10:12]], 1)
-    out_bias_total = norms[:, 12:14]
-    in_bias_total = local[:, : 2 * hid].reshape(layers, 2, hid)
-    rel_total = local[:, 2 * hid :].reshape(layers, heads, SPAN * SPAN)
-
-    def projections(w):
-        return [w[:, k * edev : (k + 1) * edev] for k in range(8)]
-
-    d_in, d_out, d_up, d_down = [], [], [], []
-    for g in grads:
-        one, two = projections(g[2]), projections(g[1])
-        d_in.append(
-            jnp.stack([jnp.stack(p, 0) for p in (one[0:3], one[3:6], two[0:3], two[3:6])])
-        )
-        d_out.append(jnp.stack([one[6].T, one[7].T, two[6].T, two[7].T]))
-        d_up.append(jnp.stack([g[0][:, 0:hid], g[0][:, hid : 2 * hid]]))
-        d_down.append(jnp.stack([g[0][:, 2 * hid : 3 * hid], g[0][:, 3 * hid :]]))
+    per_norm = 14 * layers
+    count = -(-(per_norm + (2 + heads) * layers) // 8) * 8
+    (rows,) = call(
+        lambda *r: collect(layers, heads, *r),
+        [shaped((count, width), F32)],
+        [],
+        [x for g in grads for x in g],
+        name="collect",
+    )
+    twice = lax.ppermute(rows, "tensor", swap)
+    rows = rows + jnp.where(iota((count, 1), 0) < per_norm, twice, 0.0)
+    rows = summed(rows, "dp", dp_size, [1 << k for k in range(bits)])
+    scale_total, shift_total, out_bias_total, in_bias_total, rel_total = call(
+        lambda *r: deal(layers, heads, *r),
+        [shaped((6, layers, width), F32)] * 2
+        + [shaped((layers, 2, width), F32), shaped((layers, 2, hid), F32), shaped((heads, layers, TABLE), F32)],
+        [],
+        [rows],
+        name="deal",
+    )
+
+    d_up, d_down = call(
+        lambda *r: finish_mlp(layers, *r),
+        [shaped((layers, 2, block_rows, hid), F32)] * 2,
+        [],
+        feeds[::-1],
+        name="finish_mlp",
+    )
+    sums = [reductions[2 * (layers - 1 - layer) : 2 * (layers - layer)] for layer in range(layers)]
+    d_in, d_out = call(
+        lambda *r: finish_attn(layers, *r),
+        [shaped((layers, 4, 3, block_rows, edev), F32), shaped((layers, 4, edev, block_rows), F32)],
+        [],
+        [p for r in sums for p in r[1].pieces() + r[0].pieces()],
+        name="finish_attn",
+    )
     return (
         out_v[None],
         out_q[None],
         grad_v[None],
         grad_q[None],
-        scale_total,
-        shift_total,
-        jnp.stack(d_in).transpose(0, 1, 3, 2, 4),
-        jnp.stack(d_out),
-        rel_total,
-        jnp.stack(d_up),
+        scale_total.transpose(1, 0, 2),
+        shift_total.transpose(1, 0, 2),
+        d_in.transpose(0, 1, 3, 2, 4),
+        d_out,
+        rel_total.transpose(1, 0, 2),
+        d_up,
         in_bias_total,
-        jnp.stack(d_down).transpose(0, 1, 3, 2),
+        d_down.transpose(0, 1, 3, 2),
         out_bias_total,
     )
 

time: 708 us -> 546 us (0.77)
  local copies, waits for them, and re-layouts: 151 us -> 62.4 us
  other arithmetic: 57.9 us -> 14.6 us
  waiting for transfers between devices: 288 us -> 255 us
  between operations: 5.11 us -> 18 us
    ppermute x50 -> x39, waiting for transfers between devices: 265 us -> 217 us  [the longest x12 101 us: move(): got = lax.ppermute(self.ready, 'dp', [(i, i ^ bit) for i in range(dp_size)])]
    another operation x44 -> x3, local copies, waits for them, and re-layouts: 26.4 us -> 1.46 us  [the longest x2 1.46 us: scalars(): return jnp.stack(values).astype(jnp.int32)]
    convert_element_type x34 -> x21, other arithmetic: 30.3 us -> 11.4 us  [the longest x8 5.86 us: advance(): sum((p[count:2 * count].astype(F32) for p in self.parts)).astype(BF16)]
    slice x32 -> x1, local copies, waits for them, and re-layouts: 19.2 us -> 0.89 us  [on_device(): out_q = (out[sz.vpiece:] + mlp_out_bias[layers - 1, 1]).astype(BF16)]
    squeeze x15 -> x0, local copies, waits for them, and re-layouts: 16.4 us -> none  [the longest x1 6.42 us: on_device(): mlp_out[layer]]
    ppermute x12, waiting for transfers between devices: 2.23 us -> 17.7 us  [pair(): return (x, lax.ppermute(x, 'tensor', swap))]
    concatenate x4 -> x2, local copies, waits for them, and re-layouts: 12.7 us -> 0.15 us  [packed(): return jnp.concatenate([own_v, pad, own_q], 0)]
    add x11 -> x3, other arithmetic: 12.3 us -> 0.39 us  [the longest x1 0.19 us: on_device(): own_total = piece_of(grad, chip) + (own_grad - rounded_grad)]
  transfers between devices with their start and end apart: 66 -> 56, of which waited for: 32 -> 38; matrix products, arithmetic and copies ran while one was open for 20% -> 3% of each run, Pallas kernels for 11% -> 17%
where the time goes in v2:
time: 546 us; the launch traced here: 538 us
  waiting for transfers between devices  255 us (47%)
  Pallas kernels  142 us (26%)
  local copies, waits for them, and re-layouts  62.4 us (11%)
  starting transfers between devices  45.9 us (8%)
  between operations  18 us (3%)
  other arithmetic  14.6 us (3%)
    pallas_call x38, Pallas kernels, call(): pl.pallas_call(wrapped, out_shape=tuple(outs), in_specs=[smem] * len(scal...  139 us
    ppermute x12, waiting for transfers between devices, move(): got = lax.ppermute(self.ready, 'dp', [(i, i ^ bit) for i in range(dp_size)])  101 us
    ppermute x11, waiting for transfers between devices, shares(): return (kept, lax.ppermute(kept, 'tensor', cross))  91.7 us
    unnamed x403, local copies, waits for them, and re-layouts  58.5 us
    ppermute x3, waiting for transfers between devices, summed(): x = x + lax.ppermute(x, axis, [(i, i ^ bit) for i in range(size)])  20 us
    ppermute x11, starting transfers between devices, shares(): return (kept, lax.ppermute(kept, 'tensor', cross))  18.4 us
    ppermute x12, waiting for transfers between devices, pair(): return (x, lax.ppermute(x, 'tensor', swap))  17.7 us
    ppermute x12, starting transfers between devices, move(): got = lax.ppermute(self.ready, 'dp', [(i, i ^ bit) for i in range(dp_size)])  15 us
  transfers between devices with their start and end apart: 56, of which 38 were waited for; matrix products, arithmetic and copies ran while one was open for 3% of the time, Pallas kernels for 17%

profile of v2, /device:TPU:0, one launch (start us, length us, event | category | flops | bytes accessed | tf_op | source)
XLA Modules:
  0.0 537.9 jit_solution(1692425549744983152)
XLA Ops:
  28.8 8.7 %section1.2 = (bf16[480,768]{1,0:T(8,128)(2,1)S(1)}, bf16[480,768]{1,0:T(8,128)(2,1)S(1)}, bf16[144,768]{1,0:T(8,128)(2,1)S(1)}, bf16[144,576]{1,0:T(8,128)(2,1)...) custom-call(s32[8]{0:T(128)S(1)} %stack.21.refs_0_, ...), custom_call_target="tpu_custom_call" | custom-call | flops 1 | bytes 1 | tf_op jit(solution)/shard_map/section1/pallas_call | solution.py:82
  42.8 8.6 %collective-permute-done.3.refs_2_ = bf16[240,768]{1,0:T(8,128)(2,1)S(1)} collective-permute-done((bf16[240,768]{1,0:T(8,128)(2,1)S(1)}, bf16[240,768]{1,0:T(8,128)(2,1)S(1)}, u32[]{:S(2)}, u32[]{:S(2)}) %collective-permute-start.3) | collective-permute-done | bytes 368672 | tf_op jit(solution)/shard_map/ppermute | solution.py:786
  59.8 9.2 %collective-permute-done.4.refs_2_ = bf16[480,768]{1,0:T(8,128)(2,1)S(1)} collective-permute-done((bf16[480,768]{1,0:T(8,128)(2,1)S(1)}, bf16[480,768]{1,0:T(8,128)(2,1)S(1)}, u32[]{:S(2)}, u32[]{:S(2)}) %collective-permute-start.4) | collective-permute-done | bytes 737312 | tf_op jit(solution)/shard_map/ppermute | solution.py:734
  72.0 6.3 %section2.2 = (bf16[480,768]{1,0:T(8,128)(2,1)S(1)}, bf16[480,768]{1,0:T(8,128)(2,1)S(1)}, bf16[800,192]{1,0:T(8,128)(2,1)S(1)}, bf16[160,384]{1,0:T(8,128)(2,1)...) custom-call(s32[8]{0:T(128)S(1)} %stack.21.refs_0_, ...), custom_call_target="tpu_custom_call" | custom-call | flops 1 | bytes 1 | tf_op jit(solution)/shard_map/section2/pallas_call | solution.py:82
  87.7 11.7 %collective-permute-done.7.refs_2_ = bf16[480,768]{1,0:T(8,128)(2,1)S(1)} collective-permute-done((bf16[480,768]{1,0:T(8,128)(2,1)S(1)}, bf16[480,768]{1,0:T(8,128)(2,1)S(1)}, u32[]{:S(2)}, u32[]{:S(2)}) %collective-permute-start.7) | collective-permute-done | bytes 737312 | tf_op jit(solution)/shard_map/ppermute | solution.py:734
  112.5 16.2 %collective-permute-done.10.refs_2_ = bf16[480,768]{1,0:T(8,128)(2,1)S(1)} collective-permute-done((bf16[480,768]{1,0:T(8,128)(2,1)S(1)}, bf16[480,768]{1,0:T(8,128)(2,1)S(1)}, u32[]{:S(2)}, u32[]{:S(2)}) %collective-permute-start.10) | collective-permute-done | bytes 737312 | tf_op jit(solution)/shard_map/ppermute | solution.py:734
  138.2 9.1 %section1.3 = (bf16[480,768]{1,0:T(8,128)(2,1)S(1)}, bf16[480,768]{1,0:T(8,128)(2,1)S(1)}, bf16[144,768]{1,0:T(8,128)(2,1)S(1)}, bf16[144,576]{1,0:T(8,128)(2,1)...) custom-call(s32[8]{0:T(128)S(1)} %stack.22.refs_0_, ...), custom_call_target="tpu_custom_call" | custom-call | flops 1 | bytes 1 | tf_op jit(solution)/shard_map/section1/pallas_call | solution.py:82
  155.3 13.2 %collective-permute-done.13.refs_2_ = bf16[480,768]{1,0:T(8,128)(2,1)S(1)} collective-permute-done((bf16[480,768]{1,0:T(8,128)(2,1)S(1)}, bf16[480,768]{1,0:T(8,128)(2,1)S(1)}, u32[]{:S(2)}, u32[]{:S(2)}) %collective-permute-start.13) | collective-permute-done | bytes 737312 | tf_op jit(solution)/shard_map/ppermute | solution.py:734
  171.5 6.3 %section2.3 = (bf16[480,768]{1,0:T(8,128)(2,1)S(1)}, bf16[480,768]{1,0:T(8,128)(2,1)S(1)}, bf16[800,192]{1,0:T(8,128)(2,1)S(1)}, bf16[160,384]{1,0:T(8,128)(2,1)...) custom-call(s32[8]{0:T(128)S(1)} %stack.22.refs_0_, ...), custom_call_target="tpu_custom_call" | custom-call | flops 1 | bytes 1 | tf_op jit(solution)/shard_map/section2/pallas_call | solution.py:82
  187.6 11.4 %collective-permute-done.16.refs_2_ = bf16[480,768]{1,0:T(8,128)(2,1)S(1)} collective-permute-done((bf16[480,768]{1,0:T(8,128)(2,1)S(1)}, bf16[480,768]{1,0:T(8,128)(2,1)S(1)}, u32[]{:S(2)}, u32[]{:S(2)}) %collective-permute-start.16) | collective-permute-done | bytes 737312 | tf_op jit(solution)/shard_map/ppermute | solution.py:734
  222.9 16.8 %collective-permute-done.22.refs_2_ = bf16[480,768]{1,0:T(8,128)(2,1)S(1)} collective-permute-done((bf16[480,768]{1,0:T(8,128)(2,1)S(1)}, bf16[480,768]{1,0:T(8,128)(2,1)S(1)}, u32[]{:S(2)}, u32[]{:S(2)}) %collective-permute-start.22) | collective-permute-done | bytes 737312 | tf_op jit(solution)/shard_map/ppermute | solution.py:734
  244.8 7.2 %section2_back.2 = (bf16[480,768]{1,0:T(8,128)(2,1)S(1)}, bf16[480,768]{1,0:T(8,128)(2,1)S(1)}, bf16[800,192]{1,0:T(8,128)(2,1)S(1)}, bf16[160,384]{1,0:T(8,128)...) custom-call(s32[8]{0:T(128)S(1)} %stack.22.refs_0_, ...), custom_call_target="tpu_custom_call" | custom-call | flops 1 | bytes 1 | tf_op jit(solution)/shard_map/section2_back/pallas_call | solution.py:82
  260.0 13.1 %collective-permute-done.25.refs_2_ = bf16[480,768]{1,0:T(8,128)(2,1)S(1)} collective-permute-done((bf16[480,768]{1,0:T(8,128)(2,1)S(1)}, bf16[480,768]{1,0:T(8,128)(2,1)S(1)}, u32[]{:S(2)}, u32[]{:S(2)}) %collective-permute-start.25) | collective-permute-done | bytes 737312 | tf_op jit(solution)/shard_map/ppermute | solution.py:734
  277.2 11.6 %section1_back.2 = (bf16[480,768]{1,0:T(8,128)(2,1)S(1)}, bf16[480,768]{1,0:T(8,128)(2,1)S(1)}, bf16[144,576]{1,0:T(8,128)(2,1)S(1)}, bf16[800,576]{1,0:T(8,128)(2,1)S(1)}, bf16[3,144,144]{2,1,0:T(8,128)(2,1)S(1)}) custom-call(s32[8]{0:T(128)S(1)} %stack.22.refs_0_, bf16[480,768]{1,0:T(8,128)(2,1)S(1)} %get-tuple-element.437.refs_1_.refs_3_, ...), custom_call_target="tpu_custom_call" | custom-call | flops 1 | bytes 1 | tf_op jit(solution)/shard_map/section1_back/pallas_call | solution.py:82
  299.9 23.8 %collective-permute-done.29.refs_13_ = bf16[4,96,1536]{2,1,0:T(8,128)(2,1)S(1)} collective-permute-done((bf16[4,96,1536]{2,1,0:T(8,128)(2,1)S(1)}, bf16[4,96,1536]{2,1,0:T(8,128)(2,1)S(1)}, u32[]{:S(2)}, u32[]{:S(2)}) %collective-permute-start.29) | collective-permute-done | bytes 1179680 | tf_op jit(solution)/shard_map/ppermute | solution.py:888
  345.1 6.4 %collective-permute-done.33.refs_14_ = bf16[2,96,1536]{2,1,0:T(8,128)(2,1)} collective-permute-done((bf16[2,96,1536]{2,1,0:T(8,128)(2,1)}, bf16[2,96,1536]{2,1,0:T(8,128)(2,1)}, u32[]{:S(2)}, u32[]{:S(2)}) %collective-permute-start.33) | collective-permute-done | bytes 589856 | tf_op jit(solution)/shard_map/ppermute | solution.py:888
  351.5 14.5 %collective-permute-done.34.refs_9_ = bf16[4,96,1536]{2,1,0:T(8,128)(2,1)} collective-permute-done((bf16[4,96,1536]{2,1,0:T(8,128)(2,1)}, bf16[4,96,1536]{2,1,0:T(8,128)(2,1)}, u32[]{:S(2)}, u32[]{:S(2)}) %collective-permute-start.34) | collective-permute-done | bytes 1179680 | tf_op jit(solution)/shard_map/ppermute | solution.py:888
  374.9 7.4 %section2_back.3 = (bf16[480,768]{1,0:T(8,128)(2,1)S(1)}, bf16[480,768]{1,0:T(8,128)(2,1)S(1)}, bf16[800,192]{1,0:T(8,128)(2,1)S(1)}, bf16[160,384]{1,0:T(8,128)...) custom-call(s32[8]{0:T(128)S(1)} %stack.21.refs_0_, ...), custom_call_target="tpu_custom_call" | custom-call | flops 1 | bytes 1 | tf_op jit(solution)/shard_map/section2_back/pallas_call | solution.py:82
  402.1 6.4 %collective-permute-done.38.refs_10_ = bf16[2,96,1536]{2,1,0:T(8,128)(2,1)} collective-permute-done((bf16[2,96,1536]{2,1,0:T(8,128)(2,1)}, bf16[2,96,1536]{2,1,0:T(8,128)(2,1)}, u32[]{:S(2)}, u32[]{:S(2)}) %collective-permute-start.38) | collective-permute-done | bytes 589856 | tf_op jit(solution)/shard_map/ppermute | solution.py:888
  413.9 12.0 %section1_back.3 = (bf16[480,768]{1,0:T(8,128)(2,1)S(1)}, bf16[480,768]{1,0:T(8,128)(2,1)S(1)}, bf16[144,576]{1,0:T(8,128)(2,1)S(1)}, bf16[800,576]{1,0:T(8,128)(2,1)S(1)}, bf16[3,144,144]{2,1,0:T(8,128)(2,1)S(1)}) custom-call(s32[8]{0:T(128)S(1)} %stack.21.refs_0_, bf16[480,768]{1,0:T(8,128)(2,1)S(1)} %get-tuple-element.515.refs_1_.refs_3_, ...), custom_call_target="tpu_custom_call" | custom-call | flops 1 | bytes 1 | tf_op jit(solution)/shard_map/section1_back/pallas_call | solution.py:82
  433.5 14.0 %collective-permute-done.42.refs_5_ = bf16[4,96,1536]{2,1,0:T(8,128)(2,1)S(1)} collective-permute-done((bf16[4,96,1536]{2,1,0:T(8,128)(2,1)S(1)}, bf16[4,96,1536]{2,1,0:T(8,128)(2,1)S(1)}, u32[]{:S(2)}, u32[]{:S(2)}) %collective-permute-start.42) | collective-permute-done | bytes 1179680 | tf_op jit(solution)/shard_map/ppermute | solution.py:888
  455.7 18.9 %collective-permute-done.50.refs_6_ = bf16[2,96,1536]{2,1,0:T(8,128)(2,1)S(1)} collective-permute-done((bf16[2,96,1536]{2,1,0:T(8,128)(2,1)S(1)}, bf16[2,96,1536]{2,1,0:T(8,128)(2,1)S(1)}, u32[]{:S(2)}, u32[]{:S(2)}) %collective-permute-start.50) | collective-permute-done | bytes 589856 | tf_op jit(solution)/shard_map/ppermute | solution.py:888
  486.1 15.3 %collective-permute-done.48.refs_2_ = bf16[2,96,1536]{2,1,0:T(8,128)(2,1)S(1)} collective-permute-done((bf16[2,96,1536]{2,1,0:T(8,128)(2,1)S(1)}, bf16[2,96,1536]{2,1,0:T(8,128)(2,1)S(1)}, u32[]{:S(2)}, u32[]{:S(2)}) %collective-permute-start.48) | collective-permute-done | bytes 589856 | tf_op jit(solution)/shard_map/ppermute | solution.py:888
  505.4 15.9 %collective-permute-done.46 = f32[40,768]{1,0:T(8,128)S(1)} collective-permute-done((f32[40,768]{1,0:T(8,128)S(1)}, f32[40,768]{1,0:T(8,128)S(1)}, u32[]{:S(2)}, u32[]{:S(2)}) %collective-permute-start.46) | collective-permute-done | bytes 122912 | tf_op jit(solution)/shard_map/ppermute | solution.py:1071
  (589 shorter events, 235.9 us)
Async XLA Ops:
  7.2 520.0 %reduce-scatter.5.cloned.1.call-start = ((), (), s32[]{:S(2)}) async-start(), calls=%async_computation.3 | async-start | bytes 5308416 | tf_op jit(solution)/shard_map/reduce_scatter | solution.py:873
  80.9 18.6 %collective-permute-start.7 = (bf16[480,768]{1,0:T(8,128)(2,1)S(1)}, bf16[480,768]{1,0:T(8,128)(2,1)S(1)}, u32[]{:S(2)}, u32[]{:S(2)}) collective-permute-start(bf16[480,768]{1,0:T(8,128)(2,1)S(1)} %add_convert_fusion.10.refs_1_), channel_id=1, source_target_pairs={{0,2},{1,3},{2,0},{3,1},{4,6},{5,7},{6,4},{7,5},{8,10},{9,11},{10,... | collective-permute-start | bytes 2211848 | tf_op jit(solution)/shard_map/ppermute | solution.py:734
  110.1 18.6 %collective-permute-start.10 = (bf16[480,768]{1,0:T(8,128)(2,1)S(1)}, bf16[480,768]{1,0:T(8,128)(2,1)S(1)}, u32[]{:S(2)}, u32[]{:S(2)}) collective-permute-start(bf16[480,768]{1,0:T(8,128)(2,1)S(1)} %add_convert_fusion.9.refs_1_), channel_id=1, source_target_pairs={{0,2},{1,3},{2,0},{3,1},{4,6},{5,7},{6,4},{7,5},{8,10},{9,11},{10,... | collective-permute-start | bytes 2211848 | tf_op jit(solution)/shard_map/ppermute | solution.py:734
  149.9 18.6 %collective-permute-start.13 = (bf16[480,768]{1,0:T(8,128)(2,1)S(1)}, bf16[480,768]{1,0:T(8,128)(2,1)S(1)}, u32[]{:S(2)}, u32[]{:S(2)}) collective-permute-start(bf16[480,768]{1,0:T(8,128)(2,1)S(1)} %add_convert_fusion.8.refs_1_), channel_id=1, source_target_pairs={{0,2},{1,3},{2,0},{3,1},{4,6},{5,7},{6,4},{7,5},{8,10},{9,11},{10,... | collective-permute-start | bytes 2211848 | tf_op jit(solution)/shard_map/ppermute | solution.py:734
  180.4 18.6 %collective-permute-start.16 = (bf16[480,768]{1,0:T(8,128)(2,1)S(1)}, bf16[480,768]{1,0:T(8,128)(2,1)S(1)}, u32[]{:S(2)}, u32[]{:S(2)}) collective-permute-start(bf16[480,768]{1,0:T(8,128)(2,1)S(1)} %add_convert_fusion.7.refs_1_), channel_id=1, source_target_pairs={{0,2},{1,3},{2,0},{3,1},{4,6},{5,7},{6,4},{7,5},{8,10},{9,11},{10,... | collective-permute-start | bytes 2211848 | tf_op jit(solution)/shard_map/ppermute | solution.py:734
  220.9 306.3 %reduce-scatter.3.cloned.1.call-start = ((), (), s32[]{:S(2)}) async-start(), calls=%async_computation.2 | async-start | bytes 5308416 | tf_op jit(solution)/shard_map/reduce_scatter | solution.py:873
  221.1 18.6 %collective-permute-start.22 = (bf16[480,768]{1,0:T(8,128)(2,1)S(1)}, bf16[480,768]{1,0:T(8,128)(2,1)S(1)}, u32[]{:S(2)}, u32[]{:S(2)}) collective-permute-start(bf16[480,768]{1,0:T(8,128)(2,1)S(1)} %add_convert_fusion.5.refs_1_), channel_id=1, source_target_pairs={{0,2},{1,3},{2,0},{3,1},{4,6},{5,7},{6,4},{7,5},{8,10},{9,11},{10,... | collective-permute-start | bytes 2211848 | tf_op jit(solution)/shard_map/ppermute | solution.py:734
  254.5 18.6 %collective-permute-start.25 = (bf16[480,768]{1,0:T(8,128)(2,1)S(1)}, bf16[480,768]{1,0:T(8,128)(2,1)S(1)}, u32[]{:S(2)}, u32[]{:S(2)}) collective-permute-start(bf16[480,768]{1,0:T(8,128)(2,1)S(1)} %add_convert_fusion.4.refs_1_), channel_id=1, source_target_pairs={{0,2},{1,3},{2,0},{3,1},{4,6},{5,7},{6,4},{7,5},{8,10},{9,11},{10,... | collective-permute-start | bytes 2211848 | tf_op jit(solution)/shard_map/ppermute | solution.py:734
  289.1 34.6 %collective-permute-start.29 = (bf16[4,96,1536]{2,1,0:T(8,128)(2,1)S(1)}, bf16[4,96,1536]{2,1,0:T(8,128)(2,1)S(1)}, u32[]{:S(2)}, u32[]{:S(2)}) collective-permute-start(bf16[4,96,1536]{2,1,0:T(8,128)(2,1)S(1)} %get-tuple-element.446), channel_id=1, source_target_pairs={{0,4},{4,0},{8,12},{12,8},{16,20},{20,16},{24,28},{28,24},{1,5},{5... | collective-permute-start | bytes 3538952 | tf_op jit(solution)/shard_map/ppermute | solution.py:888
  291.4 32.3 %collective-permute-start.28 = (bf16[480,768]{1,0:T(8,128)(2,1)S(1)}, bf16[480,768]{1,0:T(8,128)(2,1)S(1)}, u32[]{:S(2)}, u32[]{:S(2)}) collective-permute-start(bf16[480,768]{1,0:T(8,128)(2,1)S(1)} %add_convert_fusion.3.refs_1_), channel_id=1, source_target_pairs={{0,2},{1,3},{2,0},{3,1},{4,6},{5,7},{6,4},{7,5},{8,10},{9,11},{10,... | collective-permute-start | bytes 2211848 | tf_op jit(solution)/shard_map/ppermute | solution.py:734
  331.1 34.9 %collective-permute-start.34 = (bf16[4,96,1536]{2,1,0:T(8,128)(2,1)}, bf16[4,96,1536]{2,1,0:T(8,128)(2,1)}, u32[]{:S(2)}, u32[]{:S(2)}) collective-permute-start(bf16[4,96,1536]{2,1,0:T(8,128)(2,1)} %get-tuple-element.466), channel_id=1, source_target_pairs={{0,4},{4,0},{8,12},{12,8},{16,20},{20,16},{24,28},{28,24},{1,5},{5... | collective-permute-start | bytes 3538952 | tf_op jit(solution)/shard_map/ppermute | solution.py:888
  333.4 32.6 %collective-permute-start.32 = (bf16[480,768]{1,0:T(8,128)(2,1)S(1)}, bf16[480,768]{1,0:T(8,128)(2,1)}, u32[]{:S(2)}, u32[]{:S(2)}) collective-permute-start(bf16[480,768]{1,0:T(8,128)(2,1)S(1)} %add_convert_fusion.2.refs_1_), channel_id=1, source_target_pairs={{0,2},{1,3},{2,0},{3,1},{4,6},{5,7},{6,4},{7,5},{8,10},{9,11},{10,... | collective-permute-start | bytes 2211848 | tf_op jit(solution)/shard_map/ppermute | solution.py:734
  385.7 22.8 %collective-permute-start.37 = (bf16[480,768]{1,0:T(8,128)(2,1)}, bf16[480,768]{1,0:T(8,128)(2,1)}, u32[]{:S(2)}, u32[]{:S(2)}) collective-permute-start(bf16[480,768]{1,0:T(8,128)(2,1)} %add_convert_fusion.1.refs_1_), channel_id=1, source_target_pairs={{0,2},{1,3},{2,0},{3,1},{4,6},{5,7},{6,4},{7,5},{8,10},{9,11},{10,... | collective-permute-start | bytes 2211848 | tf_op jit(solution)/shard_map/ppermute | solution.py:734
  389.6 18.9 %collective-permute-start.38 = (bf16[2,96,1536]{2,1,0:T(8,128)(2,1)}, bf16[2,96,1536]{2,1,0:T(8,128)(2,1)}, u32[]{:S(2)}, u32[]{:S(2)}) collective-permute-start(bf16[2,96,1536]{2,1,0:T(8,128)(2,1)} %add_convert_fusion.14), channel_id=1, source_target_pairs={{0,8},{4,12},{8,0},{12,4},{16,24},{20,28},{24,16},{28,20},{1,9},{5... | collective-permute-start | bytes 1769480 | tf_op jit(solution)/shard_map/ppermute | solution.py:888
  413.1 34.4 %collective-permute-start.42 = (bf16[4,96,1536]{2,1,0:T(8,128)(2,1)S(1)}, bf16[4,96,1536]{2,1,0:T(8,128)(2,1)S(1)}, u32[]{:S(2)}, u32[]{:S(2)}) collective-permute-start(bf16[4,96,1536]{2,1,0:T(8,128)(2,1)S(1)} %get-tuple-element.524), channel_id=1, source_target_pairs={{0,4},{4,0},{8,12},{12,8},{16,20},{20,16},{24,28},{28,24},{1,5},{5... | collective-permute-start | bytes 3538952 | tf_op jit(solution)/shard_map/ppermute | solution.py:888
  447.7 27.0 %collective-permute-start.50 = (bf16[2,96,1536]{2,1,0:T(8,128)(2,1)S(1)}, bf16[2,96,1536]{2,1,0:T(8,128)(2,1)S(1)}, u32[]{:S(2)}, u32[]{:S(2)}) collective-permute-start(bf16[2,96,1536]{2,1,0:T(8,128)(2,1)S(1)} %add_convert_fusion.12), channel_id=1, source_target_pairs={{0,8},{4,12},{8,0},{12,4},{16,24},{20,28},{24,16},{28,20},{1,9},{5... | collective-permute-start | bytes 1769480 | tf_op jit(solution)/shard_map/ppermute | solution.py:888
  449.1 73.6 %collective-permute-start.53 = (bf16[1,96,1536]{2,1,0:T(8,128)(2,1)S(1)}, bf16[1,96,1536]{2,1,0:T(8,128)(2,1)S(1)}, u32[]{:S(2)}, u32[]{:S(2)}) collective-permute-start(bf16[1,96,1536]{2,1,0:T(8,128)(2,1)S(1)} %add_convert_fusion.16), channel_id=1, source_target_pairs={{0,16},{4,20},{8,24},{12,28},{16,0},{20,4},{24,8},{28,12},{1,17},{... | collective-permute-start | bytes 884744 | tf_op jit(solution)/shard_map/ppermute | solution.py:888
  451.6 23.2 %collective-permute-start.41 = (bf16[480,768]{1,0:T(8,128)(2,1)S(1)}, bf16[480,768]{1,0:T(8,128)(2,1)S(1)}, u32[]{:S(2)}, u32[]{:S(2)}) collective-permute-start(bf16[480,768]{1,0:T(8,128)(2,1)S(1)} %add_convert_fusion.refs_1_), channel_id=1, source_target_pairs={{0,2},{1,3},{2,0},{3,1},{4,6},{5,7},{6,4},{7,5},{8,10},{9,11},{10,... | collective-permute-start | bytes 2211848 | tf_op jit(solution)/shard_map/ppermute | solution.py:734
  452.2 26.5 %collective-permute-start.47 = (bf16[4,96,1536]{2,1,0:T(8,128)(2,1)S(1)}, bf16[4,96,1536]{2,1,0:T(8,128)(2,1)S(1)}, u32[]{:S(2)}, u32[]{:S(2)}) collective-permute-start(bf16[4,96,1536]{2,1,0:T(8,128)(2,1)S(1)} %get-tuple-element.543), channel_id=1, source_target_pairs={{0,4},{4,0},{8,12},{12,8},{16,20},{20,16},{24,28},{28,24},{1,5},{5... | collective-permute-start | bytes 3538952 | tf_op jit(solution)/shard_map/ppermute | solution.py:888
  454.1 68.7 %collective-permute-start.52 = (bf16[1,96,1536]{2,1,0:T(8,128)(2,1)S(1)}, bf16[1,96,1536]{2,1,0:T(8,128)(2,1)S(1)}, u32[]{:S(2)}, u32[]{:S(2)}) collective-permute-start(bf16[1,96,1536]{2,1,0:T(8,128)(2,1)S(1)} %add_convert_fusion.17), channel_id=1, source_target_pairs={{0,16},{4,20},{8,24},{12,28},{16,0},{20,4},{24,8},{28,12},{1,17},{... | collective-permute-start | bytes 884744 | tf_op jit(solution)/shard_map/ppermute | solution.py:888
  474.7 48.0 %collective-permute-start.51 = (bf16[1,96,1536]{2,1,0:T(8,128)(2,1)S(1)}, bf16[1,96,1536]{2,1,0:T(8,128)(2,1)S(1)}, u32[]{:S(2)}, u32[]{:S(2)}) collective-permute-start(bf16[1,96,1536]{2,1,0:T(8,128)(2,1)S(1)} %add_convert_fusion.18), channel_id=1, source_target_pairs={{0,16},{4,20},{8,24},{12,28},{16,0},{20,4},{24,8},{28,12},{1,17},{... | collective-permute-start | bytes 884744 | tf_op jit(solution)/shard_map/ppermute | solution.py:888
  478.8 22.5 %collective-permute-start.48 = (bf16[2,96,1536]{2,1,0:T(8,128)(2,1)S(1)}, bf16[2,96,1536]{2,1,0:T(8,128)(2,1)S(1)}, u32[]{:S(2)}, u32[]{:S(2)}) collective-permute-start(bf16[2,96,1536]{2,1,0:T(8,128)(2,1)S(1)} %add_convert_fusion.13), channel_id=1, source_target_pairs={{0,8},{4,12},{8,0},{12,4},{16,24},{20,28},{24,16},{28,20},{1,9},{5... | collective-permute-start | bytes 1769480 | tf_op jit(solution)/shard_map/ppermute | solution.py:888
  485.6 18.5 %collective-permute-start.45 = (f32[40,768]{1,0:T(8,128)S(1)}, f32[40,768]{1,0:T(8,128)S(1)}, u32[]{:S(2)}, u32[]{:S(2)}) collective-permute-start(f32[40,768]{1,0:T(8,128)S(1)} %add.149), channel_id=1, source_target_pairs={{0,8},{4,12},{8,0},{12,4},{16,24},{20,28},{24,16},{28,20},{1,9},{5... | collective-permute-start | bytes 368648 | tf_op jit(solution)/shard_map/ppermute | solution.py:1071
  501.5 21.3 %collective-permute-start.49 = (bf16[1,96,1536]{2,1,0:T(8,128)(2,1)S(1)}, bf16[1,96,1536]{2,1,0:T(8,128)(2,1)S(1)}, u32[]{:S(2)}, u32[]{:S(2)}) collective-permute-start(bf16[1,96,1536]{2,1,0:T(8,128)(2,1)S(1)} %add_convert_fusion.19), channel_id=1, source_target_pairs={{0,16},{4,20},{8,24},{12,28},{16,0},{20,4},{24,8},{28,12},{1,17},{... | collective-permute-start | bytes 884744 | tf_op jit(solution)/shard_map/ppermute | solution.py:888
  (232 other events, 1433.6 us)
Sparse Core Ops, SparseCore 0:
  220.4 101.6 reduce-scatter.4
  344.7 105.3 reduce-scatter.2

commit v3 on v2

--- a/solution.py
+++ b/solution.py
@@ -49,18 +49,44 @@
         return self.ref[at]
 
 
-def call(body, outs, scalars, args, flops=0, name=None, scratch=()):
+class Rows:
+    def __init__(self, refs):
+        self.spans = [r if isinstance(r, tuple) else (r, 0, r.shape[0]) for r in refs]
+
+    def pieces(self, at):
+        rows = at[0] if isinstance(at, tuple) else slice(None)
+        total = sum(end - start for _, start, end in self.spans)
+        lo, hi, _ = rows.indices(total)
+        base = 0
+        for ref, start, end in self.spans:
+            first, last = max(lo - base, 0), min(hi - base, end - start)
+            if first < last:
+                yield ref, start + first, start + last, base + first - lo
+            base += end - start
+
+    def __getitem__(self, at):
+        cols = at[1] if isinstance(at, tuple) else slice(None)
+        parts = [ref[first:last, cols] for ref, first, last, _ in self.pieces(at)]
+        return parts[0] if len(parts) == 1 else jnp.concatenate(parts, 0)
+
+    def __setitem__(self, at, value):
+        for ref, first, last, place in self.pieces(at):
+            ref[first:last, :] = value[place : place + last - first, :]
+
+
+def call(body, outs, scalars, args, name=None, scratch=()):
     vmem = pl.BlockSpec(memory_space=pltpu.VMEM)
     smem = pl.BlockSpec(memory_space=pltpu.SMEM)
-    anywhere = pl.BlockSpec(memory_space=pltpu.HBM)
-    moved = sum(a.size * a.dtype.itemsize for a in list(args) + list(outs))
-    parts = [i for i, a in enumerate(args) if isinstance(a, Part)]
-    specs = [anywhere if isinstance(a, Part) else vmem for a in args]
-    arrays = [a.array if isinstance(a, Part) else a for a in args]
-    landing = [pltpu.VMEM(args[i].rest, args[i].dtype) for i in parts]
+    hbm = pl.BlockSpec(memory_space=pltpu.HBM)
+    flat = [x for a in args for x in (a if isinstance(a, list) else [a])]
+    flat_outs = [x for o in outs for x in (o if isinstance(o, list) else [o])]
+    parts = [i for i, a in enumerate(flat) if isinstance(a, Part)]
+    specs = [hbm if isinstance(a, Part) else vmem for a in flat]
+    arrays = [a.array if isinstance(a, Part) else a for a in flat]
+    landing = [pltpu.VMEM(flat[i].rest, flat[i].dtype) for i in parts]
     if parts:
         landing.append(pltpu.SemaphoreType.DMA((len(parts),)))
-    first, end = len(scalars), len(scalars) + len(args) + len(outs) + len(scratch)
+    first, end = len(scalars), len(scalars) + len(flat) + len(flat_outs) + len(scratch)
 
     def wrapped(*refs):
         refs = list(refs)
@@ -68,27 +94,34 @@
         coming = []
         for k, i in enumerate(parts):
             source = refs[first + i]
-            if args[i].lead:
-                source = source.at[args[i].lead]
+            if flat[i].lead:
+                source = source.at[flat[i].lead]
             copy = pltpu.make_async_copy(source, buffers[k], buffers[-1].at[k])
             copy.start()
             coming.append(Arriving(buffers[k], copy))
             refs[first + i] = coming[-1]
-        body(*refs[:end])
+        given = iter(refs[:end])
+        grouped = [next(given) for _ in scalars]
+        for x in list(args) + list(outs):
+            grouped.append(Rows([next(given) for _ in x]) if isinstance(x, list) else next(given))
+        body(*grouped, *given)
         for piece in coming:
             if piece.copy is not None:
                 piece.copy.wait()
 
-    return pl.pallas_call(
-        wrapped,
-        out_shape=tuple(outs),
-        in_specs=[smem] * len(scalars) + specs,
-        out_specs=tuple(vmem for _ in outs),
-        scratch_shapes=list(scratch) + landing,
-        compiler_params=pltpu.CompilerParams(vmem_limit_bytes=VMEM_LIMIT),
-        cost_estimate=pl.CostEstimate(flops=1, bytes_accessed=1, transcendentals=0),
-        name=name,
-    )(*scalars, *arrays)
+    got = iter(
+        pl.pallas_call(
+            wrapped,
+            out_shape=tuple(flat_outs),
+            in_specs=[smem] * len(scalars) + specs,
+            out_specs=tuple(vmem for _ in flat_outs),
+            scratch_shapes=list(scratch) + landing,
+            compiler_params=pltpu.CompilerParams(vmem_limit_bytes=VMEM_LIMIT),
+            cost_estimate=pl.CostEstimate(flops=1, bytes_accessed=1, transcendentals=0),
+            name=name,
+        )(*scalars, *arrays)
+    )
+    return [[next(got) for _ in o] if isinstance(o, list) else next(got) for o in outs]
 
 
 def tie(*groups):
@@ -108,6 +141,9 @@
         self.vp = 2 * self.vpiece
         self.piece = self.vpiece + self.qquart
         self.half = 2 * self.piece
+        self.near = self.half // 2
+        self.q1 = self.near - self.vp
+        self.q2 = self.half - self.near
 
 
 def iota(shape, dim):
@@ -128,10 +164,39 @@
 
 
 def query_of(index, core, sz):
-    second = (index >= sz.qh).astype(jnp.int32)
-    row = index - second * sz.qh
+    far = (index >= 2 * sz.q1).astype(jnp.int32)
+    row = index - far * 2 * sz.q1
+    size = sz.q1 + far * (sz.q2 - sz.q1)
+    second = (row >= size).astype(jnp.int32)
+    row = row - second * size + far * sz.q1
     half = second + core - 2 * second * core
     return row + jnp.where(row >= sz.qquart, sz.qquart, 0) + half * sz.qquart
+
+
+def patch_rows(mine, theirs, sz):
+    return jnp.concatenate([mine[0 : sz.vp, :], theirs[0 : sz.vp, :]], 0)
+
+
+def near_rows(mine, theirs, sz):
+    return jnp.concatenate([mine[sz.vp : sz.near, :], theirs[sz.vp : sz.near, :]], 0)
+
+
+def far_rows(mine, theirs, sz):
+    return jnp.concatenate([mine[sz.near :, :], theirs[sz.near :, :]], 0)
+
+
+def query_rows(mine, theirs, sz):
+    return jnp.concatenate([near_rows(mine, theirs, sz), far_rows(mine, theirs, sz)], 0)
+
+
+def give_patches(mine, theirs, value, sz):
+    mine[0 : sz.vp, :] = value[0 : sz.vp]
+    theirs[0 : sz.vp, :] = value[sz.vp :]
+
+
+def give_near(mine, theirs, value, sz):
+    mine[sz.vp : sz.near, :] = value[0 : sz.q1]
+    theirs[sz.vp : sz.near, :] = value[sz.q1 : 2 * sz.q1]
 
 
 def window_permutation(sc, sz):
@@ -163,9 +228,9 @@
     return keys == asks
 
 
-def self_mask(sc, sz):
+def self_mask(sc, sz, count, base):
     keys = query_of(iota((sz.qlen, 1), 0), sc[0], sz)
-    asks = query_of(iota((1, sz.qlen), 1), sc[0], sz)
+    asks = query_of(iota((1, count), 1) + base, sc[0], sz)
     return keys <= jnp.maximum(asks, sc[1] - 1)
 
 
@@ -177,9 +242,9 @@
     return patch_of(iota((2 * sz.vp, 1), 0), sc[0], sz) >= 0
 
 
-def masked(scores, kind, sc, sz):
+def masked(scores, kind, sc, sz, base=0):
     if kind == "self":
-        return jnp.where(self_mask(sc, sz), scores, NEG)
+        return jnp.where(self_mask(sc, sz, scores.shape[1], base), scores, NEG)
     if kind == "question":
         return jnp.where(question_mask(sc, sz), scores, NEG)
     if kind == "window":
@@ -190,7 +255,7 @@
 
 def allowed(kind, sc, sz):
     if kind == "self":
-        return self_mask(sc, sz)
+        return self_mask(sc, sz, sz.qlen, 0)
     if kind == "question":
         return question_mask(sc, sz)
     if kind == "window":
@@ -201,11 +266,11 @@
 SCALE = HDIM**-0.5
 
 
-def attend(q, k, v, addend, kind, sc, sz):
+def attend(q, k, v, addend, kind, sc, sz, base):
     scores = nt(k, q) * SCALE
     if addend is not None:
         scores = scores + addend
-    scores = masked(scores, kind, sc, sz)
+    scores = masked(scores, kind, sc, sz, base)
     top = jnp.max(scores, 0, keepdims=True)
     e = jnp.exp(scores - top)
     inv = 1.0 / jnp.sum(e, 0, keepdims=True)
@@ -233,11 +298,11 @@
     return ref[:, start : start + HDIM]
 
 
-def run_heads(q_of, k_of, v_of, bias, kind, sc, sz, o_ref, st_ref, heads):
+def run_heads(q_of, k_of, v_of, bias, kind, sc, sz, o_ref, st_ref, heads, base=0):
     outs = []
     for h in range(heads):
         o_t, top, inv = attend(
-            q_of(h), k_of(h), v_of(h), None if bias is None else bias[h], kind, sc, sz
+            q_of(h), k_of(h), v_of(h), None if bias is None else bias[h], kind, sc, sz, base
         )
         outs.append(o_t)
         st_ref[h : h + 1, :] = top
@@ -245,8 +310,13 @@
     o_ref[...] = jnp.concatenate(outs, 0).T.astype(BF16)
 
 
-def section1(sz, heads, sc, nm, nth, w0, w1, wo0, wo1, bias, pm, pt, nvw, qkvv, ov, stv, qkvq, oq, stq, ow):
-    vp, qh = sz.vp, sz.qh
+def section1_far(sz, sc, nm, nth, w1, qkvf):
+    qkvf[0 : sz.q2, :] = nt(nm[...], w1[...]).astype(BF16)
+    qkvf[sz.q2 :, :] = nt(nth[...], w1[...]).astype(BF16)
+
+
+def section1_near(sz, heads, sc, nm, nth, qkvf, w0, w1, wo0, wo1, bias, pm, pt, nvw, qkvv, ov, stv, qkvn, on, stn, ow):
+    vp = sz.vp
     mine, theirs = window_permutation(sc, sz)
     nv = (nn(mine, nm[0:vp, :]) + nn(theirs, nth[0:vp, :])).astype(BF16)
     nvw[...] = nv
@@ -259,57 +329,82 @@
     )
     ov[0:vp, :] = tn(mine, ow[...]).astype(BF16)
     ov[vp : 2 * vp, :] = tn(theirs, ow[...]).astype(BF16)
-    pm[0:vp, :] = nn(ov[0:vp, :], wo0[...]).astype(BF16)
-    pt[0:vp, :] = nn(ov[vp : 2 * vp, :], wo0[...]).astype(BF16)
-    qkvq[0:qh, :] = nt(nm[vp:, :], w1[...]).astype(BF16)
-    qkvq[qh:, :] = nt(nth[vp:, :], w1[...]).astype(BF16)
+    give_patches(pm, pt, nn(ov[...], wo0[...]).astype(BF16), sz)
+    qkvn[0 : sz.q1, :] = nt(nm[vp:, :], w1[...]).astype(BF16)
+    qkvn[sz.q1 :, :] = nt(nth[vp:, :], w1[...]).astype(BF16)
+    every = Rows([qkvn, qkvf])
     run_heads(
-        lambda h: head(qkvq, 0, h, heads),
-        lambda h: head(qkvq, 1, h, heads),
-        lambda h: head(qkvq, 2, h, heads),
-        None, "self", sc, sz, oq, stq, heads,
-    )
-    pm[vp:, :] = nn(oq[0:qh, :], wo1[...]).astype(BF16)
-    pt[vp:, :] = nn(oq[qh:, :], wo1[...]).astype(BF16)
-
-
-def section2(sz, heads, sc, nm, nth, w2, w3, wo2, wo3, pm, pt, qq, kvv, oq, stq, qv, kvq, ov, stv):
-    vp, qh = sz.vp, sz.qh
+        lambda h: head(qkvn, 0, h, heads),
+        lambda h: head(every, 1, h, heads),
+        lambda h: head(every, 2, h, heads),
+        None, "self", sc, sz, on, stn, heads,
+    )
+    give_near(pm, pt, nn(on[...], wo1[...]).astype(BF16), sz)
+
+
+def section1_rest(sz, heads, sc, qkvn, qkvf, wo1, pm, pt, of, stf):
+    every = Rows([qkvn, qkvf])
+    run_heads(
+        lambda h: head(qkvf, 0, h, heads),
+        lambda h: head(every, 1, h, heads),
+        lambda h: head(every, 2, h, heads),
+        None, "self", sc, sz, of, stf, heads, 2 * sz.q1,
+    )
+    pm[...] = nn(of[0 : sz.q2, :], wo1[...]).astype(BF16)
+    pt[...] = nn(of[sz.q2 :, :], wo1[...]).astype(BF16)
+
+
+def section2_near(sz, heads, sc, nm, nth, w2, w3, qv, kvv, qn, kvn, on, stn):
     e = heads * HDIM
-    for rows, ref in ((slice(0, qh), nm), (slice(qh, 2 * qh), nth)):
-        x = ref[vp:, :]
-        qq[rows, :] = nt(x, w2[0:e, :]).astype(BF16)
-        kvq[rows, :] = nt(x, w3[e:, :]).astype(BF16)
-    for rows, ref in ((slice(0, vp), nm), (slice(vp, 2 * vp), nth)):
-        x = ref[0:vp, :]
-        qv[rows, :] = nt(x, w3[0:e, :]).astype(BF16)
-        kvv[rows, :] = nt(x, w2[e:, :]).astype(BF16)
+    v = patch_rows(nm, nth, sz)
+    q = near_rows(nm, nth, sz)
+    qv[...] = nt(v, w3[0:e, :]).astype(BF16)
+    kvv[...] = nt(v, w2[e:, :]).astype(BF16)
+    qn[...] = nt(q, w2[0:e, :]).astype(BF16)
+    kvn[...] = nt(q, w3[e:, :]).astype(BF16)
     run_heads(
-        lambda h: head(qq, 0, h, heads),
+        lambda h: head(qn, 0, h, heads),
         lambda h: head(kvv, 0, h, heads),
         lambda h: head(kvv, 1, h, heads),
-        None, "patch", sc, sz, oq, stq, heads,
-    )
+        None, "patch", sc, sz, on, stn, heads,
+    )
+
+
+def section2_far(sz, heads, sc, nm, nth, kvv, w2, w3, wo2, pm, pt, qf, kvf, of, stf):
+    e = heads * HDIM
+    x = jnp.concatenate([nm[...], nth[...]], 0)
+    qf[...] = nt(x, w2[0:e, :]).astype(BF16)
+    kvf[...] = nt(x, w3[e:, :]).astype(BF16)
+    run_heads(
+        lambda h: head(qf, 0, h, heads),
+        lambda h: head(kvv, 0, h, heads),
+        lambda h: head(kvv, 1, h, heads),
+        None, "patch", sc, sz, of, stf, heads,
+    )
+    pm[...] = nn(of[0 : sz.q2, :], wo2[...]).astype(BF16)
+    pt[...] = nn(of[sz.q2 :, :], wo2[...]).astype(BF16)
+
+
+def section2_rest(sz, heads, sc, qv, kvn, kvf, on, wo2, wo3, pm, pt, ov, stv):
+    every = Rows([kvn, kvf])
+    give_near(pm, pt, nn(on[...], wo2[...]).astype(BF16), sz)
     run_heads(
         lambda h: head(qv, 0, h, heads),
-        lambda h: head(kvq, 0, h, heads),
-        lambda h: head(kvq, 1, h, heads),
+        lambda h: head(every, 0, h, heads),
+        lambda h: head(every, 1, h, heads),
         None, "question", sc, sz, ov, stv, heads,
     )
-    pm[0:vp, :] = nn(ov[0:vp, :], wo3[...]).astype(BF16)
-    pt[0:vp, :] = nn(ov[vp:, :], wo3[...]).astype(BF16)
-    pm[vp:, :] = nn(oq[0:qh, :], wo2[...]).astype(BF16)
-    pt[vp:, :] = nn(oq[qh:, :], wo2[...]).astype(BF16)
+    give_patches(pm, pt, nn(ov[...], wo3[...]).astype(BF16), sz)
 
 
 GELU_C = 0.7978845608028654
 GELU_A = 0.044715
 
 
-def section3(sz, layer, nm, nth, wi, bi, wo, pm, pt, g, gp):
-    vp, half = sz.vp, sz.half
-    for ref, out, base in ((nm, pm, 0), (nth, pt, half)):
-        for lo, hi, e in ((0, vp, 0), (vp, half, 1)):
+def section3(sz, layer, spans, nm, nth, wi, bi, wo, pm, pt, g, gp):
+    count = g.shape[0] // 2
+    for ref, out, base in ((nm, pm, 0), (nth, pt, count)):
+        for lo, hi, e in spans:
             h = nn(ref[lo:hi, :], wi[e]) + bi[layer, e : e + 1, :]
             h2 = h * h
             t = jnp.tanh(GELU_C * h * (1.0 + GELU_A * h2))
@@ -348,18 +443,27 @@
     return dq, dkv
 
 
-def section2_back(sz, heads, sc, dm, dt, w2, w3, wo2, wo3, qq, kvv, stq, qv, kvq, stv, pm, pt, dqq, dkvv, dqv, dkvq, doq, dov):
-    vp, qh = sz.vp, sz.qh
+def stats(near, far):
+    return jnp.concatenate([near[...], far[...]], 1)
+
+
+def give_queries(mine, theirs, value, sz):
+    give_near(mine, theirs, value[0 : 2 * sz.q1], sz)
+    mine[sz.near :, :] = value[2 * sz.q1 : 2 * sz.q1 + sz.q2]
+    theirs[sz.near :, :] = value[2 * sz.q1 + sz.q2 :]
+
+
+def section2_back(
+    sz, heads, sc, dm, dt, w2, w3, wo2, wo3, qq, kvv, stn, stf, qv, kvq, stv, pm, pt, dqq, dkvv, dqv, dkvq, doq, dov
+):
     e = heads * HDIM
-    doq[0:qh, :] = nt(dm[vp:, :], wo2[...]).astype(BF16)
-    doq[qh:, :] = nt(dt[vp:, :], wo2[...]).astype(BF16)
-    dov[0:vp, :] = nt(dm[0:vp, :], wo3[...]).astype(BF16)
-    dov[vp:, :] = nt(dt[0:vp, :], wo3[...]).astype(BF16)
+    doq[...] = nt(query_rows(dm, dt, sz), wo2[...]).astype(BF16)
+    dov[...] = nt(patch_rows(dm, dt, sz), wo3[...]).astype(BF16)
     dq, dkv = back_heads(
         lambda h: head(qq, 0, h, heads),
         lambda h: head(kvv, 0, h, heads),
         lambda h: head(kvv, 1, h, heads),
-        None, "patch", sc, sz, stq, lambda h: head(doq, 0, h, heads), None, heads,
+        None, "patch", sc, sz, stats(stn, stf), lambda h: head(doq, 0, h, heads), None, heads,
     )
     dqq[...] = dq
     dkvv[...] = dkv
@@ -371,13 +475,14 @@
     )
     dqv[...] = dq
     dkvq[...] = dkv
-    for out, qrow, vrow in ((pm, slice(0, qh), slice(0, vp)), (pt, slice(qh, 2 * qh), slice(vp, 2 * vp))):
-        out[vp:, :] = (nn(dqq[qrow, :], w2[0:e, :]) + nn(dkvq[qrow, :], w3[e:, :])).astype(BF16)
-        out[0:vp, :] = (nn(dqv[vrow, :], w3[0:e, :]) + nn(dkvv[vrow, :], w2[e:, :])).astype(BF16)
-
-
-def section1_back(sz, heads, sc, dm, dt, w0, w1, wo0, wo1, bias, qkvv, stv, qkvq, stq, pm, pt, dqkvv, dqkvq, ds, doq, dov):
-    vp, qh = sz.vp, sz.qh
+    give_queries(pm, pt, (nn(dqq[...], w2[0:e, :]) + nn(dkvq[...], w3[e:, :])).astype(BF16), sz)
+    give_patches(pm, pt, (nn(dqv[...], w3[0:e, :]) + nn(dkvv[...], w2[e:, :])).astype(BF16), sz)
+
+
+def section1_back(
+    sz, heads, sc, dm, dt, w0, w1, wo0, wo1, bias, qkvv, stv, qkvq, stn, stf, pm, pt, dqkvv, dqkvq, ds, doq, dov
+):
+    vp = sz.vp
     e = heads * HDIM
     mine, theirs = window_permutation(sc, sz)
     do_m = nt(dm[0:vp, :], wo0[...]).astype(BF16)
@@ -394,18 +499,16 @@
     dn = nn(dqkvv[...], w0[...]).astype(BF16)
     pm[0:vp, :] = tn(mine, dn).astype(BF16)
     pt[0:vp, :] = tn(theirs, dn).astype(BF16)
-    doq[0:qh, :] = nt(dm[vp:, :], wo1[...]).astype(BF16)
-    doq[qh:, :] = nt(dt[vp:, :], wo1[...]).astype(BF16)
+    doq[...] = nt(query_rows(dm, dt, sz), wo1[...]).astype(BF16)
     dq, dkv = back_heads(
         lambda h: head(qkvq, 0, h, heads),
         lambda h: head(qkvq, 1, h, heads),
         lambda h: head(qkvq, 2, h, heads),
-        None, "self", sc, sz, stq, lambda h: head(doq, 0, h, heads), None, heads,
+        None, "self", sc, sz, stats(stn, stf), lambda h: head(doq, 0, h, heads), None, heads,
     )
     dqkvq[:, 0:e] = dq
     dqkvq[:, e:] = dkv
-    pm[vp:, :] = nn(dqkvq[0:qh, :], w1[...]).astype(BF16)
-    pt[vp:, :] = nn(dqkvq[qh:, :], w1[...]).astype(BF16)
+    give_queries(pm, pt, nn(dqkvq[...], w1[...]).astype(BF16), sz)
 
 
 def kept_order(order):
@@ -433,7 +536,7 @@
 
 def section3_weights(sz, sc, nm, nth, dm, dt, g, dh, db, out):
     vp, half = sz.vp, sz.half
-    hid = g.shape[1]
+    hid = dh.shape[1]
     for e, lo, hi in ((0, 0, vp), (1, vp, half)):
         into = tn(nm[lo:hi, :], dh[lo:hi, :]) + tn(nth[lo:hi, :], dh[half + lo : half + hi, :])
         away = tn(dm[lo:hi, :], g[lo:hi, :]) + tn(dt[lo:hi, :], g[half + lo : half + hi, :])
@@ -445,31 +548,22 @@
 
 
 def section2_weights(sz, heads, sc, nm, nth, dm, dt, dqq, dkvv, dqv, dkvq, oq, ov, store):
-    vp, qh = sz.vp, sz.qh
     e = heads * HDIM
-
-    def both(a_m, a_t, b, cut, lo, hi):
-        return tn(a_m[lo:hi, :], b[0:cut, :]) + tn(a_t[lo:hi, :], b[cut:, :])
-
-    store_blocks(sc, store, 0, both(nm, nth, dqq, qh, vp, sz.half))
-    store_blocks(sc, store, e, both(nm, nth, dkvv, vp, 0, vp))
-    store_blocks(sc, store, 3 * e, both(nm, nth, dqv, vp, 0, vp))
-    store_blocks(sc, store, 4 * e, both(nm, nth, dkvq, qh, vp, sz.half))
-    store_blocks(sc, store, 6 * e, both(dm, dt, oq, qh, vp, sz.half))
-    store_blocks(sc, store, 7 * e, both(dm, dt, ov, vp, 0, vp))
+    nq, nv = query_rows(nm, nth, sz), patch_rows(nm, nth, sz)
+    store_blocks(sc, store, 0, tn(nq, dqq[...]))
+    store_blocks(sc, store, e, tn(nv, dkvv[...]))
+    store_blocks(sc, store, 3 * e, tn(nv, dqv[...]))
+    store_blocks(sc, store, 4 * e, tn(nq, dkvq[...]))
+    store_blocks(sc, store, 6 * e, tn(query_rows(dm, dt, sz), oq[...]))
+    store_blocks(sc, store, 7 * e, tn(patch_rows(dm, dt, sz), ov[...]))
 
 
 def section1_weights(sz, heads, sc, nm, nth, dm, dt, nvw, dqkvv, dqkvq, oq, ov, store):
-    vp, qh = sz.vp, sz.qh
     e = heads * HDIM
-
-    def both(a_m, a_t, b, cut, lo, hi):
-        return tn(a_m[lo:hi, :], b[0:cut, :]) + tn(a_t[lo:hi, :], b[cut:, :])
-
     store_blocks(sc, store, 0, tn(nvw[...], dqkvv[...]))
-    store_blocks(sc, store, 3 * e, both(nm, nth, dqkvq, qh, vp, sz.half))
-    store_blocks(sc, store, 6 * e, both(dm, dt, ov, vp, 0, vp))
-    store_blocks(sc, store, 7 * e, both(dm, dt, oq, qh, vp, sz.half))
+    store_blocks(sc, store, 3 * e, tn(query_rows(nm, nth, sz), dqkvq[...]))
+    store_blocks(sc, store, 6 * e, tn(patch_rows(dm, dt, sz), ov[...]))
+    store_blocks(sc, store, 7 * e, tn(query_rows(dm, dt, sz), oq[...]))
 
 
 def in_order(sz, chip, own, other, out):
@@ -504,8 +598,8 @@
         sums[4 + e : 5 + e, :] = jnp.sum(grad[lo:hi, :], 0, keepdims=True)
 
 
-def add_norm(sz, layer, first, x, a, b, extra, scale, shift, y, n):
-    for lo, hi, e in ((0, sz.vp, 0), (sz.vp, sz.half, 1)):
+def add_norm(spans, layer, first, x, a, b, extra, scale, shift, y, n):
+    for lo, hi, e in spans:
         gain, bias = scale[first + e, layer : layer + 1, :], shift[first + e, layer : layer + 1, :]
         value = x[lo:hi, :] + (a[lo:hi, :].astype(F32) + b[lo:hi, :].astype(F32))
         if extra is not None:
@@ -693,16 +787,49 @@
         q = jnp.where(place == 0, rows[vp : vp + qq_], rows[vp + qq_ :])
         return jnp.concatenate([v, q], 0)
 
+    def core_swap(x):
+        if isinstance(x, list):
+            return [core_swap(p) for p in x]
+        return lax.ppermute(x, "tensor", swap)
+
+    def across(x):
+        return lax.ppermute(x, "tensor", cross)
+
     def pair_sum(mine, theirs):
-        got = lax.ppermute(theirs, "tensor", swap)
-        return (mine.astype(F32) + got.astype(F32)).astype(BF16)
+        got = core_swap(theirs)
+        if not isinstance(got, list):
+            return (mine.astype(F32) + got.astype(F32)).astype(BF16)
+
+        def body(a, b, out):
+            out[...] = (a[...].astype(F32) + b[...].astype(F32)).astype(BF16)
+
+        return call(body, [shaped(mine.shape)], [], [mine, got], name="pair_sum")[0]
 
     def pair(x):
-        return x, lax.ppermute(x, "tensor", swap)
-
-    rows_bf = shaped((half, width))
+        return x, core_swap(x)
+
+    far = half - sz.near
+    near_bf, far_bf = shaped((sz.near, width)), shaped((far, width))
+
+    def halved(rows):
+        first = -(-rows // 32) * 16
+        return [shaped((first, width)), shaped((rows - first, width))]
+
+    near_two, far_two = halved(sz.near), halved(far)
+    rows_bf = [shaped((half, width))]
     rows_f = shaped((half, width), F32)
-    mac = 2 * half * width
+    near_spans = ((0, vp, 0), (vp, sz.near, 1))
+    far_spans = ((0, far, 1),)
+
+    def natural(near_part, far_part):
+        return Rows(
+            [
+                (near_part, 0, sz.near),
+                (far_part, 0, far),
+                (near_part, sz.near, 2 * sz.near),
+                (far_part, far, 2 * far),
+            ]
+        )
 
     own = packed(visual[0], queries[0])
     other = lax.ppermute(own, "tensor", cross)
@@ -720,18 +847,15 @@
     own_grad = packed(grad_visual_out[0], grad_query_out[0])
     rounded_grad = lax.reduce_precision(own_grad, 8, 7)
 
-    def next_norm(stream, a, b, layer, first, extra):
-        args = [stream, a, b] + ([mlp_out_bias] if extra else []) + [scale, shift]
+    def next_norm(spans, x, a, b, layer, first, extra=False):
+        args = [x, a, b] + ([mlp_out_bias] if extra else []) + [scale, shift]
 
         def body(x, a, b, *rest):
             if not extra:
                 rest = (None,) + rest
-            add_norm(sz, layer, first, x, a, b, *rest)
-
-        return call(body, [rows_f, rows_bf], [], args, name="norm")
-
-    def shares(kept):
-        return kept, lax.ppermute(kept, "tensor", cross)
+            add_norm(spans, layer, first, x, a, b, *rest)
+
+        return call(body, [shaped(x.shape, F32), halved(x.shape[0])], [], args, name="norm")
 
     fetched = {}
 
@@ -773,45 +897,73 @@
 
     fetch(0, 1, own)
     other, fetched[0, 1] = tie(other, fetched[0, 1])
-    stream, normed = call(
-        lambda *r: open_stream(sz, *r), [rows_f, rows_bf], scal[0:1], [own, other, scale, shift], name="open_stream"
-    )
+    (x_near, x_far), pieces = call(
+        lambda *r: open_stream(sz, *r),
+        [[shaped((sz.near, width), F32), shaped((far, width), F32)], near_two + far_two],
+        scal[0:1],
+        [own, other, scale, shift],
+        name="open_stream",
+    )
+    n_near, n_far = pieces[0:2], pieces[2:4]
 
     saved = []
     for layer in range(layers):
         sc = scal[layer]
-        nm, nth = pair(normed)
+        w0, w1, wo0, wo1 = fetched[layer, 1]
+        if layer > 0:
+            got_far, _ = tie(got_far, kept_near)
+            got_far, fetched[layer, 1] = tie(got_far, fetched[layer, 1])
+            w0, w1, wo0, wo1 = fetched[layer, 1]
+            x_far, n_far = next_norm(far_spans, x_far, kept_far, got_far, layer, 0, True)
+        t_far = core_swap(n_far)
+        (qkvf,) = call(
+            lambda *r: section1_far(sz, *r), [shaped((2 * far, 3 * edev))], [sc], [n_far, t_far, w1], name="section1"
+        )
+        if layer > 0:
+            got_near, qkvf = tie(got_near, qkvf)
+            x_near, n_near = next_norm(near_spans, x_near, kept_near, got_near, layer, 0, True)
+        t_near = core_swap(n_near)
         if layer == 0:
-            sent_grad, nth = tie(rounded_grad.astype(BF16), nth)
-            other_grad = lax.ppermute(sent_grad, "tensor", cross)
-        part = call(
-            lambda *r: section1(sz, heads, *r),
+            sent_grad, _ = tie(rounded_grad.astype(BF16), t_far)
+            other_grad = across(sent_grad)
+            other_grad, qkvf = tie(other_grad, qkvf)
+        x1, n1, t1 = [x_near, x_far], n_near + n_far, t_near + t_far
+        pm, pt, nvw, qkvv, ov, stv, qkvn, on, stn = call(
+            lambda *r: section1_near(sz, heads, *r),
             [
-                rows_bf,
-                rows_bf,
+                near_bf,
+                near_two,
                 shaped((sz.vis, width)),
                 shaped((sz.vis, 3 * edev)),
                 shaped((2 * vp, edev)),
                 shaped((8, sz.vis), F32),
-                shaped((sz.qlen, 3 * edev)),
-                shaped((sz.qlen, edev)),
-                shaped((8, sz.qlen), F32),
+                shaped((2 * sz.q1, 3 * edev)),
+                shaped((2 * sz.q1, edev)),
+                shaped((8, 2 * sz.q1), F32),
             ],
             [sc],
-            [
-                nm, nth, *fetched[layer, 1], Part(bias_all, layer),
-            ],
-            flops=mac * 4 * edev * 2 + 8 * heads * HDIM * sz.qlen * sz.qlen,
+            [n_near, t_near, qkvf, w0, w1, wo0, wo1, Part(bias_all, layer)],
             name="section1",
             scratch=[pltpu.VMEM((sz.vis, edev), BF16)],
         )
-        kept1 = (stream, nm, nth) + tuple(part[2:9])
-        kept = pair_sum(part[0], part[1])
+        kept_near = pair_sum(pm, pt)
+        got_near = across(kept_near)
+        _, later = tie(kept_near, qkvn)
+        pm, pt, of, stf = call(
+            lambda *r: section1_rest(sz, heads, *r),
+            [far_bf, far_two, shaped((2 * far, edev)), shaped((8, 2 * far), F32)],
+            [sc],
+            [later, qkvf, wo1],
+            name="section1",
+        )
+        saved1 = (x1, n1, t1, nvw, qkvv, ov, stv, [qkvn, qkvf], [on, of], stn, stf)
+        kept_far = pair_sum(pm, pt)
+        got_far = across(kept_far)
+
+        fetch(layer, 2, kept_near)
+        got_near, fetched[layer, 2], _ = tie(got_near, fetched[layer, 2], kept_far)
         if layer == 0:
-            kept, other_grad = tie(kept, other_grad)
-        a, b = shares(kept)
-        if layer == 0:
-            other_grad, sent_grad, a2 = tie(other_grad, sent_grad, a)
+            other_grad, sent_grad, _ = tie(other_grad, sent_grad, kept_far)
             grad, dy, grad_sums = call(
                 lambda *r: open_grad(sz, *r),
                 [rows_f, rows_bf, shaped((8, width), F32)],
@@ -819,49 +971,89 @@
                 [sent_grad, other_grad],
                 name="open_grad",
             )
-            b, grad, dy = tie(b, grad, dy)
-        b = fetch_beside(layer, 2, a, b)
-        stream, normed = next_norm(stream, a, b, layer, 2, False)
-        nm, nth = pair(normed)
-        part = call(
-            lambda *r: section2(sz, heads, *r),
+            got_near, grad, dy = tie(got_near, grad, dy)
+        w2, w3, wo2, wo3 = fetched[layer, 2]
+        x_near, n_near = next_norm(near_spans, x_near, kept_near, got_near, layer, 2)
+        t_near = core_swap(n_near)
+        qv, kvv, qn, kvn, on, stn = call(
+            lambda *r: section2_near(sz, heads, *r),
             [
-                rows_bf,
-                rows_bf,
-                shaped((sz.qlen, edev)),
+                shaped((2 * vp, edev)),
                 shaped((2 * vp, 2 * edev)),
-                shaped((sz.qlen, edev)),
-                shaped((8, sz.qlen), F32),
-                shaped((2 * vp, edev)),
-                shaped((sz.qlen, 2 * edev)),
-                shaped((2 * vp, edev)),
-                shaped((8, 2 * vp), F32),
+                shaped((2 * sz.q1, edev)),
+                shaped((2 * sz.q1, 2 * edev)),
+                shaped((2 * sz.q1, edev)),
+                shaped((8, 2 * sz.q1), F32),
             ],
             [sc],
-            [nm, nth, *fetched[layer, 2]],
-            flops=mac * 4 * edev * 2,
+            [n_near, t_near, w2, w3],
             name="section2",
         )
-        kept2 = (stream, nm, nth) + tuple(part[2:])
-        a, b = shares(pair_sum(part[0], part[1]))
-        b = fetch_beside(layer, 3, a, b)
-        stream, normed = next_norm(stream, a, b, layer, 4, False)
-        nm, nth = pair(normed)
-        part = call(
-            lambda *r: section3(sz, layer, *r),
-            [rows_bf, rows_bf, shaped((2 * half, hid)), shaped((2 * half, hid))],
-            [],
-            [nm, nth, fetched[layer, 3][0], mlp_in_bias, fetched[layer, 3][1]],
-            flops=mac * hid * 4,
-            name="section3",
-        )
-        kept3 = (stream, nm, nth) + tuple(part[2:])
-        saved.append((kept1, kept2, kept3))
+        got_far, kvv = tie(got_far, kvv)
+        x_far, n_far = next_norm(far_spans, x_far, kept_far, got_far, layer, 2)
+        t_far = core_swap(n_far)
+        pm, pt, qf, kvf, of, stf = call(
+            lambda *r: section2_far(sz, heads, *r),
+            [
+                far_bf,
+                far_two,
+                shaped((2 * far, edev)),
+                shaped((2 * far, 2 * edev)),
+                shaped((2 * far, edev)),
+                shaped((8, 2 * far), F32),
+            ],
+            [sc],
+            [n_far, t_far, kvv, w2, w3, wo2],
+            name="section2",
+        )
+        x2, n2, t2 = [x_near, x_far], n_near + n_far, t_near + t_far
+        kept_far = pair_sum(pm, pt)
+        got_far = across(kept_far)
+        _, later = tie(kept_far, qv)
+        pm, pt, ov, stv = call(
+            lambda *r: section2_rest(sz, heads, *r),
+            [near_bf, near_two, shaped((2 * vp, edev)), shaped((8, 2 * vp), F32)],
+            [sc],
+            [later, kvn, kvf, on, wo2, wo3],
+            name="section2",
+        )
+        saved2 = (x2, n2, t2, [qn, qf], kvv, [on, of], stn, stf, qv, [kvn, kvf], ov, stv)
+        kept_near = pair_sum(pm, pt)
+        got_near = across(kept_near)
+
+        fetch(layer, 3, kept_far)
+        got_far, fetched[layer, 3], _ = tie(got_far, fetched[layer, 3], kept_near)
+        up, down = fetched[layer, 3]
+
+        def feed_forward(spans, n, t):
+            rows = sum(p.shape[0] for p in n)
+            return call(
+                lambda *r: section3(sz, layer, spans, *r),
+                [shaped((rows, width)), halved(rows)] + [shaped((2 * rows, hid))] * 2,
+                [],
+                [n, t, up, mlp_in_bias, down],
+                name="section3",
+            )
+
+        x_far, n_far = next_norm(far_spans, x_far, kept_far, got_far, layer, 4)
+        t_far = core_swap(n_far)
+        pm, pt, act_far, slope_far = feed_forward(far_spans, n_far, t_far)
+        kept_far = pair_sum(pm, pt)
         if layer + 1 < layers:
-            a, b = shares(pair_sum(part[0], part[1]))
-            b = fetch_beside(layer + 1, 1, a, b)
-            stream, normed = next_norm(stream, a, b, layer + 1, 0, True)
-    last = pair_sum(part[0], part[1])
+            got_far = across(kept_far)
+        got_near, _ = tie(got_near, kept_far)
+        x_near, n_near = next_norm(near_spans, x_near, kept_near, got_near, layer, 4)
+        t_near = core_swap(n_near)
+        pm, pt, act_near, slope_near = feed_forward(near_spans, n_near, t_near)
+        kept_near = pair_sum(pm, pt)
+        if layer + 1 < layers:
+            got_near = across(kept_near)
+            fetch(layer + 1, 1, kept_far)
+        x3, n3, t3 = [x_near, x_far], n_near + n_far, t_near + t_far
+        saved3 = (x3, n3, t3, (act_near, act_far), (slope_near, slope_far))
+        saved.append((saved1, saved2, saved3))
+    stream = jnp.concatenate([x_near, x_far], 0)
+    last = jnp.concatenate([kept_near, kept_far], 0)
     away = lax.ppermute(piece_of(last, 1 - chip), "tensor", cross)
     out = piece_of(stream, chip) + (piece_of(last, chip).astype(F32) + away.astype(F32))
     out_v = (out[0:vq] + mlp_out_bias[layers - 1, 0]).astype(BF16)
@@ -871,6 +1063,10 @@
 
     def whole_sum(rows):
         return lax.psum_scatter(rows, "dp", scatter_dimension=0, tiled=True)
+
+    def shares(mine, theirs):
+        kept = [pair_sum(m, t) for m, t in zip(mine, theirs)]
+        return kept, [across(k) for k in kept]
 
     class Reduction:
         def __init__(self, outs, order):
@@ -974,17 +1170,20 @@
         _, nm, nth, act, slope = kept3
         up, down = fetched[layer, 3]
         pm, pt, dh = call(
-            lambda *r: section3_back(sz, *r),
+            lambda dm, dt, wi, wo, near_part, far_part, *r: section3_back(
+                sz, dm, dt, wi, wo, natural(near_part, far_part), *r
+            ),
             [rows_bf, rows_bf, shaped((2 * half, hid))],
             [],
-            [dm, dt, up, down, slope],
-            flops=mac * hid * 4,
+            [dm, dt, up, down, *slope],
             name="section3_back",
         )
-        a, b = shares(pair_sum(pm, pt))
-        args = window(a, [nm, nth, dm, dt, act, dh])
+        a, b = shares(pm, pt)
+        args = window(a, [nm, nth, dm, dt, *act, dh])
         db, feed = call(
-            lambda *r: section3_weights(sz, *r),
+            lambda sc, nm, nth, dm, dt, near_part, far_part, *r: section3_weights(
+                sz, sc, nm, nth, dm, dt, natural(near_part, far_part), *r
+            ),
             [shaped((2, hid), F32), shaped((width, 4 * hid))],
             [sc],
             args,
@@ -997,7 +1196,7 @@
         grad, dy, sums3 = close(grad, a, b, kept3, layer, 4)
 
         dm, dt = pair(dy)
-        _, nm, nth, qq, kvv, oq, stq, qv, kvq, ov, stv = kept2
+        _, nm, nth, qq, kvv, oq, stn, stf, qv, kvq, ov, stv = kept2
         part = call(
             lambda *r: section2_back(sz, heads, *r),
             [
@@ -1011,13 +1210,12 @@
             [sc],
             [
                 dm, dt, *fetched[layer, 2],
-                qq, kvv, stq, qv, kvq, stv,
+                qq, kvv, stn, stf, qv, kvq, stv,
             ],
-            flops=mac * 4 * edev * 2,
             name="section2_back",
             scratch=[pltpu.VMEM((sz.qlen, edev), BF16), pltpu.VMEM((2 * vp, edev), BF16)],
         )
-        a, b = shares(pair_sum(part[0], part[1]))
+        a, b = shares(part[0], part[1])
         args = window(a, [nm, nth, dm, dt, part[2], part[3], part[4], part[5], oq, ov])
         _, made = weights(
             lambda *r: section2_weights(sz, heads, *r), [], [straight], 8 * edev, args, 2 * edev, "section2_weights"
@@ -1027,7 +1225,7 @@
         grad, dy, sums2 = close(grad, a, b, kept2, layer, 2)
 
         dm, dt = pair(dy)
-        _, nm, nth, nvw, qkvv, ov, stv, qkvq, oq, stq = kept1
+        _, nm, nth, nvw, qkvv, ov, stv, qkvq, oq, stn, stf = kept1
         part = call(
             lambda *r: section1_back(sz, heads, *r),
             [
@@ -1040,13 +1238,12 @@
             [sc],
             [
                 dm, dt, *fetched[layer, 1],
-                Part(bias_all, layer), qkvv, stv, qkvq, stq,
+                Part(bias_all, layer), qkvv, stv, qkvq, stn, stf,
             ],
-            flops=mac * 4 * edev * 2 + 20 * heads * HDIM * sz.qlen * sz.qlen,
             name="section1_back",
             scratch=[pltpu.VMEM((sz.qlen, edev), BF16), pltpu.VMEM((sz.vis, edev), BF16)],
         )
-        a, b = shares(pair_sum(part[0], part[1]))
+        a, b = shares(part[0], part[1])
         args = window(a, [nm, nth, dm, dt, nvw, part[2], part[3], oq, ov])
         _, made = weights(
             lambda *r: section1_weights(sz, heads, *r), [], [straight], 8 * edev, args, 3 * edev, "section1_weights"

time: 546 us -> 535 us (0.980)
  waiting for transfers between devices: 255 us -> 199 us
  Pallas kernels: 142 us -> 158 us
  local copies, waits for them, and re-layouts: 62.4 us -> 76.6 us
  starting transfers between devices: 45.9 us -> 59.1 us
    ppermute x36 -> x77, waiting for transfers between devices: 133 us -> 90.3 us  [the longest x17 54.4 us: across(): return lax.ppermute(x, 'tensor', cross)]
    unnamed x403 -> x607, local copies, waits for them, and re-layouts: 58.5 us -> 73.4 us
    pallas_call x38 -> x65, Pallas kernels: 139 us -> 154 us  [call(): pl.pallas_call(wrapped, out_shape=tuple(flat_outs), in_specs=[smem] * len...]
    ppermute x12, waiting for transfers between devices: 101 us -> 89.7 us  [move(): got = lax.ppermute(self.ready, 'dp', [(i, i ^ bit) for i in range(dp_size)])]
    ppermute x36 -> x77, starting transfers between devices: 23.6 us -> 33.8 us  [the longest x17 19.1 us: across(): return lax.ppermute(x, 'tensor', cross)]
  transfers between devices with their start and end apart: 56 -> 97, of which waited for: 38 -> 47; matrix products, arithmetic and copies ran while one was open for 3% -> 3% of each run, Pallas kernels for 17% -> 24%
where the time goes in v3:
time: 535 us; the launch traced here: 525 us
  waiting for transfers between devices  199 us (37%)
  Pallas kernels  158 us (30%)
  local copies, waits for them, and re-layouts  76.6 us (14%)
  starting transfers between devices  59.1 us (11%)
  between operations  19.3 us (4%)
  other arithmetic  13.8 us (3%)
    pallas_call x65, Pallas kernels, call(): pl.pallas_call(wrapped, out_shape=tuple(flat_outs), in_specs=[smem] * len...  154 us
    ppermute x12, waiting for transfers between devices, move(): got = lax.ppermute(self.ready, 'dp', [(i, i ^ bit) for i in range(dp_size)])  89.7 us
    unnamed x607, local copies, waits for them, and re-layouts  73.4 us
    ppermute x17, waiting for transfers between devices, across(): return lax.ppermute(x, 'tensor', cross)  54.4 us
    ppermute x60, waiting for transfers between devices, core_swap(): return lax.ppermute(x, 'tensor', swap)  35.9 us
    ppermute x17, starting transfers between devices, across(): return lax.ppermute(x, 'tensor', cross)  19.1 us
    ppermute x3, waiting for transfers between devices, summed(): x = x + lax.ppermute(x, axis, [(i, i ^ bit) for i in range(size)])  18.7 us
    ppermute x12, starting transfers between devices, move(): got = lax.ppermute(self.ready, 'dp', [(i, i ^ bit) for i in range(dp_size)])  17.5 us
  transfers between devices with their start and end apart: 97, of which 47 were waited for; matrix products, arithmetic and copies ran while one was open for 3% of the time, Pallas kernels for 24%

profile of v3, /device:TPU:0, one launch (start us, length us, event | category | flops | bytes accessed | tf_op | source)
XLA Modules:
  0.0 525.5 jit_solution(5766369847255573620)
XLA Ops:
  41.9 6.5 %section1.7 = (bf16[240,768]{1,0:T(8,128)(2,1)S(1)}, bf16[128,768]{1,0:T(8,128)(2,1)S(1)}, bf16[112,768]{1,0:T(8,128)(2,1)S(1)}, bf16[144,768]{1,0:T(8,128)(2,1)...) custom-call(s32[8]{0:T(128)S(1)} %stack.21.refs_0_, ...), custom_call_target="tpu_custom_call" | custom-call | flops 1 | bytes 1 | tf_op jit(solution)/shard_map/section1/pallas_call | solution.py:113
  99.2 3.8 collective-permute-done.20.refs_2_
  128.5 5.9 %section1.10 = (bf16[240,768]{1,0:T(8,128)(2,1)S(1)}, bf16[128,768]{1,0:T(8,128)(2,1)S(1)}, bf16[112,768]{1,0:T(8,128)(2,1)S(1)}, bf16[144,768]{1,0:T(8,128)(2,1...) custom-call(s32[8]{0:T(128)S(1)} %stack.22.refs_0_, ...), custom_call_target="tpu_custom_call" | custom-call | flops 1 | bytes 1 | tf_op jit(solution)/shard_map/section1/pallas_call | solution.py:113
  137.7 3.7 section1.11
  168.6 3.9 collective-permute-done.51.refs_2_
  179.2 4.8 collective-permute-done.50.refs_2_
  196.0 4.6 section3_weights.2
  204.7 17.5 %collective-permute-done.63.refs_2_ = bf16[480,768]{1,0:T(8,128)(2,1)S(1)} collective-permute-done((bf16[480,768]{1,0:T(8,128)(2,1)S(1)}, bf16[480,768]{1,0:T(8,128)(2,1)S(1)}, u32[]{:S(2)}, u32[]{:S(2)}) %collective-permute-start.63) | collective-permute-done | bytes 737312 | tf_op jit(solution)/shard_map/ppermute | solution.py:796
  227.2 7.3 %section2_back.2 = (bf16[480,768]{1,0:T(8,128)(2,1)S(1)}, bf16[480,768]{1,0:T(8,128)(2,1)S(1)}, bf16[800,192]{1,0:T(8,128)(2,1)S(1)}, bf16[160,384]{1,0:T(8,128)...) custom-call(s32[8]{0:T(128)S(1)} %stack.22.refs_0_, ...), custom_call_target="tpu_custom_call" | custom-call | flops 1 | bytes 1 | tf_op jit(solution)/shard_map/section2_back/pallas_call | solution.py:113
  241.7 14.0 %collective-permute-done.66.refs_2_ = bf16[480,768]{1,0:T(8,128)(2,1)S(1)} collective-permute-done((bf16[480,768]{1,0:T(8,128)(2,1)S(1)}, bf16[480,768]{1,0:T(8,128)(2,1)S(1)}, u32[]{:S(2)}, u32[]{:S(2)}) %collective-permute-start.66) | collective-permute-done | bytes 737312 | tf_op jit(solution)/shard_map/ppermute | solution.py:796
  259.5 12.6 %section1_back.2 = (bf16[480,768]{1,0:T(8,128)(2,1)S(1)}, bf16[480,768]{1,0:T(8,128)(2,1)S(1)}, bf16[144,576]{1,0:T(8,128)(2,1)S(1)}, bf16[800,576]{1,0:T(8,128)(2,1)S(1)}, bf16[3,144,144]{2,1,0:T(8,128)(2,1)S(1)}) custom-call(s32[8]{0:T(128)S(1)} %stack.22.refs_0_, bf16[480,768]{1,0:T(8,128)(2,1)S(1)} %get-tuple-element.649.refs_1_.refs_9_, ...), custom_call_target="tpu_custom_call" | custom-call | flops 1 | bytes 1 | tf_op jit(solution)/shard_map/section1_back/pallas_call | solution.py:113
  276.5 5.6 %section1_weights.2 = (bf16[4,96,1536]{2,1,0:T(8,128)(2,1)S(1)}, bf16[4,96,1536]{2,1,0:T(8,128)(2,1)}) custom-call(s32[8]{0:T(128)S(1)} %stack.21.refs_0_, bf16[128,768]{1,0:T(8,128)(2,1)S(1)} %copy-done.125, bf16[112,768]{1,0:T(8,128)(2,1)S(1)} %copy-done.167, bf16[128,768]{1,0:T(8,128)(2,1)} %get-tuple-element.643.refs_1_.refs_3_, ...), custom_call_target="tpu_custom_call" | custom-call | flops 1 | bytes 1 | tf_op jit(solution)/shard_map/section1_weights/pallas_call | solution.py:113
  283.2 24.4 %collective-permute-done.70.refs_13_ = bf16[4,96,1536]{2,1,0:T(8,128)(2,1)S(1)} collective-permute-done((bf16[4,96,1536]{2,1,0:T(8,128)(2,1)S(1)}, bf16[4,96,1536]{2,1,0:T(8,128)(2,1)S(1)}, u32[]{:S(2)}, u32[]{:S(2)}) %collective-permute-start.70) | collective-permute-done | bytes 1179680 | tf_op jit(solution)/shard_map/ppermute | solution.py:1084
  322.9 4.6 section3_weights.3
  330.3 6.4 %collective-permute-done.74.refs_14_ = bf16[2,96,1536]{2,1,0:T(8,128)(2,1)} collective-permute-done((bf16[2,96,1536]{2,1,0:T(8,128)(2,1)}, bf16[2,96,1536]{2,1,0:T(8,128)(2,1)}, u32[]{:S(2)}, u32[]{:S(2)}) %collective-permute-start.74) | collective-permute-done | bytes 589856 | tf_op jit(solution)/shard_map/ppermute | solution.py:1084
  336.7 14.1 %collective-permute-done.75.refs_9_ = bf16[4,96,1536]{2,1,0:T(8,128)(2,1)} collective-permute-done((bf16[4,96,1536]{2,1,0:T(8,128)(2,1)}, bf16[4,96,1536]{2,1,0:T(8,128)(2,1)}, u32[]{:S(2)}, u32[]{:S(2)}) %collective-permute-start.75) | collective-permute-done | bytes 1179680 | tf_op jit(solution)/shard_map/ppermute | solution.py:1084
  360.7 7.5 %section2_back.3 = (bf16[480,768]{1,0:T(8,128)(2,1)S(1)}, bf16[480,768]{1,0:T(8,128)(2,1)S(1)}, bf16[800,192]{1,0:T(8,128)(2,1)S(1)}, bf16[160,384]{1,0:T(8,128)...) custom-call(s32[8]{0:T(128)S(1)} %stack.21.refs_0_, ...), custom_call_target="tpu_custom_call" | custom-call | flops 1 | bytes 1 | tf_op jit(solution)/shard_map/section2_back/pallas_call | solution.py:113
  402.2 12.6 %section1_back.3 = (bf16[480,768]{1,0:T(8,128)(2,1)S(1)}, bf16[480,768]{1,0:T(8,128)(2,1)S(1)}, bf16[144,576]{1,0:T(8,128)(2,1)S(1)}, bf16[800,576]{1,0:T(8,128)(2,1)S(1)}, bf16[3,144,144]{2,1,0:T(8,128)(2,1)S(1)}) custom-call(s32[8]{0:T(128)S(1)} %stack.21.refs_0_, bf16[480,768]{1,0:T(8,128)(2,1)S(1)} %get-tuple-element.750.refs_1_.refs_9_, ...), custom_call_target="tpu_custom_call" | custom-call | flops 1 | bytes 1 | tf_op jit(solution)/shard_map/section1_back/pallas_call | solution.py:113
  419.2 4.3 section1_weights.3
  423.5 11.3 %collective-permute-done.83.refs_5_ = bf16[4,96,1536]{2,1,0:T(8,128)(2,1)S(1)} collective-permute-done((bf16[4,96,1536]{2,1,0:T(8,128)(2,1)S(1)}, bf16[4,96,1536]{2,1,0:T(8,128)(2,1)S(1)}, u32[]{:S(2)}, u32[]{:S(2)}) %collective-permute-start.83) | collective-permute-done | bytes 1179680 | tf_op jit(solution)/shard_map/ppermute | solution.py:1084
  444.8 17.1 %collective-permute-done.91.refs_6_ = bf16[2,96,1536]{2,1,0:T(8,128)(2,1)S(1)} collective-permute-done((bf16[2,96,1536]{2,1,0:T(8,128)(2,1)S(1)}, bf16[2,96,1536]{2,1,0:T(8,128)(2,1)S(1)}, u32[]{:S(2)}, u32[]{:S(2)}) %collective-permute-start.91) | collective-permute-done | bytes 589856 | tf_op jit(solution)/shard_map/ppermute | solution.py:1084
  474.0 14.3 %collective-permute-done.89.refs_2_ = bf16[2,96,1536]{2,1,0:T(8,128)(2,1)S(1)} collective-permute-done((bf16[2,96,1536]{2,1,0:T(8,128)(2,1)S(1)}, bf16[2,96,1536]{2,1,0:T(8,128)(2,1)S(1)}, u32[]{:S(2)}, u32[]{:S(2)}) %collective-permute-start.89) | collective-permute-done | bytes 589856 | tf_op jit(solution)/shard_map/ppermute | solution.py:1084
  493.0 15.6 %collective-permute-done.87 = f32[40,768]{1,0:T(8,128)S(1)} collective-permute-done((f32[40,768]{1,0:T(8,128)S(1)}, f32[40,768]{1,0:T(8,128)S(1)}, u32[]{:S(2)}, u32[]{:S(2)}) %collective-permute-start.87) | collective-permute-done | bytes 122912 | tf_op jit(solution)/shard_map/ppermute | solution.py:1268
  510.1 4.3 finish_attn.1
  (901 shorter events, 279.4 us)
Async XLA Ops:
  7.2 507.3 %reduce-scatter.5.cloned.1.call-start = ((), (), s32[]{:S(2)}) async-start(), calls=%async_computation.3 | async-start | bytes 5308416 | tf_op jit(solution)/shard_map/reduce_scatter | solution.py:1065
  51.0 17.6 %collective-permute-start.8 = (bf16[240,768]{1,0:T(8,128)(2,1)S(1)}, bf16[240,768]{1,0:T(8,128)(2,1)S(1)}, u32[]{:S(2)}, u32[]{:S(2)}) collective-permute-start(bf16[240,768]{1,0:T(8,128)(2,1)S(1)} %pair_sum.12.refs_1_), channel_id=1, source_target_pairs={{0,2},{1,3},{2,0},{3,1},{4,6},{5,7},{6,4},{7,5},{8,10},{9,11},{10,... | collective-permute-start | bytes 1105928 | tf_op jit(solution)/shard_map/ppermute | solution.py:796
  167.4 21.9 %collective-permute-start.61 = (bf16[480,768]{1,0:T(8,128)(2,1)S(1)}, bf16[480,768]{1,0:T(8,128)(2,1)S(1)}, u32[]{:S(2)}, u32[]{:S(2)}) collective-permute-start(bf16[480,768]{1,0:T(8,128)(2,1)S(1)} %copy-done.69), channel_id=1, source_target_pairs={{0,1},{1,0},{2,3},{3,2},{4,5},{5,4},{6,7},{7,6},{8,9},{9,8},{10,11... | collective-permute-start | bytes 2211848 | tf_op jit(solution)/shard_map/ppermute | solution.py:793
  203.3 311.2 %reduce-scatter.3.cloned.1.call-start = ((), (), s32[]{:S(2)}) async-start(), calls=%async_computation.2 | async-start | bytes 5308416 | tf_op jit(solution)/shard_map/reduce_scatter | solution.py:1065
  203.5 18.7 %collective-permute-start.63 = (bf16[480,768]{1,0:T(8,128)(2,1)S(1)}, bf16[480,768]{1,0:T(8,128)(2,1)S(1)}, u32[]{:S(2)}, u32[]{:S(2)}) collective-permute-start(bf16[480,768]{1,0:T(8,128)(2,1)S(1)} %add_convert_fusion.5.refs_1_), channel_id=1, source_target_pairs={{0,2},{1,3},{2,0},{3,1},{4,6},{5,7},{6,4},{7,5},{8,10},{9,11},{10,... | collective-permute-start | bytes 2211848 | tf_op jit(solution)/shard_map/ppermute | solution.py:796
  237.1 18.6 %collective-permute-start.66 = (bf16[480,768]{1,0:T(8,128)(2,1)S(1)}, bf16[480,768]{1,0:T(8,128)(2,1)S(1)}, u32[]{:S(2)}, u32[]{:S(2)}) collective-permute-start(bf16[480,768]{1,0:T(8,128)(2,1)S(1)} %add_convert_fusion.4.refs_1_), channel_id=1, source_target_pairs={{0,2},{1,3},{2,0},{3,1},{4,6},{5,7},{6,4},{7,5},{8,10},{9,11},{10,... | collective-permute-start | bytes 2211848 | tf_op jit(solution)/shard_map/ppermute | solution.py:796
  273.0 34.6 %collective-permute-start.70 = (bf16[4,96,1536]{2,1,0:T(8,128)(2,1)S(1)}, bf16[4,96,1536]{2,1,0:T(8,128)(2,1)S(1)}, u32[]{:S(2)}, u32[]{:S(2)}) collective-permute-start(bf16[4,96,1536]{2,1,0:T(8,128)(2,1)S(1)} %get-tuple-element.659), channel_id=1, source_target_pairs={{0,4},{4,0},{8,12},{12,8},{16,20},{20,16},{24,28},{28,24},{1,5},{5... | collective-permute-start | bytes 3538952 | tf_op jit(solution)/shard_map/ppermute | solution.py:1084
  275.3 32.3 %collective-permute-start.69 = (bf16[480,768]{1,0:T(8,128)(2,1)S(1)}, bf16[480,768]{1,0:T(8,128)(2,1)S(1)}, u32[]{:S(2)}, u32[]{:S(2)}) collective-permute-start(bf16[480,768]{1,0:T(8,128)(2,1)S(1)} %add_convert_fusion.3.refs_1_), channel_id=1, source_target_pairs={{0,2},{1,3},{2,0},{3,1},{4,6},{5,7},{6,4},{7,5},{8,10},{9,11},{10,... | collective-permute-start | bytes 2211848 | tf_op jit(solution)/shard_map/ppermute | solution.py:796
  316.0 34.8 %collective-permute-start.75 = (bf16[4,96,1536]{2,1,0:T(8,128)(2,1)}, bf16[4,96,1536]{2,1,0:T(8,128)(2,1)}, u32[]{:S(2)}, u32[]{:S(2)}) collective-permute-start(bf16[4,96,1536]{2,1,0:T(8,128)(2,1)} %get-tuple-element.688), channel_id=1, source_target_pairs={{0,4},{4,0},{8,12},{12,8},{16,20},{20,16},{24,28},{28,24},{1,5},{5... | collective-permute-start | bytes 3538952 | tf_op jit(solution)/shard_map/ppermute | solution.py:1084
  319.1 31.6 %collective-permute-start.73 = (bf16[480,768]{1,0:T(8,128)(2,1)}, bf16[480,768]{1,0:T(8,128)(2,1)}, u32[]{:S(2)}, u32[]{:S(2)}) collective-permute-start(bf16[480,768]{1,0:T(8,128)(2,1)} %add_convert_fusion.2.refs_1_), channel_id=1, source_target_pairs={{0,2},{1,3},{2,0},{3,1},{4,6},{5,7},{6,4},{7,5},{8,10},{9,11},{10,... | collective-permute-start | bytes 2211848 | tf_op jit(solution)/shard_map/ppermute | solution.py:796
  371.7 24.2 %collective-permute-start.78 = (bf16[480,768]{1,0:T(8,128)(2,1)}, bf16[480,768]{1,0:T(8,128)(2,1)}, u32[]{:S(2)}, u32[]{:S(2)}) collective-permute-start(bf16[480,768]{1,0:T(8,128)(2,1)} %add_convert_fusion.1.refs_1_), channel_id=1, source_target_pairs={{0,2},{1,3},{2,0},{3,1},{4,6},{5,7},{6,4},{7,5},{8,10},{9,11},{10,... | collective-permute-start | bytes 2211848 | tf_op jit(solution)/shard_map/ppermute | solution.py:796
  374.6 21.3 %collective-permute-start.79 = (bf16[2,96,1536]{2,1,0:T(8,128)(2,1)}, bf16[2,96,1536]{2,1,0:T(8,128)(2,1)}, u32[]{:S(2)}, u32[]{:S(2)}) collective-permute-start(bf16[2,96,1536]{2,1,0:T(8,128)(2,1)} %add_convert_fusion.8), channel_id=1, source_target_pairs={{0,8},{4,12},{8,0},{12,4},{16,24},{20,28},{24,16},{28,20},{1,9},{5... | collective-permute-start | bytes 1769480 | tf_op jit(solution)/shard_map/ppermute | solution.py:1084
  399.2 15.7 %collective-permute-start.60 = (bf16[240,768]{1,0:T(8,128)(2,1)S(1)}, bf16[240,768]{1,0:T(8,128)(2,1)S(1)}, u32[]{:S(2)}, u32[]{:S(2)}) collective-permute-start(bf16[240,768]{1,0:T(8,128)(2,1)S(1)} %pad_maximum_fusion.3), channel_id=1, source_target_pairs={{0,2},{1,3},{2,0},{3,1},{4,6},{5,7},{6,4},{7,5},{8,10},{9,11},{10,... | collective-permute-start | bytes 1105928 | tf_op jit(solution)/shard_map/ppermute | solution.py:1057
  400.5 34.3 %collective-permute-start.83 = (bf16[4,96,1536]{2,1,0:T(8,128)(2,1)S(1)}, bf16[4,96,1536]{2,1,0:T(8,128)(2,1)S(1)}, u32[]{:S(2)}, u32[]{:S(2)}) collective-permute-start(bf16[4,96,1536]{2,1,0:T(8,128)(2,1)S(1)} %get-tuple-element.760), channel_id=1, source_target_pairs={{0,4},{4,0},{8,12},{12,8},{16,20},{20,16},{24,28},{28,24},{1,5},{5... | collective-permute-start | bytes 3538952 | tf_op jit(solution)/shard_map/ppermute | solution.py:1084
  435.0 26.9 %collective-permute-start.91 = (bf16[2,96,1536]{2,1,0:T(8,128)(2,1)S(1)}, bf16[2,96,1536]{2,1,0:T(8,128)(2,1)S(1)}, u32[]{:S(2)}, u32[]{:S(2)}) collective-permute-start(bf16[2,96,1536]{2,1,0:T(8,128)(2,1)S(1)} %add_convert_fusion.6), channel_id=1, source_target_pairs={{0,8},{4,12},{8,0},{12,4},{16,24},{20,28},{24,16},{28,20},{1,9},{5... | collective-permute-start | bytes 1769480 | tf_op jit(solution)/shard_map/ppermute | solution.py:1084
  436.5 73.6 %collective-permute-start.94 = (bf16[1,96,1536]{2,1,0:T(8,128)(2,1)S(1)}, bf16[1,96,1536]{2,1,0:T(8,128)(2,1)S(1)}, u32[]{:S(2)}, u32[]{:S(2)}) collective-permute-start(bf16[1,96,1536]{2,1,0:T(8,128)(2,1)S(1)} %add_convert_fusion.10), channel_id=1, source_target_pairs={{0,16},{4,20},{8,24},{12,28},{16,0},{20,4},{24,8},{28,12},{1,17},{... | collective-permute-start | bytes 884744 | tf_op jit(solution)/shard_map/ppermute | solution.py:1084
  439.2 22.9 %collective-permute-start.82 = (bf16[480,768]{1,0:T(8,128)(2,1)S(1)}, bf16[480,768]{1,0:T(8,128)(2,1)S(1)}, u32[]{:S(2)}, u32[]{:S(2)}) collective-permute-start(bf16[480,768]{1,0:T(8,128)(2,1)S(1)} %add_convert_fusion.refs_1_), channel_id=1, source_target_pairs={{0,2},{1,3},{2,0},{3,1},{4,6},{5,7},{6,4},{7,5},{8,10},{9,11},{10,... | collective-permute-start | bytes 2211848 | tf_op jit(solution)/shard_map/ppermute | solution.py:796
  440.3 26.3 %collective-permute-start.88 = (bf16[4,96,1536]{2,1,0:T(8,128)(2,1)S(1)}, bf16[4,96,1536]{2,1,0:T(8,128)(2,1)S(1)}, u32[]{:S(2)}, u32[]{:S(2)}) collective-permute-start(bf16[4,96,1536]{2,1,0:T(8,128)(2,1)S(1)} %get-tuple-element.779), channel_id=1, source_target_pairs={{0,4},{4,0},{8,12},{12,8},{16,20},{20,16},{24,28},{28,24},{1,5},{5... | collective-permute-start | bytes 3538952 | tf_op jit(solution)/shard_map/ppermute | solution.py:1084
  443.1 67.0 %collective-permute-start.93 = (bf16[1,96,1536]{2,1,0:T(8,128)(2,1)S(1)}, bf16[1,96,1536]{2,1,0:T(8,128)(2,1)S(1)}, u32[]{:S(2)}, u32[]{:S(2)}) collective-permute-start(bf16[1,96,1536]{2,1,0:T(8,128)(2,1)S(1)} %add_convert_fusion.11), channel_id=1, source_target_pairs={{0,16},{4,20},{8,24},{12,28},{16,0},{20,4},{24,8},{28,12},{1,17},{... | collective-permute-start | bytes 884744 | tf_op jit(solution)/shard_map/ppermute | solution.py:1084
  462.0 48.1 %collective-permute-start.92 = (bf16[1,96,1536]{2,1,0:T(8,128)(2,1)S(1)}, bf16[1,96,1536]{2,1,0:T(8,128)(2,1)S(1)}, u32[]{:S(2)}, u32[]{:S(2)}) collective-permute-start(bf16[1,96,1536]{2,1,0:T(8,128)(2,1)S(1)} %add_convert_fusion.12), channel_id=1, source_target_pairs={{0,16},{4,20},{8,24},{12,28},{16,0},{20,4},{24,8},{28,12},{1,17},{... | collective-permute-start | bytes 884744 | tf_op jit(solution)/shard_map/ppermute | solution.py:1084
  466.7 21.6 %collective-permute-start.89 = (bf16[2,96,1536]{2,1,0:T(8,128)(2,1)S(1)}, bf16[2,96,1536]{2,1,0:T(8,128)(2,1)S(1)}, u32[]{:S(2)}, u32[]{:S(2)}) collective-permute-start(bf16[2,96,1536]{2,1,0:T(8,128)(2,1)S(1)} %add_convert_fusion.7), channel_id=1, source_target_pairs={{0,8},{4,12},{8,0},{12,4},{16,24},{20,28},{24,16},{28,20},{1,9},{5... | collective-permute-start | bytes 1769480 | tf_op jit(solution)/shard_map/ppermute | solution.py:1084
  473.3 18.7 %collective-permute-start.86 = (f32[40,768]{1,0:T(8,128)S(1)}, f32[40,768]{1,0:T(8,128)S(1)}, u32[]{:S(2)}, u32[]{:S(2)}) collective-permute-start(f32[40,768]{1,0:T(8,128)S(1)} %add.125), channel_id=1, source_target_pairs={{0,8},{4,12},{8,0},{12,4},{16,24},{20,28},{24,16},{28,20},{1,9},{5... | collective-permute-start | bytes 368648 | tf_op jit(solution)/shard_map/ppermute | solution.py:1268
  488.4 21.7 %collective-permute-start.90 = (bf16[1,96,1536]{2,1,0:T(8,128)(2,1)S(1)}, bf16[1,96,1536]{2,1,0:T(8,128)(2,1)S(1)}, u32[]{:S(2)}, u32[]{:S(2)}) collective-permute-start(bf16[1,96,1536]{2,1,0:T(8,128)(2,1)S(1)} %add_convert_fusion.13), channel_id=1, source_target_pairs={{0,16},{4,20},{8,24},{12,28},{16,0},{20,4},{24,8},{28,12},{1,17},{... | collective-permute-start | bytes 884744 | tf_op jit(solution)/shard_map/ppermute | solution.py:1084
  492.1 16.6 %collective-permute-start.87 = (f32[40,768]{1,0:T(8,128)S(1)}, f32[40,768]{1,0:T(8,128)S(1)}, u32[]{:S(2)}, u32[]{:S(2)}) collective-permute-start(f32[40,768]{1,0:T(8,128)S(1)} %add.126), channel_id=1, source_target_pairs={{0,16},{4,20},{8,24},{12,28},{16,0},{20,4},{24,8},{28,12},{1,17},{... | collective-permute-start | bytes 368648 | tf_op jit(solution)/shard_map/ppermute | solution.py:1268
  (375 other events, 2046.8 us)
Sparse Core Ops, SparseCore 0:
  202.8 101.0 reduce-scatter.4
  329.8 104.3 reduce-scatter.2

commit v4 on v3

--- a/solution.py
+++ b/solution.py
@@ -869,8 +869,10 @@
             blocks = [(0, (layer, first)), (0, (layer, first + 1)), (1, (layer, first)), (1, (layer, first + 1))]
         arrays = tie(after, arrays)[1]
         outs = [shaped(arrays[k].shape[len(lead) :]) for k, lead in blocks]
+        marked = outs + [shaped((8, 128), F32)]
 
         def body(one, two, *refs):
+            refs[len(outs)][...] = jnp.zeros((8, 128), F32)
             copies = [
                 pltpu.make_async_copy((one, two)[k].at[lead], refs[j], refs[-1].at[j])
                 for j, (k, lead) in enumerate(blocks)
@@ -880,30 +882,44 @@
             for copy in copies:
                 copy.wait()
 
-        fetched[layer, section] = pl.pallas_call(
+        *fetched[layer, section], mark = pl.pallas_call(
             body,
-            out_shape=outs,
+            out_shape=marked,
             in_specs=[pl.BlockSpec(memory_space=pltpu.HBM)] * 2,
-            out_specs=[pl.BlockSpec(memory_space=pltpu.VMEM)] * len(outs),
+            out_specs=[pl.BlockSpec(memory_space=pltpu.VMEM)] * len(marked),
             scratch_shapes=[pltpu.SemaphoreType.DMA((len(outs),))],
             compiler_params=pltpu.CompilerParams(vmem_limit_bytes=VMEM_LIMIT),
             name="fetch",
         )(*arrays)
+        return mark
 
     def fetch_beside(layer, section, a, b):
         fetch(layer, section, a)
         b, fetched[layer, section] = tie(b, fetched[layer, section])
         return b
 
-    fetch(0, 1, own)
-    other, fetched[0, 1] = tie(other, fetched[0, 1])
-    (x_near, x_far), pieces = call(
-        lambda *r: open_stream(sz, *r),
-        [[shaped((sz.near, width), F32), shaped((far, width), F32)], near_two + far_two],
-        scal[0:1],
-        [own, other, scale, shift],
+    mark = fetch(0, 1, own)
+    sent_grad = rounded_grad.astype(BF16)
+    opening, bias_all, spread = tie(scal[0], bias_all, spread)
+
+    def open_body(sc, own, other, scale, shift, mark, *refs):
+        open_stream(sz, sc, own, other, scale, shift, *refs[:-1])
+        refs[-1][...] = jnp.zeros(refs[-1].shape, F32)
+
+    (x_near, x_far), pieces, token = call(
+        open_body,
+        [
+            [shaped((sz.near, width), F32), shaped((far, width), F32)],
+            near_two + far_two,
+            shaped((8, 128), F32),
+        ],
+        [opening],
+        [own, other, scale, shift, mark],
         name="open_stream",
     )
+    sent_grad, token = tie(sent_grad, token)
+    other_grad = across(sent_grad)
+    near_sc, other_grad = tie(scal[0], other_grad)
     n_near, n_far = pieces[0:2], pieces[2:4]
 
     saved = []
@@ -916,17 +932,18 @@
             w0, w1, wo0, wo1 = fetched[layer, 1]
             x_far, n_far = next_norm(far_spans, x_far, kept_far, got_far, layer, 0, True)
         t_far = core_swap(n_far)
+        first = [token] if layer == 0 else []
         (qkvf,) = call(
-            lambda *r: section1_far(sz, *r), [shaped((2 * far, 3 * edev))], [sc], [n_far, t_far, w1], name="section1"
+            lambda sc, nm, nth, w1, *r: section1_far(sz, sc, nm, nth, w1, r[-1]),
+            [shaped((2 * far, 3 * edev))],
+            [sc],
+            [n_far, t_far, w1] + first,
+            name="section1",
         )
         if layer > 0:
             got_near, qkvf = tie(got_near, qkvf)
             x_near, n_near = next_norm(near_spans, x_near, kept_near, got_near, layer, 0, True)
         t_near = core_swap(n_near)
-        if layer == 0:
-            sent_grad, _ = tie(rounded_grad.astype(BF16), t_far)
-            other_grad = across(sent_grad)
-            other_grad, qkvf = tie(other_grad, qkvf)
         x1, n1, t1 = [x_near, x_far], n_near + n_far, t_near + t_far
         pm, pt, nvw, qkvv, ov, stv, qkvn, on, stn = call(
             lambda *r: section1_near(sz, heads, *r),
@@ -952,7 +969,7 @@
         pm, pt, of, stf = call(
             lambda *r: section1_rest(sz, heads, *r),
             [far_bf, far_two, shaped((2 * far, edev)), shaped((8, 2 * far), F32)],
-            [sc],
+            [sc if layer else near_sc],
             [later, qkvf, wo1],
             name="section1",
         )

time: 535 us -> 522 us (0.976)
  local copies, waits for them, and re-layouts: 76.6 us -> 63 us
  waiting for transfers between devices: 199 us -> 207 us
    unnamed x607 -> x641, local copies, waits for them, and re-layouts: 73.4 us -> 59.9 us
  transfers between devices with their start and end apart: 97 -> 97, of which waited for: 47 -> 48; matrix products, arithmetic and copies ran while one was open for 3% -> 3% of each run, Pallas kernels for 24% -> 26%
where the time goes in v4:
time: 522 us; the launch traced here: 513 us
  waiting for transfers between devices  207 us (40%)
  Pallas kernels  157 us (30%)
  local copies, waits for them, and re-layouts  63 us (12%)
  starting transfers between devices  56.2 us (11%)
  between operations  19.8 us (4%)
  other arithmetic  10.1 us (2%)
    pallas_call x65, Pallas kernels, call(): pl.pallas_call(wrapped, out_shape=tuple(flat_outs), in_specs=[smem] * len...  150 us
    ppermute x12, waiting for transfers between devices, move(): got = lax.ppermute(self.ready, 'dp', [(i, i ^ bit) for i in range(dp_size)])  93.4 us
    unnamed x641, local copies, waits for them, and re-layouts  59.9 us
    ppermute x17, waiting for transfers between devices, across(): return lax.ppermute(x, 'tensor', cross)  57.9 us
    ppermute x60, waiting for transfers between devices, core_swap(): return lax.ppermute(x, 'tensor', swap)  36.6 us
    ppermute x3, waiting for transfers between devices, summed(): x = x + lax.ppermute(x, axis, [(i, i ^ bit) for i in range(size)])  18.6 us
    ppermute x17, starting transfers between devices, across(): return lax.ppermute(x, 'tensor', cross)  16.9 us
    ppermute x12, starting transfers between devices, move(): got = lax.ppermute(self.ready, 'dp', [(i, i ^ bit) for i in range(dp_size)])  15.6 us
  transfers between devices with their start and end apart: 97, of which 48 were waited for; matrix products, arithmetic and copies ran while one was open for 3% of the time, Pallas kernels for 26%

profile of v4, /device:TPU:0, one launch (start us, length us, event | category | flops | bytes accessed | tf_op | source)
XLA Modules:
  0.0 512.6 jit_solution(17492584942591288149)
XLA Ops:
  29.9 5.8 %section1.7 = (bf16[240,768]{1,0:T(8,128)(2,1)S(1)}, bf16[128,768]{1,0:T(8,128)(2,1)S(1)}, bf16[112,768]{1,0:T(8,128)(2,1)S(1)}, bf16[144,768]{1,0:T(8,128)(2,1)...) custom-call(s32[8]{0:T(128)S(1)} %stack.21.refs_0_, ...), custom_call_target="tpu_custom_call" | custom-call | flops 1 | bytes 1 | tf_op jit(solution)/shard_map/section1/pallas_call | solution.py:113
  40.7 3.7 section1.8
  81.8 5.5 %collective-permute-done.20.refs_2_ = bf16[240,768]{1,0:T(8,128)(2,1)S(1)} collective-permute-done((bf16[240,768]{1,0:T(8,128)(2,1)S(1)}, bf16[240,768]{1,0:T(8,128)(2,1)S(1)}, u32[]{:S(2)}, u32[]{:S(2)}) %collective-permute-start.20) | collective-permute-done | bytes 368672 | tf_op jit(solution)/shard_map/ppermute | solution.py:796
  113.4 5.9 %section1.10 = (bf16[240,768]{1,0:T(8,128)(2,1)S(1)}, bf16[128,768]{1,0:T(8,128)(2,1)S(1)}, bf16[112,768]{1,0:T(8,128)(2,1)S(1)}, bf16[144,768]{1,0:T(8,128)(2,1...) custom-call(s32[8]{0:T(128)S(1)} %stack.22.refs_0_, ...), custom_call_target="tpu_custom_call" | custom-call | flops 1 | bytes 1 | tf_op jit(solution)/shard_map/section1/pallas_call | solution.py:113
  123.6 3.7 section1.11
  155.0 4.3 collective-permute-done.51.refs_2_
  165.2 5.6 %collective-permute-done.50.refs_2_ = bf16[240,768]{1,0:T(8,128)(2,1)S(1)} collective-permute-done((bf16[240,768]{1,0:T(8,128)(2,1)S(1)}, bf16[240,768]{1,0:T(8,128)(2,1)S(1)}, u32[]{:S(2)}, u32[]{:S(2)}) %collective-permute-start.50) | collective-permute-done | bytes 368672 | tf_op jit(solution)/shard_map/ppermute | solution.py:796
  182.7 4.6 section3_weights.2
  191.4 17.6 %collective-permute-done.63.refs_2_ = bf16[480,768]{1,0:T(8,128)(2,1)S(1)} collective-permute-done((bf16[480,768]{1,0:T(8,128)(2,1)S(1)}, bf16[480,768]{1,0:T(8,128)(2,1)S(1)}, u32[]{:S(2)}, u32[]{:S(2)}) %collective-permute-start.63) | collective-permute-done | bytes 737312 | tf_op jit(solution)/shard_map/ppermute | solution.py:796
  215.3 7.3 %section2_back.2 = (bf16[480,768]{1,0:T(8,128)(2,1)S(1)}, bf16[480,768]{1,0:T(8,128)(2,1)S(1)}, bf16[800,192]{1,0:T(8,128)(2,1)S(1)}, bf16[160,384]{1,0:T(8,128)...) custom-call(s32[8]{0:T(128)S(1)} %stack.22.refs_0_, ...), custom_call_target="tpu_custom_call" | custom-call | flops 1 | bytes 1 | tf_op jit(solution)/shard_map/section2_back/pallas_call | solution.py:113
  229.6 14.2 %collective-permute-done.66.refs_2_ = bf16[480,768]{1,0:T(8,128)(2,1)S(1)} collective-permute-done((bf16[480,768]{1,0:T(8,128)(2,1)S(1)}, bf16[480,768]{1,0:T(8,128)(2,1)S(1)}, u32[]{:S(2)}, u32[]{:S(2)}) %collective-permute-start.66) | collective-permute-done | bytes 737312 | tf_op jit(solution)/shard_map/ppermute | solution.py:796
  247.5 12.5 %section1_back.2 = (bf16[480,768]{1,0:T(8,128)(2,1)S(1)}, bf16[480,768]{1,0:T(8,128)(2,1)S(1)}, bf16[144,576]{1,0:T(8,128)(2,1)S(1)}, bf16[800,576]{1,0:T(8,128)(2,1)S(1)}, bf16[3,144,144]{2,1,0:T(8,128)(2,1)S(1)}) custom-call(s32[8]{0:T(128)S(1)} %stack.22.refs_0_, bf16[480,768]{1,0:T(8,128)(2,1)S(1)} %get-tuple-element.651.refs_1_.refs_9_, ...), custom_call_target="tpu_custom_call" | custom-call | flops 1 | bytes 1 | tf_op jit(solution)/shard_map/section1_back/pallas_call | solution.py:113
  263.7 5.6 %section1_weights.2 = (bf16[4,96,1536]{2,1,0:T(8,128)(2,1)S(1)}, bf16[4,96,1536]{2,1,0:T(8,128)(2,1)}) custom-call(s32[8]{0:T(128)S(1)} %stack.21.refs_0_, bf16[128,768]{1,0:T(8,128)(2,1)S(1)} %copy-done.133, bf16[112,768]{1,0:T(8,128)(2,1)S(1)} %copy-done.177, bf16[128,768]{1,0:T(8,128)(2,1)} %get-tuple-element.645.refs_1_.refs_3_, ...), custom_call_target="tpu_custom_call" | custom-call | flops 1 | bytes 1 | tf_op jit(solution)/shard_map/section1_weights/pallas_call | solution.py:113
  270.4 24.5 %collective-permute-done.70.refs_13_ = bf16[4,96,1536]{2,1,0:T(8,128)(2,1)S(1)} collective-permute-done((bf16[4,96,1536]{2,1,0:T(8,128)(2,1)S(1)}, bf16[4,96,1536]{2,1,0:T(8,128)(2,1)S(1)}, u32[]{:S(2)}, u32[]{:S(2)}) %collective-permute-start.70) | collective-permute-done | bytes 1179680 | tf_op jit(solution)/shard_map/ppermute | solution.py:1101
  308.3 4.6 section3_weights.3
  315.1 6.8 %collective-permute-done.74.refs_14_ = bf16[2,96,1536]{2,1,0:T(8,128)(2,1)S(1)} collective-permute-done((bf16[2,96,1536]{2,1,0:T(8,128)(2,1)}, bf16[2,96,1536]{2,1,0:T(8,128)(2,1)S(1)}, u32[]{:S(2)}, u32[]{:S(2)}) %collective-permute-start.74) | collective-permute-done | bytes 589856 | tf_op jit(solution)/shard_map/ppermute | solution.py:1101
  321.9 15.2 %collective-permute-done.75.refs_9_ = bf16[4,96,1536]{2,1,0:T(8,128)(2,1)} collective-permute-done((bf16[4,96,1536]{2,1,0:T(8,128)(2,1)}, bf16[4,96,1536]{2,1,0:T(8,128)(2,1)}, u32[]{:S(2)}, u32[]{:S(2)}) %collective-permute-start.75) | collective-permute-done | bytes 1179680 | tf_op jit(solution)/shard_map/ppermute | solution.py:1101
  348.6 7.5 %section2_back.3 = (bf16[480,768]{1,0:T(8,128)(2,1)S(1)}, bf16[480,768]{1,0:T(8,128)(2,1)S(1)}, bf16[800,192]{1,0:T(8,128)(2,1)S(1)}, bf16[160,384]{1,0:T(8,128)...) custom-call(s32[8]{0:T(128)S(1)} %stack.21.refs_0_, ...), custom_call_target="tpu_custom_call" | custom-call | flops 1 | bytes 1 | tf_op jit(solution)/shard_map/section2_back/pallas_call | solution.py:113
  389.6 12.5 %section1_back.3 = (bf16[480,768]{1,0:T(8,128)(2,1)S(1)}, bf16[480,768]{1,0:T(8,128)(2,1)S(1)}, bf16[144,576]{1,0:T(8,128)(2,1)S(1)}, bf16[800,576]{1,0:T(8,128)(2,1)S(1)}, bf16[3,144,144]{2,1,0:T(8,128)(2,1)S(1)}) custom-call(s32[8]{0:T(128)S(1)} %stack.21.refs_0_, bf16[480,768]{1,0:T(8,128)(2,1)S(1)} %get-tuple-element.752.refs_1_.refs_9_, ...), custom_call_target="tpu_custom_call" | custom-call | flops 1 | bytes 1 | tf_op jit(solution)/shard_map/section1_back/pallas_call | solution.py:113
  410.4 12.1 %collective-permute-done.83.refs_5_ = bf16[4,96,1536]{2,1,0:T(8,128)(2,1)S(1)} collective-permute-done((bf16[4,96,1536]{2,1,0:T(8,128)(2,1)S(1)}, bf16[4,96,1536]{2,1,0:T(8,128)(2,1)S(1)}, u32[]{:S(2)}, u32[]{:S(2)}) %collective-permute-start.83) | collective-permute-done | bytes 1179680 | tf_op jit(solution)/shard_map/ppermute | solution.py:1101
  431.4 18.8 %collective-permute-done.91.refs_6_ = bf16[2,96,1536]{2,1,0:T(8,128)(2,1)S(1)} collective-permute-done((bf16[2,96,1536]{2,1,0:T(8,128)(2,1)S(1)}, bf16[2,96,1536]{2,1,0:T(8,128)(2,1)S(1)}, u32[]{:S(2)}, u32[]{:S(2)}) %collective-permute-start.91) | collective-permute-done | bytes 589856 | tf_op jit(solution)/shard_map/ppermute | solution.py:1101
  460.8 15.3 %collective-permute-done.89.refs_2_ = bf16[2,96,1536]{2,1,0:T(8,128)(2,1)S(1)} collective-permute-done((bf16[2,96,1536]{2,1,0:T(8,128)(2,1)S(1)}, bf16[2,96,1536]{2,1,0:T(8,128)(2,1)S(1)}, u32[]{:S(2)}, u32[]{:S(2)}) %collective-permute-start.89) | collective-permute-done | bytes 589856 | tf_op jit(solution)/shard_map/ppermute | solution.py:1101
  480.2 15.5 %collective-permute-done.87 = f32[40,768]{1,0:T(8,128)S(1)} collective-permute-done((f32[40,768]{1,0:T(8,128)S(1)}, f32[40,768]{1,0:T(8,128)S(1)}, u32[]{:S(2)}, u32[]{:S(2)}) %collective-permute-start.87) | collective-permute-done | bytes 122912 | tf_op jit(solution)/shard_map/ppermute | solution.py:1285
  497.2 4.4 finish_attn.1
  (935 shorter events, 259.3 us)
Async XLA Ops:
  7.2 494.4 %reduce-scatter.5.cloned.1.call-start = ((), (), s32[]{:S(2)}) async-start(), calls=%async_computation.3 | async-start | bytes 5308416 | tf_op jit(solution)/shard_map/reduce_scatter | solution.py:1082
  24.7 16.0 %collective-permute-start.8 = (bf16[240,768]{1,0:T(8,128)(2,1)S(1)}, bf16[240,768]{1,0:T(8,128)(2,1)S(1)}, u32[]{:S(2)}, u32[]{:S(2)}) collective-permute-start(bf16[240,768]{1,0:T(8,128)(2,1)S(1)} %reduce-precision_convert_fusion.refs_1_), channel_id=1, source_target_pairs={{0,2},{1,3},{2,0},{3,1},{4,6},{5,7},{6,4},{7,5},{8,10},{9,11},{10,... | collective-permute-start | bytes 1105928 | tf_op jit(solution)/shard_map/ppermute | solution.py:796
  153.4 22.5 %collective-permute-start.61 = (bf16[480,768]{1,0:T(8,128)(2,1)S(1)}, bf16[480,768]{1,0:T(8,128)(2,1)S(1)}, u32[]{:S(2)}, u32[]{:S(2)}) collective-permute-start(bf16[480,768]{1,0:T(8,128)(2,1)S(1)} %copy-done.70), channel_id=1, source_target_pairs={{0,1},{1,0},{2,3},{3,2},{4,5},{5,4},{6,7},{7,6},{8,9},{9,8},{10,11... | collective-permute-start | bytes 2211848 | tf_op jit(solution)/shard_map/ppermute | solution.py:793
  190.1 311.5 %reduce-scatter.3.cloned.1.call-start = ((), (), s32[]{:S(2)}) async-start(), calls=%async_computation.2 | async-start | bytes 5308416 | tf_op jit(solution)/shard_map/reduce_scatter | solution.py:1082
  190.3 18.7 %collective-permute-start.63 = (bf16[480,768]{1,0:T(8,128)(2,1)S(1)}, bf16[480,768]{1,0:T(8,128)(2,1)S(1)}, u32[]{:S(2)}, u32[]{:S(2)}) collective-permute-start(bf16[480,768]{1,0:T(8,128)(2,1)S(1)} %add_convert_fusion.5.refs_1_), channel_id=1, source_target_pairs={{0,2},{1,3},{2,0},{3,1},{4,6},{5,7},{6,4},{7,5},{8,10},{9,11},{10,... | collective-permute-start | bytes 2211848 | tf_op jit(solution)/shard_map/ppermute | solution.py:796
  225.2 18.6 %collective-permute-start.66 = (bf16[480,768]{1,0:T(8,128)(2,1)S(1)}, bf16[480,768]{1,0:T(8,128)(2,1)S(1)}, u32[]{:S(2)}, u32[]{:S(2)}) collective-permute-start(bf16[480,768]{1,0:T(8,128)(2,1)S(1)} %add_convert_fusion.4.refs_1_), channel_id=1, source_target_pairs={{0,2},{1,3},{2,0},{3,1},{4,6},{5,7},{6,4},{7,5},{8,10},{9,11},{10,... | collective-permute-start | bytes 2211848 | tf_op jit(solution)/shard_map/ppermute | solution.py:796
  260.3 34.6 %collective-permute-start.70 = (bf16[4,96,1536]{2,1,0:T(8,128)(2,1)S(1)}, bf16[4,96,1536]{2,1,0:T(8,128)(2,1)S(1)}, u32[]{:S(2)}, u32[]{:S(2)}) collective-permute-start(bf16[4,96,1536]{2,1,0:T(8,128)(2,1)S(1)} %get-tuple-element.661), channel_id=1, source_target_pairs={{0,4},{4,0},{8,12},{12,8},{16,20},{20,16},{24,28},{28,24},{1,5},{5... | collective-permute-start | bytes 3538952 | tf_op jit(solution)/shard_map/ppermute | solution.py:1101
  262.6 32.3 %collective-permute-start.69 = (bf16[480,768]{1,0:T(8,128)(2,1)S(1)}, bf16[480,768]{1,0:T(8,128)(2,1)S(1)}, u32[]{:S(2)}, u32[]{:S(2)}) collective-permute-start(bf16[480,768]{1,0:T(8,128)(2,1)S(1)} %add_convert_fusion.3.refs_1_), channel_id=1, source_target_pairs={{0,2},{1,3},{2,0},{3,1},{4,6},{5,7},{6,4},{7,5},{8,10},{9,11},{10,... | collective-permute-start | bytes 2211848 | tf_op jit(solution)/shard_map/ppermute | solution.py:796
  302.2 34.9 %collective-permute-start.75 = (bf16[4,96,1536]{2,1,0:T(8,128)(2,1)}, bf16[4,96,1536]{2,1,0:T(8,128)(2,1)}, u32[]{:S(2)}, u32[]{:S(2)}) collective-permute-start(bf16[4,96,1536]{2,1,0:T(8,128)(2,1)} %get-tuple-element.690), channel_id=1, source_target_pairs={{0,4},{4,0},{8,12},{12,8},{16,20},{20,16},{24,28},{28,24},{1,5},{5... | collective-permute-start | bytes 3538952 | tf_op jit(solution)/shard_map/ppermute | solution.py:1101
  304.6 32.5 %collective-permute-start.73 = (bf16[480,768]{1,0:T(8,128)(2,1)S(1)}, bf16[480,768]{1,0:T(8,128)(2,1)}, u32[]{:S(2)}, u32[]{:S(2)}) collective-permute-start(bf16[480,768]{1,0:T(8,128)(2,1)S(1)} %add_convert_fusion.2.refs_1_), channel_id=1, source_target_pairs={{0,2},{1,3},{2,0},{3,1},{4,6},{5,7},{6,4},{7,5},{8,10},{9,11},{10,... | collective-permute-start | bytes 2211848 | tf_op jit(solution)/shard_map/ppermute | solution.py:796
  359.5 24.2 %collective-permute-start.78 = (bf16[480,768]{1,0:T(8,128)(2,1)}, bf16[480,768]{1,0:T(8,128)(2,1)}, u32[]{:S(2)}, u32[]{:S(2)}) collective-permute-start(bf16[480,768]{1,0:T(8,128)(2,1)} %add_convert_fusion.1.refs_1_), channel_id=1, source_target_pairs={{0,2},{1,3},{2,0},{3,1},{4,6},{5,7},{6,4},{7,5},{8,10},{9,11},{10,... | collective-permute-start | bytes 2211848 | tf_op jit(solution)/shard_map/ppermute | solution.py:796
  362.5 21.1 %collective-permute-start.79 = (bf16[2,96,1536]{2,1,0:T(8,128)(2,1)}, bf16[2,96,1536]{2,1,0:T(8,128)(2,1)}, u32[]{:S(2)}, u32[]{:S(2)}) collective-permute-start(bf16[2,96,1536]{2,1,0:T(8,128)(2,1)} %add_convert_fusion.8), channel_id=1, source_target_pairs={{0,8},{4,12},{8,0},{12,4},{16,24},{20,28},{24,16},{28,20},{1,9},{5... | collective-permute-start | bytes 1769480 | tf_op jit(solution)/shard_map/ppermute | solution.py:1101
  386.9 15.4 %collective-permute-start.60 = (bf16[240,768]{1,0:T(8,128)(2,1)S(1)}, bf16[240,768]{1,0:T(8,128)(2,1)S(1)}, u32[]{:S(2)}, u32[]{:S(2)}) collective-permute-start(bf16[240,768]{1,0:T(8,128)(2,1)S(1)} %pad_maximum_fusion.3), channel_id=1, source_target_pairs={{0,2},{1,3},{2,0},{3,1},{4,6},{5,7},{6,4},{7,5},{8,10},{9,11},{10,... | collective-permute-start | bytes 1105928 | tf_op jit(solution)/shard_map/ppermute | solution.py:1074
  388.0 34.6 %collective-permute-start.83 = (bf16[4,96,1536]{2,1,0:T(8,128)(2,1)S(1)}, bf16[4,96,1536]{2,1,0:T(8,128)(2,1)S(1)}, u32[]{:S(2)}, u32[]{:S(2)}) collective-permute-start(bf16[4,96,1536]{2,1,0:T(8,128)(2,1)S(1)} %get-tuple-element.762), channel_id=1, source_target_pairs={{0,4},{4,0},{8,12},{12,8},{16,20},{20,16},{24,28},{28,24},{1,5},{5... | collective-permute-start | bytes 3538952 | tf_op jit(solution)/shard_map/ppermute | solution.py:1101
  422.7 27.5 %collective-permute-start.91 = (bf16[2,96,1536]{2,1,0:T(8,128)(2,1)S(1)}, bf16[2,96,1536]{2,1,0:T(8,128)(2,1)S(1)}, u32[]{:S(2)}, u32[]{:S(2)}) collective-permute-start(bf16[2,96,1536]{2,1,0:T(8,128)(2,1)S(1)} %add_convert_fusion.6), channel_id=1, source_target_pairs={{0,8},{4,12},{8,0},{12,4},{16,24},{20,28},{24,16},{28,20},{1,9},{5... | collective-permute-start | bytes 1769480 | tf_op jit(solution)/shard_map/ppermute | solution.py:1101
  423.3 73.8 %collective-permute-start.94 = (bf16[1,96,1536]{2,1,0:T(8,128)(2,1)S(1)}, bf16[1,96,1536]{2,1,0:T(8,128)(2,1)S(1)}, u32[]{:S(2)}, u32[]{:S(2)}) collective-permute-start(bf16[1,96,1536]{2,1,0:T(8,128)(2,1)S(1)} %add_convert_fusion.10), channel_id=1, source_target_pairs={{0,16},{4,20},{8,24},{12,28},{16,0},{20,4},{24,8},{28,12},{1,17},{... | collective-permute-start | bytes 884744 | tf_op jit(solution)/shard_map/ppermute | solution.py:1101
  426.0 24.4 %collective-permute-start.82 = (bf16[480,768]{1,0:T(8,128)(2,1)S(1)}, bf16[480,768]{1,0:T(8,128)(2,1)S(1)}, u32[]{:S(2)}, u32[]{:S(2)}) collective-permute-start(bf16[480,768]{1,0:T(8,128)(2,1)S(1)} %add_convert_fusion.refs_1_), channel_id=1, source_target_pairs={{0,2},{1,3},{2,0},{3,1},{4,6},{5,7},{6,4},{7,5},{8,10},{9,11},{10,... | collective-permute-start | bytes 2211848 | tf_op jit(solution)/shard_map/ppermute | solution.py:796
  427.0 26.5 %collective-permute-start.88 = (bf16[4,96,1536]{2,1,0:T(8,128)(2,1)S(1)}, bf16[4,96,1536]{2,1,0:T(8,128)(2,1)S(1)}, u32[]{:S(2)}, u32[]{:S(2)}) collective-permute-start(bf16[4,96,1536]{2,1,0:T(8,128)(2,1)S(1)} %get-tuple-element.781), channel_id=1, source_target_pairs={{0,4},{4,0},{8,12},{12,8},{16,20},{20,16},{24,28},{28,24},{1,5},{5... | collective-permute-start | bytes 3538952 | tf_op jit(solution)/shard_map/ppermute | solution.py:1101
  429.6 67.5 %collective-permute-start.93 = (bf16[1,96,1536]{2,1,0:T(8,128)(2,1)S(1)}, bf16[1,96,1536]{2,1,0:T(8,128)(2,1)S(1)}, u32[]{:S(2)}, u32[]{:S(2)}) collective-permute-start(bf16[1,96,1536]{2,1,0:T(8,128)(2,1)S(1)} %add_convert_fusion.11), channel_id=1, source_target_pairs={{0,16},{4,20},{8,24},{12,28},{16,0},{20,4},{24,8},{28,12},{1,17},{... | collective-permute-start | bytes 884744 | tf_op jit(solution)/shard_map/ppermute | solution.py:1101
  450.3 46.8 %collective-permute-start.92 = (bf16[1,96,1536]{2,1,0:T(8,128)(2,1)S(1)}, bf16[1,96,1536]{2,1,0:T(8,128)(2,1)S(1)}, u32[]{:S(2)}, u32[]{:S(2)}) collective-permute-start(bf16[1,96,1536]{2,1,0:T(8,128)(2,1)S(1)} %add_convert_fusion.12), channel_id=1, source_target_pairs={{0,16},{4,20},{8,24},{12,28},{16,0},{20,4},{24,8},{28,12},{1,17},{... | collective-permute-start | bytes 884744 | tf_op jit(solution)/shard_map/ppermute | solution.py:1101
  453.6 22.5 %collective-permute-start.89 = (bf16[2,96,1536]{2,1,0:T(8,128)(2,1)S(1)}, bf16[2,96,1536]{2,1,0:T(8,128)(2,1)S(1)}, u32[]{:S(2)}, u32[]{:S(2)}) collective-permute-start(bf16[2,96,1536]{2,1,0:T(8,128)(2,1)S(1)} %add_convert_fusion.7), channel_id=1, source_target_pairs={{0,8},{4,12},{8,0},{12,4},{16,24},{20,28},{24,16},{28,20},{1,9},{5... | collective-permute-start | bytes 1769480 | tf_op jit(solution)/shard_map/ppermute | solution.py:1101
  460.3 17.5 %collective-permute-start.86 = (f32[40,768]{1,0:T(8,128)S(1)}, f32[40,768]{1,0:T(8,128)S(1)}, u32[]{:S(2)}, u32[]{:S(2)}) collective-permute-start(f32[40,768]{1,0:T(8,128)S(1)} %add.125), channel_id=1, source_target_pairs={{0,8},{4,12},{8,0},{12,4},{16,24},{20,28},{24,16},{28,20},{1,9},{5... | collective-permute-start | bytes 368648 | tf_op jit(solution)/shard_map/ppermute | solution.py:1285
  476.2 20.9 %collective-permute-start.90 = (bf16[1,96,1536]{2,1,0:T(8,128)(2,1)S(1)}, bf16[1,96,1536]{2,1,0:T(8,128)(2,1)S(1)}, u32[]{:S(2)}, u32[]{:S(2)}) collective-permute-start(bf16[1,96,1536]{2,1,0:T(8,128)(2,1)S(1)} %add_convert_fusion.13), channel_id=1, source_target_pairs={{0,16},{4,20},{8,24},{12,28},{16,0},{20,4},{24,8},{28,12},{1,17},{... | collective-permute-start | bytes 884744 | tf_op jit(solution)/shard_map/ppermute | solution.py:1101
  477.9 17.8 %collective-permute-start.87 = (f32[40,768]{1,0:T(8,128)S(1)}, f32[40,768]{1,0:T(8,128)S(1)}, u32[]{:S(2)}, u32[]{:S(2)}) collective-permute-start(f32[40,768]{1,0:T(8,128)S(1)} %add.126), channel_id=1, source_target_pairs={{0,16},{4,20},{8,24},{12,28},{16,0},{20,4},{24,8},{28,12},{1,17},{... | collective-permute-start | bytes 368648 | tf_op jit(solution)/shard_map/ppermute | solution.py:1285
  (392 other events, 2407.4 us)
Sparse Core Ops, SparseCore 0:
  189.7 101.0 reduce-scatter.4
  315.2 103.2 reduce-scatter.2

commit v5 on v4

--- a/solution.py
+++ b/solution.py
@@ -266,8 +266,12 @@
 SCALE = HDIM**-0.5
 
 
+def scaled(q):
+    return (q.astype(F32) * SCALE).astype(BF16)
+
+
 def attend(q, k, v, addend, kind, sc, sz, base):
-    scores = nt(k, q) * SCALE
+    scores = nt(k, scaled(q))
     if addend is not None:
         scores = scores + addend
     scores = masked(scores, kind, sc, sz, base)
@@ -279,7 +283,8 @@
 
 
 def attend_back(q, k, v, addend, kind, sc, sz, top, inv, do):
-    scores = nt(k, q) * SCALE
+    q = scaled(q)
+    scores = nt(k, q)
     if addend is not None:
         scores = scores + addend
     scores = masked(scores, kind, sc, sz)
@@ -287,8 +292,10 @@
     dv = nn(p.astype(BF16), do)
     dp = nt(v, do)
     ds = p * (dp - jnp.sum(p * dp, 0, keepdims=True))
-    ds = jnp.where(allowed(kind, sc, sz), ds, 0.0).astype(BF16)
-    dk = nn(ds, q) * SCALE
+    if kind in ("patch", "window"):
+        ds = jnp.where(allowed(kind, sc, sz), ds, 0.0)
+    ds = ds.astype(BF16)
+    dk = nn(ds, q)
     dq = tn(k, ds) * SCALE
     return dq, dk, dv, ds
 

time: 522 us -> 521 us (level)
  transfers between devices with their start and end apart: 97 -> 97, of which waited for: 48 -> 48; matrix products, arithmetic and copies ran while one was open for 3% -> 3% of each run, Pallas kernels for 26% -> 25%
where the time goes in v5:
time: 521 us; the launch traced here: 512 us
  waiting for transfers between devices  207 us (40%)
  Pallas kernels  155 us (30%)
  local copies, waits for them, and re-layouts  63 us (12%)
  starting transfers between devices  56.4 us (11%)
  between operations  19.8 us (4%)
  other arithmetic  10.1 us (2%)
    pallas_call x65, Pallas kernels, call(): pl.pallas_call(wrapped, out_shape=tuple(flat_outs), in_specs=[smem] * len...  148 us
    ppermute x12, waiting for transfers between devices, move(): got = lax.ppermute(self.ready, 'dp', [(i, i ^ bit) for i in range(dp_size)])  93.7 us
    unnamed x641, local copies, waits for them, and re-layouts  59.9 us
    ppermute x17, waiting for transfers between devices, across(): return lax.ppermute(x, 'tensor', cross)  58.2 us
    ppermute x60, waiting for transfers between devices, core_swap(): return lax.ppermute(x, 'tensor', swap)  36.6 us
    ppermute x3, waiting for transfers between devices, summed(): x = x + lax.ppermute(x, axis, [(i, i ^ bit) for i in range(size)])  18.6 us
    ppermute x17, starting transfers between devices, across(): return lax.ppermute(x, 'tensor', cross)  16.9 us
    ppermute x12, starting transfers between devices, move(): got = lax.ppermute(self.ready, 'dp', [(i, i ^ bit) for i in range(dp_size)])  15.7 us
  transfers between devices with their start and end apart: 97, of which 48 were waited for; matrix products, arithmetic and copies ran while one was open for 3% of the time, Pallas kernels for 25%

profile of v5, /device:TPU:0, one launch (start us, length us, event | category | flops | bytes accessed | tf_op | source)
XLA Modules:
  0.0 511.5 jit_solution(18376851698046486902)
XLA Ops:
  29.9 5.8 %section1.7 = (bf16[240,768]{1,0:T(8,128)(2,1)S(1)}, bf16[128,768]{1,0:T(8,128)(2,1)S(1)}, bf16[112,768]{1,0:T(8,128)(2,1)S(1)}, bf16[144,768]{1,0:T(8,128)(2,1)...) custom-call(s32[8]{0:T(128)S(1)} %stack.21.refs_0_, ...), custom_call_target="tpu_custom_call" | custom-call | flops 1 | bytes 1 | tf_op jit(solution)/shard_map/section1/pallas_call | solution.py:113
  40.7 3.6 section1.8
  81.8 5.5 %collective-permute-done.20.refs_2_ = bf16[240,768]{1,0:T(8,128)(2,1)S(1)} collective-permute-done((bf16[240,768]{1,0:T(8,128)(2,1)S(1)}, bf16[240,768]{1,0:T(8,128)(2,1)S(1)}, u32[]{:S(2)}, u32[]{:S(2)}) %collective-permute-start.20) | collective-permute-done | bytes 368672 | tf_op jit(solution)/shard_map/ppermute | solution.py:803
  113.4 5.9 %section1.10 = (bf16[240,768]{1,0:T(8,128)(2,1)S(1)}, bf16[128,768]{1,0:T(8,128)(2,1)S(1)}, bf16[112,768]{1,0:T(8,128)(2,1)S(1)}, bf16[144,768]{1,0:T(8,128)(2,1...) custom-call(s32[8]{0:T(128)S(1)} %stack.22.refs_0_, ...), custom_call_target="tpu_custom_call" | custom-call | flops 1 | bytes 1 | tf_op jit(solution)/shard_map/section1/pallas_call | solution.py:113
  123.6 3.7 section1.11
  155.0 4.3 collective-permute-done.51.refs_2_
  165.1 5.6 %collective-permute-done.50.refs_2_ = bf16[240,768]{1,0:T(8,128)(2,1)S(1)} collective-permute-done((bf16[240,768]{1,0:T(8,128)(2,1)S(1)}, bf16[240,768]{1,0:T(8,128)(2,1)S(1)}, u32[]{:S(2)}, u32[]{:S(2)}) %collective-permute-start.50) | collective-permute-done | bytes 368672 | tf_op jit(solution)/shard_map/ppermute | solution.py:803
  182.7 4.6 section3_weights.2
  191.4 17.6 %collective-permute-done.63.refs_2_ = bf16[480,768]{1,0:T(8,128)(2,1)S(1)} collective-permute-done((bf16[480,768]{1,0:T(8,128)(2,1)S(1)}, bf16[480,768]{1,0:T(8,128)(2,1)S(1)}, u32[]{:S(2)}, u32[]{:S(2)}) %collective-permute-start.63) | collective-permute-done | bytes 737312 | tf_op jit(solution)/shard_map/ppermute | solution.py:803
  215.2 7.0 %section2_back.2 = (bf16[480,768]{1,0:T(8,128)(2,1)S(1)}, bf16[480,768]{1,0:T(8,128)(2,1)S(1)}, bf16[800,192]{1,0:T(8,128)(2,1)S(1)}, bf16[160,384]{1,0:T(8,128)...) custom-call(s32[8]{0:T(128)S(1)} %stack.22.refs_0_, ...), custom_call_target="tpu_custom_call" | custom-call | flops 1 | bytes 1 | tf_op jit(solution)/shard_map/section2_back/pallas_call | solution.py:113
  229.3 14.2 %collective-permute-done.66.refs_2_ = bf16[480,768]{1,0:T(8,128)(2,1)S(1)} collective-permute-done((bf16[480,768]{1,0:T(8,128)(2,1)S(1)}, bf16[480,768]{1,0:T(8,128)(2,1)S(1)}, u32[]{:S(2)}, u32[]{:S(2)}) %collective-permute-start.66) | collective-permute-done | bytes 737312 | tf_op jit(solution)/shard_map/ppermute | solution.py:803
  247.2 12.0 %section1_back.2 = (bf16[480,768]{1,0:T(8,128)(2,1)S(1)}, bf16[480,768]{1,0:T(8,128)(2,1)S(1)}, bf16[144,576]{1,0:T(8,128)(2,1)S(1)}, bf16[800,576]{1,0:T(8,128)(2,1)S(1)}, bf16[3,144,144]{2,1,0:T(8,128)(2,1)S(1)}) custom-call(s32[8]{0:T(128)S(1)} %stack.22.refs_0_, bf16[480,768]{1,0:T(8,128)(2,1)S(1)} %get-tuple-element.651.refs_1_.refs_9_, ...), custom_call_target="tpu_custom_call" | custom-call | flops 1 | bytes 1 | tf_op jit(solution)/shard_map/section1_back/pallas_call | solution.py:113
  262.9 5.8 %section1_weights.2 = (bf16[4,96,1536]{2,1,0:T(8,128)(2,1)S(1)}, bf16[4,96,1536]{2,1,0:T(8,128)(2,1)}) custom-call(s32[8]{0:T(128)S(1)} %stack.21.refs_0_, bf16[128,768]{1,0:T(8,128)(2,1)S(1)} %copy-done.133, bf16[112,768]{1,0:T(8,128)(2,1)S(1)} %copy-done.177, bf16[128,768]{1,0:T(8,128)(2,1)} %get-tuple-element.645.refs_1_.refs_3_, ...), custom_call_target="tpu_custom_call" | custom-call | flops 1 | bytes 1 | tf_op jit(solution)/shard_map/section1_weights/pallas_call | solution.py:113
  269.7 24.3 %collective-permute-done.70.refs_13_ = bf16[4,96,1536]{2,1,0:T(8,128)(2,1)S(1)} collective-permute-done((bf16[4,96,1536]{2,1,0:T(8,128)(2,1)S(1)}, bf16[4,96,1536]{2,1,0:T(8,128)(2,1)S(1)}, u32[]{:S(2)}, u32[]{:S(2)}) %collective-permute-start.70) | collective-permute-done | bytes 1179680 | tf_op jit(solution)/shard_map/ppermute | solution.py:1108
  307.5 4.6 section3_weights.3
  314.2 6.8 %collective-permute-done.74.refs_14_ = bf16[2,96,1536]{2,1,0:T(8,128)(2,1)S(1)} collective-permute-done((bf16[2,96,1536]{2,1,0:T(8,128)(2,1)}, bf16[2,96,1536]{2,1,0:T(8,128)(2,1)S(1)}, u32[]{:S(2)}, u32[]{:S(2)}) %collective-permute-start.74) | collective-permute-done | bytes 589856 | tf_op jit(solution)/shard_map/ppermute | solution.py:1108
  321.1 15.2 %collective-permute-done.75.refs_9_ = bf16[4,96,1536]{2,1,0:T(8,128)(2,1)} collective-permute-done((bf16[4,96,1536]{2,1,0:T(8,128)(2,1)}, bf16[4,96,1536]{2,1,0:T(8,128)(2,1)}, u32[]{:S(2)}, u32[]{:S(2)}) %collective-permute-start.75) | collective-permute-done | bytes 1179680 | tf_op jit(solution)/shard_map/ppermute | solution.py:1108
  347.8 7.2 %section2_back.3 = (bf16[480,768]{1,0:T(8,128)(2,1)S(1)}, bf16[480,768]{1,0:T(8,128)(2,1)S(1)}, bf16[800,192]{1,0:T(8,128)(2,1)S(1)}, bf16[160,384]{1,0:T(8,128)...) custom-call(s32[8]{0:T(128)S(1)} %stack.21.refs_0_, ...), custom_call_target="tpu_custom_call" | custom-call | flops 1 | bytes 1 | tf_op jit(solution)/shard_map/section2_back/pallas_call | solution.py:113
  388.5 12.0 %section1_back.3 = (bf16[480,768]{1,0:T(8,128)(2,1)S(1)}, bf16[480,768]{1,0:T(8,128)(2,1)S(1)}, bf16[144,576]{1,0:T(8,128)(2,1)S(1)}, bf16[800,576]{1,0:T(8,128)(2,1)S(1)}, bf16[3,144,144]{2,1,0:T(8,128)(2,1)S(1)}) custom-call(s32[8]{0:T(128)S(1)} %stack.21.refs_0_, bf16[480,768]{1,0:T(8,128)(2,1)S(1)} %get-tuple-element.752.refs_1_.refs_9_, ...), custom_call_target="tpu_custom_call" | custom-call | flops 1 | bytes 1 | tf_op jit(solution)/shard_map/section1_back/pallas_call | solution.py:113
  408.8 12.6 %collective-permute-done.83.refs_5_ = bf16[4,96,1536]{2,1,0:T(8,128)(2,1)S(1)} collective-permute-done((bf16[4,96,1536]{2,1,0:T(8,128)(2,1)S(1)}, bf16[4,96,1536]{2,1,0:T(8,128)(2,1)S(1)}, u32[]{:S(2)}, u32[]{:S(2)}) %collective-permute-start.83) | collective-permute-done | bytes 1179680 | tf_op jit(solution)/shard_map/ppermute | solution.py:1108
  430.2 18.8 %collective-permute-done.91.refs_6_ = bf16[2,96,1536]{2,1,0:T(8,128)(2,1)S(1)} collective-permute-done((bf16[2,96,1536]{2,1,0:T(8,128)(2,1)S(1)}, bf16[2,96,1536]{2,1,0:T(8,128)(2,1)S(1)}, u32[]{:S(2)}, u32[]{:S(2)}) %collective-permute-start.91) | collective-permute-done | bytes 589856 | tf_op jit(solution)/shard_map/ppermute | solution.py:1108
  459.7 15.3 %collective-permute-done.89.refs_2_ = bf16[2,96,1536]{2,1,0:T(8,128)(2,1)S(1)} collective-permute-done((bf16[2,96,1536]{2,1,0:T(8,128)(2,1)S(1)}, bf16[2,96,1536]{2,1,0:T(8,128)(2,1)S(1)}, u32[]{:S(2)}, u32[]{:S(2)}) %collective-permute-start.89) | collective-permute-done | bytes 589856 | tf_op jit(solution)/shard_map/ppermute | solution.py:1108
  479.0 15.6 %collective-permute-done.87 = f32[40,768]{1,0:T(8,128)S(1)} collective-permute-done((f32[40,768]{1,0:T(8,128)S(1)}, f32[40,768]{1,0:T(8,128)S(1)}, u32[]{:S(2)}, u32[]{:S(2)}) %collective-permute-start.87) | collective-permute-done | bytes 122912 | tf_op jit(solution)/shard_map/ppermute | solution.py:1292
  496.1 4.4 finish_attn.1
  (935 shorter events, 259.4 us)
Async XLA Ops:
  7.2 493.3 %reduce-scatter.5.cloned.1.call-start = ((), (), s32[]{:S(2)}) async-start(), calls=%async_computation.3 | async-start | bytes 5308416 | tf_op jit(solution)/shard_map/reduce_scatter | solution.py:1089
  24.7 16.0 %collective-permute-start.8 = (bf16[240,768]{1,0:T(8,128)(2,1)S(1)}, bf16[240,768]{1,0:T(8,128)(2,1)S(1)}, u32[]{:S(2)}, u32[]{:S(2)}) collective-permute-start(bf16[240,768]{1,0:T(8,128)(2,1)S(1)} %reduce-precision_convert_fusion.refs_1_), channel_id=1, source_target_pairs={{0,2},{1,3},{2,0},{3,1},{4,6},{5,7},{6,4},{7,5},{8,10},{9,11},{10,... | collective-permute-start | bytes 1105928 | tf_op jit(solution)/shard_map/ppermute | solution.py:803
  153.4 22.5 %collective-permute-start.61 = (bf16[480,768]{1,0:T(8,128)(2,1)S(1)}, bf16[480,768]{1,0:T(8,128)(2,1)S(1)}, u32[]{:S(2)}, u32[]{:S(2)}) collective-permute-start(bf16[480,768]{1,0:T(8,128)(2,1)S(1)} %copy-done.70), channel_id=1, source_target_pairs={{0,1},{1,0},{2,3},{3,2},{4,5},{5,4},{6,7},{7,6},{8,9},{9,8},{10,11... | collective-permute-start | bytes 2211848 | tf_op jit(solution)/shard_map/ppermute | solution.py:800
  190.1 310.5 %reduce-scatter.3.cloned.1.call-start = ((), (), s32[]{:S(2)}) async-start(), calls=%async_computation.2 | async-start | bytes 5308416 | tf_op jit(solution)/shard_map/reduce_scatter | solution.py:1089
  190.3 18.7 %collective-permute-start.63 = (bf16[480,768]{1,0:T(8,128)(2,1)S(1)}, bf16[480,768]{1,0:T(8,128)(2,1)S(1)}, u32[]{:S(2)}, u32[]{:S(2)}) collective-permute-start(bf16[480,768]{1,0:T(8,128)(2,1)S(1)} %add_convert_fusion.5.refs_1_), channel_id=1, source_target_pairs={{0,2},{1,3},{2,0},{3,1},{4,6},{5,7},{6,4},{7,5},{8,10},{9,11},{10,... | collective-permute-start | bytes 2211848 | tf_op jit(solution)/shard_map/ppermute | solution.py:803
  224.8 18.6 %collective-permute-start.66 = (bf16[480,768]{1,0:T(8,128)(2,1)S(1)}, bf16[480,768]{1,0:T(8,128)(2,1)S(1)}, u32[]{:S(2)}, u32[]{:S(2)}) collective-permute-start(bf16[480,768]{1,0:T(8,128)(2,1)S(1)} %add_convert_fusion.4.refs_1_), channel_id=1, source_target_pairs={{0,2},{1,3},{2,0},{3,1},{4,6},{5,7},{6,4},{7,5},{8,10},{9,11},{10,... | collective-permute-start | bytes 2211848 | tf_op jit(solution)/shard_map/ppermute | solution.py:803
  259.5 34.6 %collective-permute-start.70 = (bf16[4,96,1536]{2,1,0:T(8,128)(2,1)S(1)}, bf16[4,96,1536]{2,1,0:T(8,128)(2,1)S(1)}, u32[]{:S(2)}, u32[]{:S(2)}) collective-permute-start(bf16[4,96,1536]{2,1,0:T(8,128)(2,1)S(1)} %get-tuple-element.661), channel_id=1, source_target_pairs={{0,4},{4,0},{8,12},{12,8},{16,20},{20,16},{24,28},{28,24},{1,5},{5... | collective-permute-start | bytes 3538952 | tf_op jit(solution)/shard_map/ppermute | solution.py:1108
  261.8 32.3 %collective-permute-start.69 = (bf16[480,768]{1,0:T(8,128)(2,1)S(1)}, bf16[480,768]{1,0:T(8,128)(2,1)S(1)}, u32[]{:S(2)}, u32[]{:S(2)}) collective-permute-start(bf16[480,768]{1,0:T(8,128)(2,1)S(1)} %add_convert_fusion.3.refs_1_), channel_id=1, source_target_pairs={{0,2},{1,3},{2,0},{3,1},{4,6},{5,7},{6,4},{7,5},{8,10},{9,11},{10,... | collective-permute-start | bytes 2211848 | tf_op jit(solution)/shard_map/ppermute | solution.py:803
  301.4 34.9 %collective-permute-start.75 = (bf16[4,96,1536]{2,1,0:T(8,128)(2,1)}, bf16[4,96,1536]{2,1,0:T(8,128)(2,1)}, u32[]{:S(2)}, u32[]{:S(2)}) collective-permute-start(bf16[4,96,1536]{2,1,0:T(8,128)(2,1)} %get-tuple-element.690), channel_id=1, source_target_pairs={{0,4},{4,0},{8,12},{12,8},{16,20},{20,16},{24,28},{28,24},{1,5},{5... | collective-permute-start | bytes 3538952 | tf_op jit(solution)/shard_map/ppermute | solution.py:1108
  303.8 32.5 %collective-permute-start.73 = (bf16[480,768]{1,0:T(8,128)(2,1)S(1)}, bf16[480,768]{1,0:T(8,128)(2,1)}, u32[]{:S(2)}, u32[]{:S(2)}) collective-permute-start(bf16[480,768]{1,0:T(8,128)(2,1)S(1)} %add_convert_fusion.2.refs_1_), channel_id=1, source_target_pairs={{0,2},{1,3},{2,0},{3,1},{4,6},{5,7},{6,4},{7,5},{8,10},{9,11},{10,... | collective-permute-start | bytes 2211848 | tf_op jit(solution)/shard_map/ppermute | solution.py:803
  305.8 15.3 %collective-permute-start.74 = (bf16[2,96,1536]{2,1,0:T(8,128)(2,1)}, bf16[2,96,1536]{2,1,0:T(8,128)(2,1)S(1)}, u32[]{:S(2)}, u32[]{:S(2)}) collective-permute-start(bf16[2,96,1536]{2,1,0:T(8,128)(2,1)} %add_convert_fusion.9), channel_id=1, source_target_pairs={{0,8},{4,12},{8,0},{12,4},{16,24},{20,28},{24,16},{28,20},{1,9},{5... | collective-permute-start | bytes 1769480 | tf_op jit(solution)/shard_map/ppermute | solution.py:1108
  358.4 24.1 %collective-permute-start.78 = (bf16[480,768]{1,0:T(8,128)(2,1)}, bf16[480,768]{1,0:T(8,128)(2,1)}, u32[]{:S(2)}, u32[]{:S(2)}) collective-permute-start(bf16[480,768]{1,0:T(8,128)(2,1)} %add_convert_fusion.1.refs_1_), channel_id=1, source_target_pairs={{0,2},{1,3},{2,0},{3,1},{4,6},{5,7},{6,4},{7,5},{8,10},{9,11},{10,... | collective-permute-start | bytes 2211848 | tf_op jit(solution)/shard_map/ppermute | solution.py:803
  361.4 21.0 %collective-permute-start.79 = (bf16[2,96,1536]{2,1,0:T(8,128)(2,1)}, bf16[2,96,1536]{2,1,0:T(8,128)(2,1)}, u32[]{:S(2)}, u32[]{:S(2)}) collective-permute-start(bf16[2,96,1536]{2,1,0:T(8,128)(2,1)} %add_convert_fusion.8), channel_id=1, source_target_pairs={{0,8},{4,12},{8,0},{12,4},{16,24},{20,28},{24,16},{28,20},{1,9},{5... | collective-permute-start | bytes 1769480 | tf_op jit(solution)/shard_map/ppermute | solution.py:1108
  386.9 34.6 %collective-permute-start.83 = (bf16[4,96,1536]{2,1,0:T(8,128)(2,1)S(1)}, bf16[4,96,1536]{2,1,0:T(8,128)(2,1)S(1)}, u32[]{:S(2)}, u32[]{:S(2)}) collective-permute-start(bf16[4,96,1536]{2,1,0:T(8,128)(2,1)S(1)} %get-tuple-element.762), channel_id=1, source_target_pairs={{0,4},{4,0},{8,12},{12,8},{16,20},{20,16},{24,28},{28,24},{1,5},{5... | collective-permute-start | bytes 3538952 | tf_op jit(solution)/shard_map/ppermute | solution.py:1108
  421.6 27.4 %collective-permute-start.91 = (bf16[2,96,1536]{2,1,0:T(8,128)(2,1)S(1)}, bf16[2,96,1536]{2,1,0:T(8,128)(2,1)S(1)}, u32[]{:S(2)}, u32[]{:S(2)}) collective-permute-start(bf16[2,96,1536]{2,1,0:T(8,128)(2,1)S(1)} %add_convert_fusion.6), channel_id=1, source_target_pairs={{0,8},{4,12},{8,0},{12,4},{16,24},{20,28},{24,16},{28,20},{1,9},{5... | collective-permute-start | bytes 1769480 | tf_op jit(solution)/shard_map/ppermute | solution.py:1108
  422.2 73.9 %collective-permute-start.94 = (bf16[1,96,1536]{2,1,0:T(8,128)(2,1)S(1)}, bf16[1,96,1536]{2,1,0:T(8,128)(2,1)S(1)}, u32[]{:S(2)}, u32[]{:S(2)}) collective-permute-start(bf16[1,96,1536]{2,1,0:T(8,128)(2,1)S(1)} %add_convert_fusion.10), channel_id=1, source_target_pairs={{0,16},{4,20},{8,24},{12,28},{16,0},{20,4},{24,8},{28,12},{1,17},{... | collective-permute-start | bytes 884744 | tf_op jit(solution)/shard_map/ppermute | solution.py:1108
  424.9 24.3 %collective-permute-start.82 = (bf16[480,768]{1,0:T(8,128)(2,1)S(1)}, bf16[480,768]{1,0:T(8,128)(2,1)S(1)}, u32[]{:S(2)}, u32[]{:S(2)}) collective-permute-start(bf16[480,768]{1,0:T(8,128)(2,1)S(1)} %add_convert_fusion.refs_1_), channel_id=1, source_target_pairs={{0,2},{1,3},{2,0},{3,1},{4,6},{5,7},{6,4},{7,5},{8,10},{9,11},{10,... | collective-permute-start | bytes 2211848 | tf_op jit(solution)/shard_map/ppermute | solution.py:803
  425.8 26.5 %collective-permute-start.88 = (bf16[4,96,1536]{2,1,0:T(8,128)(2,1)S(1)}, bf16[4,96,1536]{2,1,0:T(8,128)(2,1)S(1)}, u32[]{:S(2)}, u32[]{:S(2)}) collective-permute-start(bf16[4,96,1536]{2,1,0:T(8,128)(2,1)S(1)} %get-tuple-element.781), channel_id=1, source_target_pairs={{0,4},{4,0},{8,12},{12,8},{16,20},{20,16},{24,28},{28,24},{1,5},{5... | collective-permute-start | bytes 3538952 | tf_op jit(solution)/shard_map/ppermute | solution.py:1108
  428.6 67.5 %collective-permute-start.93 = (bf16[1,96,1536]{2,1,0:T(8,128)(2,1)S(1)}, bf16[1,96,1536]{2,1,0:T(8,128)(2,1)S(1)}, u32[]{:S(2)}, u32[]{:S(2)}) collective-permute-start(bf16[1,96,1536]{2,1,0:T(8,128)(2,1)S(1)} %add_convert_fusion.11), channel_id=1, source_target_pairs={{0,16},{4,20},{8,24},{12,28},{16,0},{20,4},{24,8},{28,12},{1,17},{... | collective-permute-start | bytes 884744 | tf_op jit(solution)/shard_map/ppermute | solution.py:1108
  449.1 47.0 %collective-permute-start.92 = (bf16[1,96,1536]{2,1,0:T(8,128)(2,1)S(1)}, bf16[1,96,1536]{2,1,0:T(8,128)(2,1)S(1)}, u32[]{:S(2)}, u32[]{:S(2)}) collective-permute-start(bf16[1,96,1536]{2,1,0:T(8,128)(2,1)S(1)} %add_convert_fusion.12), channel_id=1, source_target_pairs={{0,16},{4,20},{8,24},{12,28},{16,0},{20,4},{24,8},{28,12},{1,17},{... | collective-permute-start | bytes 884744 | tf_op jit(solution)/shard_map/ppermute | solution.py:1108
  452.4 22.5 %collective-permute-start.89 = (bf16[2,96,1536]{2,1,0:T(8,128)(2,1)S(1)}, bf16[2,96,1536]{2,1,0:T(8,128)(2,1)S(1)}, u32[]{:S(2)}, u32[]{:S(2)}) collective-permute-start(bf16[2,96,1536]{2,1,0:T(8,128)(2,1)S(1)} %add_convert_fusion.7), channel_id=1, source_target_pairs={{0,8},{4,12},{8,0},{12,4},{16,24},{20,28},{24,16},{28,20},{1,9},{5... | collective-permute-start | bytes 1769480 | tf_op jit(solution)/shard_map/ppermute | solution.py:1108
  459.2 17.6 %collective-permute-start.86 = (f32[40,768]{1,0:T(8,128)S(1)}, f32[40,768]{1,0:T(8,128)S(1)}, u32[]{:S(2)}, u32[]{:S(2)}) collective-permute-start(f32[40,768]{1,0:T(8,128)S(1)} %add.125), channel_id=1, source_target_pairs={{0,8},{4,12},{8,0},{12,4},{16,24},{20,28},{24,16},{28,20},{1,9},{5... | collective-permute-start | bytes 368648 | tf_op jit(solution)/shard_map/ppermute | solution.py:1292
  475.0 21.0 %collective-permute-start.90 = (bf16[1,96,1536]{2,1,0:T(8,128)(2,1)S(1)}, bf16[1,96,1536]{2,1,0:T(8,128)(2,1)S(1)}, u32[]{:S(2)}, u32[]{:S(2)}) collective-permute-start(bf16[1,96,1536]{2,1,0:T(8,128)(2,1)S(1)} %add_convert_fusion.13), channel_id=1, source_target_pairs={{0,16},{4,20},{8,24},{12,28},{16,0},{20,4},{24,8},{28,12},{1,17},{... | collective-permute-start | bytes 884744 | tf_op jit(solution)/shard_map/ppermute | solution.py:1108
  476.8 17.8 %collective-permute-start.87 = (f32[40,768]{1,0:T(8,128)S(1)}, f32[40,768]{1,0:T(8,128)S(1)}, u32[]{:S(2)}, u32[]{:S(2)}) collective-permute-start(f32[40,768]{1,0:T(8,128)S(1)} %add.126), channel_id=1, source_target_pairs={{0,16},{4,20},{8,24},{12,28},{16,0},{20,4},{24,8},{28,12},{1,17},{... | collective-permute-start | bytes 368648 | tf_op jit(solution)/shard_map/ppermute | solution.py:1292
  (392 other events, 2406.9 us)
Sparse Core Ops, SparseCore 0:
  189.6 101.0 reduce-scatter.4
  314.4 103.3 reduce-scatter.2
